TPU v7x, 256 devices: a whole 4x4x8 slice. The times are simulated.
256 devices in a mesh: frame: 4 (over y_lo, core), patch: 64 (over y_hi, z, x).
Axes of the slice: x: 4, y: 4 (y_hi: 2, y_lo: 2; y = y_hi * 2 + y_lo), z: 8, core: 2. Of those that a mesh axis runs over, the one named last changes fastest.
Arguments:
- latent: bfloat16 [4, 64, 16, 1280], P(None, 'patch', None, 'frame'), may hold values from -24 to 24
- stale_latent: bfloat16 [4, 64, 16, 1280], P(None, 'patch', None, 'frame'), may hold values from -6 to 6
- conv_weight: bfloat16 [9, 1280, 1280], P(None, 'frame', 'patch'), may hold values from -1 to 1
- temb_table: bfloat16 [1000, 1280], replicated, may hold values from -4 to 4
- step_index: int32 [1], replicated, may hold values from 0 to 999
- gn_gain: float32 [1280], replicated, may hold values from 0.25 to 1.75
- gn_shift: float32 [1280], replicated, may hold values from -0.6 to 0.6
- w_sqkv: bfloat16 [1280, 3, 768], P('patch', None, 'frame'), may hold values from -0.15625 to 0.15625
- stale_kv: bfloat16 [4, 64, 16, 2, 768], P(None, 'patch', None, None, 'frame'), may hold values from -60 to 60
- w_sout: bfloat16 [768, 1280], P('frame', 'patch'), may hold values from -0.21875 to 0.21875
- w_tqkv: bfloat16 [1280, 3, 1280], P('patch', None, 'frame'), may hold values from -0.15625 to 0.15625
- w_tout: bfloat16 [1280, 1280], P('frame', 'patch'), may hold values from -0.15625 to 0.15625
Outputs:
- mixed: bfloat16 [4, 64, 16, 1280], P(None, 'patch')
- fresh_kv: bfloat16 [4, 64, 16, 2, 768], P(None, 'patch', None, None, 'frame')
All inputs are finite; a program needn't handle non-finite values.
Results may differ from a plain program's by a relative error of at most 0.019.
Values may be sent and summed in bfloat16 or wider, within the bound.
No kernel may reach another device: no remote copies, remote signals or barrier semaphores. Data moves between devices by JAX's collectives and lax.ppermute only.
A program may use at most 128 MiB of HBM per device.

v0:
```python
import jax
import jax.numpy as jnp
from jax import lax
from jax.experimental import pallas as pl
from jax.experimental.pallas import tpu as pltpu
from jax.sharding import Mesh
from jax.sharding import PartitionSpec as P

CHANNELS = 1280
GROUPS = 32
GROUP_WIDTH = CHANNELS // GROUPS
HEAD_DIM = 64
FRAMES = 4
COLUMNS = 16
SIZES = {"yl": 2, "c": 2, "yh": 2, "z": 8, "x": 4}
FRAME = ("yl", "c")
PATCH = ("yh", "z", "x")
BF16 = jnp.bfloat16
F32 = jnp.float32
VMEM = pl.BlockSpec(memory_space=pltpu.VMEM)
SMEM = pl.BlockSpec(memory_space=pltpu.SMEM)
HBM = pl.BlockSpec(memory_space=pl.ANY)
PARAMS = pltpu.CompilerParams(vmem_limit_bytes=40 * 1024 * 1024)
NT = (((1,), (1,)), ((), ()))


def from_shift(value, axis, offset):
    size = SIZES[axis]
    return lax.ppermute(value, axis, [((i + offset) % size, i) for i in range(size)])


def pair_yh(block, yh):
    other = from_shift(block, "yh", 1)
    return jnp.concatenate(
        [jnp.where(yh == 0, block, other), jnp.where(yh == 0, other, block)], axis=0
    )


def gather_x(pair, x):
    parts = [pair] + [from_shift(pair, "x", k) for k in (1, 2, 3)]
    ordered = []
    for place in range(4):
        chosen = parts[place]
        for mine in (1, 2, 3):
            chosen = jnp.where(x == mine, parts[(place - mine) % 4], chosen)
        ordered.append(chosen)
    return ordered


def conv_kernel(where_ref, rows_ref, weight_ref, keep_ref, send_ref):
    yl, c = where_ref[0], where_ref[1]
    column = lax.broadcasted_iota(jnp.int32, (512, 1), 0) % COLUMNS
    sums = []
    for col_tap in range(3):
        total = None
        for row_tap in range(3):
            lhs = rows_ref[:, row_tap].reshape(512, 320)
            tap = 3 * row_tap + col_tap
            part = lax.dot_general(
                lhs,
                weight_ref[:, tap * 320 : (tap + 1) * 320],
                NT,
                preferred_element_type=F32,
            )
            total = part if total is None else total + part
        sums.append(total)
    left = jnp.where(column == 0, 0.0, pltpu.roll(sums[0], 1, 0))
    right = jnp.where(column == COLUMNS - 1, 0.0, pltpu.roll(sums[2], 511, 0))
    hidden = (sums[1] + left + right).reshape(8, FRAMES, COLUMNS, 160)
    for frame in range(FRAMES):
        value = hidden[:, frame].reshape(128, 160)
        place = yl ^ (frame // 2)

        @pl.when(c == frame % 2)
        def _():
            keep_ref[place] = value

        @pl.when(c != frame % 2)
        def _():
            send_ref[place] = value


def group_masks():
    lane = lax.broadcasted_iota(jnp.int32, (1, 160), 1)
    return [(lane // 80) * 2 + (lane % 40) // 20 == g for g in range(4)]


def stats_kernel(keep_ref, got_ref, embed_ref, hidden_ref, stats_ref):
    hidden = keep_ref[...] + got_ref[...] + embed_ref[...]
    hidden_ref[...] = hidden
    count = 128.0 * GROUP_WIDTH
    masks = group_masks()
    sums = jnp.sum(hidden, axis=0, keepdims=True)
    means = [jnp.sum(jnp.where(m, sums, 0.0), axis=1, keepdims=True) / count for m in masks]
    mean = sum(jnp.where(m, v, 0.0) for m, v in zip(masks, means))
    centred = hidden - mean
    squares = jnp.sum(centred * centred, axis=0, keepdims=True)
    lane = lax.broadcasted_iota(jnp.int32, (8, 128), 1)
    out = jnp.zeros((8, 128), F32)
    for g in range(4):
        spread = jnp.sum(jnp.where(masks[g], squares, 0.0), axis=1, keepdims=True)
        out = jnp.where(lane == g, means[g], out)
        out = jnp.where(lane == 4 + g, spread, out)
    stats_ref[...] = out


def norm_kernel(hidden_ref, stats_ref, gain_ref, shift_ref, out_ref):
    stats = stats_ref[...]
    masks = group_masks()
    local = 128.0 * GROUP_WIDTH
    mean_row = jnp.zeros((1, 160), F32)
    scale_row = jnp.zeros((1, 160), F32)
    for g in range(4):
        means = stats[:, 0:1, g : g + 1]
        mean = jnp.sum(means, axis=0, keepdims=True) / 8.0
        gap = means - mean
        spread = jnp.sum(stats[:, 0:1, 4 + g : 5 + g] + local * gap * gap, axis=0) / (8.0 * local)
        mean_row = jnp.where(masks[g], mean[0], mean_row)
        scale_row = jnp.where(masks[g], lax.rsqrt(spread + 1e-05), scale_row)
    normed = (hidden_ref[...] - mean_row) * scale_row
    value = normed * gain_ref[...] + shift_ref[...]
    out_ref[...] = jax.nn.silu(value).astype(BF16).reshape(8, COLUMNS, 160)


def softmax_parts(scores):
    top = jnp.max(scores, axis=-1, keepdims=True)
    expo = jnp.exp(scores - top)
    return expo.astype(BF16), jnp.sum(expo, axis=-1, keepdims=True)


def order_matrix():
    row = lax.broadcasted_iota(jnp.int32, (160, 160), 0)
    col = lax.broadcasted_iota(jnp.int32, (160, 160), 1)
    return (row // 40 * 20 + row % 20 + (row % 40) // 20 * 80 == col).astype(BF16)


def reorder_rows(turn, chunks):
    turned = []
    for rows in chunks:
        value = lax.dot_general(turn, rows, (((0,), (0,)), ((), ())), preferred_element_type=F32)
        turned.append(value.astype(BF16))
    return jnp.concatenate([t[80 * h : 80 * h + 80] for h in range(2) for t in turned], axis=0)


def chunk_of(w_scr, chunk, blocks):
    places = slice(4 * chunk, 4 * chunk + 4)
    parts = [w_scr[places, 40 * k : 40 * k + 40, :].reshape(160, 384) for k in blocks]
    return jnp.concatenate(parts, axis=1)


def spatial_kernel(where_ref, *refs):
    acts, packed_ref = refs[:4], refs[4]
    keep_ref, send_ref, fresh_ref, own_ref, w_scr, kv_scr, w_sem, kv_sem = refs[5:]
    w_copy = pltpu.make_async_copy(packed_ref.at[:, 128:208], w_scr, w_sem)
    kv_copy = pltpu.make_async_copy(packed_ref.at[:, :128], kv_scr, kv_sem)
    w_copy.start()
    kv_copy.start()
    yl, c, place = where_ref[0], where_ref[1], where_ref[2] * 4 + where_ref[4]
    turn = order_matrix()
    own = [
        jnp.dot(acts[0][chunk], turn, preferred_element_type=F32).astype(BF16) for chunk in range(8)
    ]
    own_ref[...] = jnp.concatenate([o[:, 80 * h : 80 * h + 80] for h in range(2) for o in own], axis=1)
    w_copy.wait()
    projected = None
    out_weights = []
    for chunk in range(8):
        lhs = jnp.concatenate([a[chunk] for a in acts], axis=0)
        rhs = chunk_of(w_scr, chunk, (0, 1))
        part = jnp.dot(lhs, rhs[:, :576], preferred_element_type=F32)
        projected = part if projected is None else projected + part
        out_weights.append(rhs[:, 576:])
    projected = projected.astype(BF16)
    out_weights = reorder_rows(turn, out_weights)
    score_scale = HEAD_DIM ** (-0.5)
    head_of = lax.broadcasted_iota(jnp.int32, (COLUMNS, 192), 1) // HEAD_DIM
    key_row = lax.broadcasted_iota(jnp.int32, (1, 512), 1) // COLUMNS
    attended = []
    kv_copy.wait()
    for rel in range(FRAMES):
        frame = (2 * yl + c) ^ rel
        mine = projected[rel * COLUMNS : (rel + 1) * COLUMNS]
        fresh = mine[:, 192:]
        fresh_ref[frame] = fresh
        query = mine[:, :192]
        zero = jnp.zeros_like(query)
        queries = jnp.concatenate([jnp.where(head_of == h, query, zero) for h in range(3)], axis=0)
        blocks = [fresh]
        for half in range(2):
            start = pl.multiple_of(half * 64 + frame * COLUMNS, COLUMNS)
            blocks.append(kv_scr[:, pl.ds(start, COLUMNS), :].reshape(512, 384))
        scores = [
            lax.dot_general(queries, b[:, :192], NT, preferred_element_type=F32) * score_scale
            for b in blocks
        ]
        scores[1] = jnp.where(key_row == place, -jnp.inf, scores[1])
        top = jnp.max(scores[0], axis=-1, keepdims=True)
        for s in scores[1:]:
            top = jnp.maximum(top, jnp.max(s, axis=-1, keepdims=True))
        numerator, total = None, None
        for s, b in zip(scores, blocks):
            expo = jnp.exp(s - top)
            part = jnp.dot(expo.astype(BF16), b[:, 192:], preferred_element_type=F32)
            weight = jnp.sum(expo, axis=-1, keepdims=True)
            numerator = part if numerator is None else numerator + part
            total = weight if total is None else total + weight
        result = numerator / total
        rows = jnp.zeros((COLUMNS, 192), F32)
        for h in range(3):
            rows = jnp.where(head_of == h, result[h * COLUMNS : (h + 1) * COLUMNS], rows)
        attended.append(rows.astype(BF16))
    attended = jnp.concatenate(attended, axis=0)
    part = lax.dot_general(attended, out_weights, NT, preferred_element_type=F32)
    for rel in range(FRAMES):
        target = send_ref if rel % 2 else keep_ref
        target[rel // 2] = part[rel * COLUMNS : (rel + 1) * COLUMNS]


def temporal_kernel(where_ref, *refs):
    pieces, packed_ref = refs[:4], refs[4]
    keep_ref, send_ref, w_scr, w_sem = refs[5:]
    w_copy = pltpu.make_async_copy(packed_ref.at[:, 208:], w_scr, w_sem)
    w_copy.start()
    turn = order_matrix()
    section = jnp.concatenate([p[...] for p in pieces], axis=0)
    sources = []
    for chunk in range(8):
        lhs = jnp.concatenate(
            [section[:, k * 640 + chunk * 80 : k * 640 + chunk * 80 + 80] for k in range(2)], axis=1
        )
        sources.append(lax.dot_general(lhs, turn, NT, preferred_element_type=F32).astype(BF16))
    w_copy.wait()
    temporal = None
    out_weights = []
    for chunk in range(8):
        rhs = chunk_of(w_scr, chunk, range(4))
        part = jnp.dot(sources[chunk], rhs[:, :960], preferred_element_type=F32)
        temporal = part if temporal is None else temporal + part
        out_weights.append(rhs[:, 960:1280])
    temporal = temporal.astype(BF16)
    score_scale = HEAD_DIM ** (-0.5)
    row = lax.broadcasted_iota(jnp.int32, (64, 64), 0) % COLUMNS
    col = lax.broadcasted_iota(jnp.int32, (64, 64), 1) % COLUMNS
    outs = []
    for head in range(5):
        query, key, value = [
            temporal[:, k * 320 + head * 64 : k * 320 + (head + 1) * 64] for k in range(3)
        ]
        scores = lax.dot_general(query, key, NT, preferred_element_type=F32) * score_scale
        expo, total = softmax_parts(jnp.where(row == col, scores, -jnp.inf))
        outs.append(jnp.dot(expo, value, preferred_element_type=F32) / total)
    mixed = jnp.concatenate(outs, axis=1).astype(BF16)
    part = lax.dot_general(
        mixed, reorder_rows(turn, out_weights), NT, preferred_element_type=F32
    )
    for rel in range(FRAMES):
        target = send_ref if rel % 2 else keep_ref
        target[rel // 2] = part[rel * COLUMNS : (rel + 1) * COLUMNS]


def final_kernel(where_ref, *refs):
    out_ref = refs[4]
    mine = 2 * where_ref[0] + where_ref[1]
    for rel in range(FRAMES):
        out_ref[mine ^ rel] = refs[rel][...]


def call(kernel, out_shape, *args, scratch=(), flops=0, smem=False, hbm=None):
    moved = sum(a.size * a.dtype.itemsize for a in args)
    return pl.pallas_call(
        kernel,
        out_shape=out_shape,
        in_specs=[
            SMEM if smem and i == 0 else HBM if i == hbm else VMEM for i in range(len(args))
        ],
        out_specs=jax.tree.map(lambda _: VMEM, out_shape),
        scratch_shapes=list(scratch),
        compiler_params=PARAMS,
        cost_estimate=pl.CostEstimate(flops=flops, bytes_accessed=moved, transcendentals=0),
    )(*args)


def shape(dims, dtype):
    return jax.ShapeDtypeStruct(dims, dtype)


def swap(value, axis):
    return lax.ppermute(value, axis, [(0, 1), (1, 0)])


def sum_over_frame(keep, send):
    got = swap(send, "c")
    away = keep[1] + got[1]
    return keep[0] + got[0], swap(away, "yl")


def gather_frame(piece):
    other = swap(piece, "c")
    return [piece, other, swap(piece, "yl"), swap(other, "yl")]


def shards(
    latent,
    stale_latent,
    conv_weight,
    temb_table,
    step_index,
    gn_gain,
    gn_shift,
    w_sqkv,
    stale_kv,
    w_sout,
    w_tqkv,
    w_tout,
):
    yl, c, yh, z, x = (lax.axis_index(a) for a in ("yl", "c", "yh", "z", "x"))
    where = jnp.stack([yl, c, z, yh, x]).astype(jnp.int32)

    count = 64
    above = lax.ppermute(stale_latent, PATCH, [(i, i + 1) for i in range(count - 1)])
    below = lax.ppermute(stale_latent, PATCH, [(i + 1, i) for i in range(count - 1)])
    conv_block = jnp.transpose(conv_weight, (2, 0, 1)).reshape(20, 9 * 320)
    conv_parts = gather_x(pair_yh(conv_block, yh), x)
    conv_full = jnp.concatenate(conv_parts, axis=0)

    weights = jnp.concatenate(
        [
            w_sqkv.reshape(20, 576),
            w_sout.T,
            w_tqkv.reshape(20, 960),
            w_tout.T,
            jnp.zeros((20, 256), BF16),
        ],
        axis=1,
    )
    kv = stale_kv.reshape(FRAMES * COLUMNS, 384)
    kv_other = from_shift(kv, "yh", 1)
    weights = pair_yh(weights, yh)
    weights = [weights[:, k * 384 : (k + 1) * 384] for k in range(6)]
    packed = jnp.concatenate([kv, kv_other] + weights, axis=0)
    packed = lax.all_gather(packed, ("z", "x"), axis=0, tiled=False)

    rows = jnp.concatenate([above, latent, below], axis=1).transpose(1, 0, 2, 3)
    rows = lax.all_to_all(jnp.broadcast_to(rows, (8,) + rows.shape), "z", 0, 0)
    half = shape((2, 128, 160), F32)
    keep, send = call(conv_kernel, (half, half), where, rows, conv_full, smem=True, flops=3 * 10**9)
    mine, got = sum_over_frame(keep, send)

    def channels_of(vector):
        local = lax.dynamic_index_in_dim(vector.reshape(2, 8, 4, 20), z, 1, keepdims=False)
        return local.transpose(1, 0, 2).reshape(1, 160)

    embed = channels_of(lax.dynamic_index_in_dim(temb_table, step_index[0], 0, keepdims=False))
    hidden, stats = call(
        stats_kernel, (shape((128, 160), F32), shape((8, 128), F32)), mine, got, embed.astype(F32)
    )
    stats = lax.all_to_all(jnp.broadcast_to(stats, (8, 8, 128)), ("yh", "x"), 0, 0)
    activated = call(
        norm_kernel,
        shape((8, COLUMNS, 160), BF16),
        hidden,
        stats,
        channels_of(gn_gain),
        channels_of(gn_shift),
    )
    activated = lax.all_to_all(activated, "z", 0, 0)

    share = shape((2, COLUMNS, CHANNELS), F32)
    keep, send, fresh, own = call(
        spatial_kernel,
        (share, share, shape((FRAMES, COLUMNS, 384), BF16), shape((COLUMNS, CHANNELS), BF16)),
        where,
        *gather_frame(activated),
        packed,
        smem=True,
        hbm=5,
        scratch=[
            pltpu.VMEM((32, 80, 384), BF16),
            pltpu.VMEM((32, 128, 384), BF16),
            pltpu.SemaphoreType.DMA,
            pltpu.SemaphoreType.DMA,
        ],
        flops=10**9,
    )
    mine, got = sum_over_frame(keep, send)
    section = (own.astype(F32) + (mine + got)).astype(BF16)
    keep, send = call(
        temporal_kernel,
        (share, share),
        where,
        *gather_frame(section),
        packed,
        smem=True,
        hbm=5,
        scratch=[pltpu.VMEM((32, 160, 384), BF16), pltpu.SemaphoreType.DMA],
        flops=10**9,
    )
    mine, got = sum_over_frame(keep, send)
    mixed = (section.astype(F32) + (mine + got)).astype(BF16)
    mixed = call(
        final_kernel,
        shape((FRAMES, COLUMNS, CHANNELS), BF16),
        where,
        *gather_frame(mixed),
        smem=True,
    )
    return (
        mixed.reshape(FRAMES, 1, COLUMNS, CHANNELS),
        fresh.reshape(FRAMES, 1, COLUMNS, 2, 192),
    )


def solution(mesh):
    fine = Mesh(mesh.devices.reshape(2, 2, 2, 8, 4), ("yl", "c", "yh", "z", "x"))
    return jax.shard_map(
        shards,
        mesh=fine,
        in_specs=(
            P(None, PATCH, None, FRAME),
            P(None, PATCH, None, FRAME),
            P(None, FRAME, PATCH),
            P(),
            P(),
            P(),
            P(),
            P(PATCH, None, FRAME),
            P(None, PATCH, None, None, FRAME),
            P(FRAME, PATCH),
            P(PATCH, None, FRAME),
            P(FRAME, PATCH),
        ),
        out_specs=(P(None, PATCH, None, None), P(None, PATCH, None, None, FRAME)),
        check_vma=False,
    )
```

profile of v0, /device:TPU:1, one launch (start us, length us, event | category | flops | bytes accessed | tf_op | source)
XLA Modules:
  0.0 180.1 jit_solution(16062540305050781966)
XLA Ops:
  7.2 1.0 copy.31
  9.3 0.8 concatenate.21
  10.1 3.8 %collective-permute-start.12 = (bf16[20,2304]{1,0:T(8,128)(2,1)S(1)}, bf16[20,2304]{1,0:T(8,128)(2,1)S(1)}, u32[]{:S(2)}, u32[]{:S(2)}) collective-permute-start(bf16[20,2304]{1,0:T(8,128)(2,1)S(1)} %concatenate.21), channel_id=1, source_target_pairs={{32,0},{0,32},{33,1},{1,33},{34,2},{2,34},{35,3},{3,35},{36,4},{4,... | collective-permute-start | bytes 276488 | tf_op jit(solution)/shard_map/ppermute | solution.py:29
  13.9 0.9 reshape.67
  15.0 4.5 %collective-permute-done.11 = bf16[64,384]{1,0:T(8,128)(2,1)S(1)} collective-permute-done((bf16[64,384]{1,0:T(8,128)(2,1)S(1)}, bf16[64,384]{1,0:T(8,128)(2,1)S(1)}, u32[]{:S(2)}, u32[]{:S(2)}) %collective-permute-start.11) | collective-permute-done | bytes 49184 | tf_op jit(solution)/shard_map/ppermute | solution.py:29
  20.4 3.0 %collective-permute-start = (bf16[4,1,16,320]{3,2,1,0:T(8,128)(2,1)S(1)}, bf16[4,1,16,320]{3,2,1,0:T(8,128)(2,1)S(1)}, u32[]{:S(2)}, u32[]{:S(2)}) collective-permute-start(bf16[4,1,16,320]{3,2,1,0:T(8,128)(2,1)S(1)} %copy-done.9), channel_id=1, source_target_pairs={{0,1},{1,2},{2,3},{3,4},{4,5},{5,6},{6,7},{7,8},{8,9},{9,10},{10,1... | collective-permute-start | bytes 122888 | tf_op jit(solution)/shard_map/ppermute | solution.py:320
  23.4 1.3 collective-permute-start.1
  24.9 10.0 %collective-permute-start.2 = (bf16[20,2880]{1,0:T(8,128)(2,1)S(1)}, bf16[20,2880]{1,0:T(8,128)(2,1)S(1)}, u32[]{:S(2)}, u32[]{:S(2)}) collective-permute-start(bf16[20,2880]{1,0:T(8,128)(2,1)S(1)} %reshape.61), channel_id=1, source_target_pairs={{32,0},{0,32},{33,1},{1,33},{34,2},{2,34},{35,3},{3,35},{36,4},{4,... | collective-permute-start | bytes 345608 | tf_op jit(solution)/shard_map/ppermute | solution.py:29
  35.0 1.2 broadcast_in_dim.9
  36.2 4.3 %all-to-all-start = ((bf16[8,3,4,16,320]{4,3,2,1,0:T(8,128)(2,1)}), bf16[8,3,4,16,320]{4,3,2,1,0:T(8,128)(2,1)}, u32[]{:S(2)}, u32[]{:S(2)}) async-start(bf16[8,3,4,16,320]{4,3,2,1,0:T(8,128)(2,1)} %broadcast_in_dim.9), calls=%async_computation | async-start | bytes 2359296 | tf_op jit(solution)/shard_map/all_to_all | solution.py:344
  40.5 3.0 %collective-permute-start.3 = (bf16[40,2880]{1,0:T(8,128)(2,1)S(1)}, bf16[40,2880]{1,0:T(8,128)(2,1)S(1)}, u32[]{:S(2)}, u32[]{:S(2)}) collective-permute-start(bf16[40,2880]{1,0:T(8,128)(2,1)S(1)} %pad_maximum_fusion.1), channel_id=1, source_target_pairs={{1,0},{2,1},{3,2},{0,3},{5,4},{6,5},{7,6},{4,7},{9,8},{10,9},{11,1... | collective-permute-start | bytes 691208 | tf_op jit(solution)/shard_map/ppermute | solution.py:29
  44.3 3.0 %collective-permute-done.3 = bf16[40,2880]{1,0:T(8,128)(2,1)S(1)} collective-permute-done((bf16[40,2880]{1,0:T(8,128)(2,1)S(1)}, bf16[40,2880]{1,0:T(8,128)(2,1)S(1)}, u32[]{:S(2)}, u32[]{:S(2)}) %collective-permute-start.3) | collective-permute-done | bytes 230432 | tf_op jit(solution)/shard_map/ppermute | solution.py:29
  47.4 3.1 %collective-permute-done.4 = bf16[40,2880]{1,0:T(8,128)(2,1)} collective-permute-done((bf16[40,2880]{1,0:T(8,128)(2,1)S(1)}, bf16[40,2880]{1,0:T(8,128)(2,1)}, u32[]{:S(2)}, u32[]{:S(2)}) %collective-permute-start.4) | collective-permute-done | bytes 230432 | tf_op jit(solution)/shard_map/ppermute | solution.py:29
  50.4 7.9 %collective-permute-done.5 = bf16[40,2880]{1,0:T(8,128)(2,1)} collective-permute-done((bf16[40,2880]{1,0:T(8,128)(2,1)S(1)}, bf16[40,2880]{1,0:T(8,128)(2,1)}, u32[]{:S(2)}, u32[]{:S(2)}) %collective-permute-start.5) | collective-permute-done | bytes 230432 | tf_op jit(solution)/shard_map/ppermute | solution.py:29
  58.3 1.4 select_select_fusion.3
  59.8 18.8 %all-to-all-done.rows_ref = bf16[8,3,4,16,320]{4,3,2,1,0:T(8,128)(2,1)} async-done(((bf16[8,3,4,16,320]{4,3,2,1,0:T(8,128)(2,1)}), bf16[8,3,4,16,320]{4,3,2,1,0:T(8,128)(2,1)}, u32[]{:S(2)}, u32[]{:S(2)}) %all-to-all-start) | async-done | bytes 983072 | tf_op jit(solution)/shard_map/all_to_all | solution.py:344
  78.6 3.5 %shard_map.131 = (f32[2,128,160]{2,1,0:T(8,128)S(1)}, f32[2,128,160]{2,1,0:T(8,128)}) custom-call(s32[5]{0:T(128)S(1)} %stack.23.where_ref, bf16[8,3,4,16,320]{4,3,2,1,0:T(8,128)(2,1)} %all-to-all-done.rows_ref, bf16[160,2880]{1,0:T(8,128)(2,1)S(1)} %pad_maximum_fusion.weight_ref), custom_call_target="tpu_custom_call" | custom-call | flops 3000000000 | bytes 1904660 | tf_op jit(solution)/shard_map/pallas_call | solution.py:270
  82.8 3.3 %collective-permute-start.6 = (f32[2,128,160]{2,1,0:T(8,128)}, f32[2,128,160]{2,1,0:T(8,128)S(1)}, u32[]{:S(2)}, u32[]{:S(2)}) collective-permute-start(f32[2,128,160]{2,1,0:T(8,128)} %get-tuple-element.13), channel_id=1, source_target_pairs={{0,64},{64,0},{1,65},{65,1},{2,66},{66,2},{3,67},{67,3},{4,68},{68... | collective-permute-start | bytes 491528 | tf_op jit(solution)/shard_map/ppermute | solution.py:288
  87.4 1.0 fusion
  89.5 3.8 %collective-permute-done.7.got_ref = f32[128,160]{1,0:T(8,128)S(1)} collective-permute-done((f32[128,160]{1,0:T(8,128)S(1)}, f32[128,160]{1,0:T(8,128)S(1)}, u32[]{:S(2)}, u32[]{:S(2)}) %collective-permute-start.7) | collective-permute-done | bytes 81952 | tf_op jit(solution)/shard_map/ppermute | solution.py:288
  94.2 4.1 %all-to-all-start.1 = ((f32[8,8,128]{2,1,0:T(8,128)}), f32[8,8,128]{2,1,0:T(8,128)S(1)}, u32[]{:S(2)}, u32[]{:S(2)}) async-start(f32[8,8,128]{2,1,0:T(8,128)} %broadcast_in_dim.10), calls=%async_computation.1 | async-start | bytes 65536 | tf_op jit(solution)/shard_map/all_to_all | solution.py:357
  98.5 6.6 %all-to-all-done.1.stats_ref = f32[8,8,128]{2,1,0:T(8,128)S(1)} async-done(((f32[8,8,128]{2,1,0:T(8,128)}), f32[8,8,128]{2,1,0:T(8,128)S(1)}, u32[]{:S(2)}, u32[]{:S(2)}) %all-to-all-start.1) | async-done | bytes 32800 | tf_op jit(solution)/shard_map/all_to_all | solution.py:357
  105.3 10.3 %all_to_all.15.refs_0_ = bf16[8,16,160]{2,1,0:T(8,128)(2,1)S(1)} all-to-all(bf16[8,16,160]{2,1,0:T(8,128)(2,1)S(1)} %shard_map.133), channel_id=1, replica_groups=mesh['yl'=2,'c'=2,'yh'=2,'z'=8,'x'=4] {'z'}, dimensions={0} | all-to-all | bytes 81920 | tf_op jit(solution)/shard_map/all_to_all | solution.py:366
  115.6 3.7 %collective-permute-start.8 = (bf16[8,16,160]{2,1,0:T(8,128)(2,1)S(1)}, bf16[8,16,160]{2,1,0:T(8,128)(2,1)S(1)}, u32[]{:S(2)}, u32[]{:S(2)}) collective-permute-start(bf16[8,16,160]{2,1,0:T(8,128)(2,1)S(1)} %all_to_all.15.refs_0_), channel_id=1, source_target_pairs={{0,64},{64,0},{1,65},{65,1},{2,66},{66,2},{3,67},{67,3},{4,68},{68... | collective-permute-start | bytes 122888 | tf_op jit(solution)/shard_map/ppermute | solution.py:288
  121.0 2.1 %collective-permute-done.9.refs_2_ = bf16[8,16,160]{2,1,0:T(8,128)(2,1)S(1)} collective-permute-done((bf16[8,16,160]{2,1,0:T(8,128)(2,1)S(1)}, bf16[8,16,160]{2,1,0:T(8,128)(2,1)S(1)}, u32[]{:S(2)}, u32[]{:S(2)}) %collective-permute-start.9) | collective-permute-done | bytes 40992 | tf_op jit(solution)/shard_map/ppermute | solution.py:288
  123.2 1.4 collective-permute-done.10.refs_3_
  124.6 13.1 %all-gather.3.cloned.1.call-done = bf16[11776,384]{1,0:T(8,128)(2,1)} async-done(((bf16[368,384]{1,0:T(8,128)(2,1)}), bf16[11776,384]{1,0:T(8,128)(2,1)}) %all-gather.3.cloned.1.call-update) | async-done | bytes 9043984 | tf_op jit(solution)/shard_map/all_gather | solution.py:341
  137.6 3.6 %copy-done.1 = bf16[11776,384]{1,0:T(8,128)(2,1)S(1)} copy-done((bf16[11776,384]{1,0:T(8,128)(2,1)S(1)}, bf16[11776,384]{1,0:T(8,128)(2,1)}, u32[]{:S(2)}) %copy-start.1) | copy-done | bytes 9043992
  141.2 4.1 %shard_map.134 = (f32[2,16,1280]{2,1,0:T(8,128)S(1)}, f32[2,16,1280]{2,1,0:T(8,128)S(1)}, bf16[4,16,384]{2,1,0:T(8,128)(2,1)S(1)}, bf16[16,1280]{1,0:T(8,128)(2,1)S(1)}) custom-call(s32[5]{0:T(128)S(1)} %stack.23.where_ref, bf16[8,16,160]{2,1,0:T(8,128)(2,1)S(1)} %all_to_all.15.refs_0_, bf16[8,16,160]{2,1,0:T(8,128)(2,1)S(1)} %collective-permute-done.8.refs_1_, ...), custom_call_target="tpu_custom_call" | custom-call | flops 1000000000 | bytes 9207828 | tf_op jit(solution)/shard_map/pallas_call | solution.py:270
  145.3 1.4 collective-permute-start.13
  146.7 1.0 collective-permute-done.13
  147.7 1.3 collective-permute-start.14
  149.0 2.5 %collective-permute-done.14 = f32[16,1280]{1,0:T(8,128)S(1)} collective-permute-done((f32[16,1280]{1,0:T(8,128)S(1)}, f32[16,1280]{1,0:T(8,128)S(1)}, u32[]{:S(2)}, u32[]{:S(2)}) %collective-permute-start.14) | collective-permute-done | bytes 81952 | tf_op jit(solution)/shard_map/ppermute | solution.py:288
  151.5 1.3 collective-permute-start.15
  152.8 1.2 collective-permute-start.16
  154.0 0.8 collective-permute-start.17
  154.9 0.8 collective-permute-done.16.refs_2_
  155.7 1.2 collective-permute-done.17.refs_3_
  156.9 3.6 %shard_map.135 = (f32[2,16,1280]{2,1,0:T(8,128)S(1)}, f32[2,16,1280]{2,1,0:T(8,128)S(1)}) custom-call(s32[5]{0:T(128)S(1)} %stack.23.where_ref, bf16[16,1280]{1,0:T(8,128)(2,1)S(1)} %fusion.11.refs_0_, bf16[16,1280]{1,0:T(8,128)(2,1)S(1)} %collective-permute-done.15.refs_1_, bf16[16,1280]{1,0:T(8,128)(2,1)S(1)} %collective-permute-done.16.refs_2_, ...), custom_call_target="tpu_custom_call" | custom-call | flops 1000000000 | bytes 9207828 | tf_op jit(solution)/shard_map/pallas_call | solution.py:270
  160.5 1.6 collective-permute-start.18
  162.1 1.0 collective-permute-done.18
  163.1 0.9 collective-permute-start.19
  164.0 2.8 %collective-permute-done.19 = f32[16,1280]{1,0:T(8,128)S(1)} collective-permute-done((f32[16,1280]{1,0:T(8,128)S(1)}, f32[16,1280]{1,0:T(8,128)S(1)}, u32[]{:S(2)}, u32[]{:S(2)}) %collective-permute-start.19) | collective-permute-done | bytes 81952 | tf_op jit(solution)/shard_map/ppermute | solution.py:288
  166.9 1.3 collective-permute-start.20
  168.2 0.9 collective-permute-start.21
  169.0 0.8 collective-permute-start.22
  171.0 1.0 collective-permute-done.22.refs_3_
  172.0 1.2 shard_map.136
  (77 shorter events, 9.8 us)
Async XLA Ops:
  7.2 79.5 %copy-start = (bf16[1000,1280]{1,0:T(8,128)(2,1)S(1)}, bf16[1000,1280]{1,0:T(8,128)(2,1)}, u32[]{:S(2)}) copy-start(bf16[1000,1280]{1,0:T(8,128)(2,1)} %param.15) | copy-start | bytes 7680004
  7.2 13.2 %copy-start.9 = (bf16[4,1,16,320]{3,2,1,0:T(8,128)(2,1)S(1)}, bf16[4,1,16,320]{3,2,1,0:T(8,128)(2,1)}, u32[]{:S(2)}) copy-start(bf16[4,1,16,320]{3,2,1,0:T(8,128)(2,1)} %param.13) | copy-start | bytes 122884
  7.2 17.5 %copy-start.5 = (bf16[9,320,20]{1,2,0:T(8,128)(2,1)S(1)}, bf16[9,320,20]{1,2,0:T(8,128)(2,1)}, u32[]{:S(2)}) copy-start(bf16[9,320,20]{1,2,0:T(8,128)(2,1)} %param.14) | copy-start | bytes 345604
  7.2 130.4 %all-gather.3.cloned.1.call-start = ((), (), s32[]{:S(2)}) async-start(), calls=%async_computation.3 | async-start | bytes 9326592 | tf_op jit(solution)/shard_map/all_gather | solution.py:341
  8.3 26.6 %copy-start.6 = (bf16[4,1,16,320]{3,2,1,0:T(8,128)(2,1)S(1)}, bf16[4,1,16,320]{3,2,1,0:T(8,128)(2,1)}, u32[]{:S(2)}) copy-start(bf16[4,1,16,320]{3,2,1,0:T(8,128)(2,1)} %param.12) | copy-start | bytes 122884
  10.1 9.4 %collective-permute-start.12 = (bf16[20,2304]{1,0:T(8,128)(2,1)S(1)}, bf16[20,2304]{1,0:T(8,128)(2,1)S(1)}, u32[]{:S(2)}, u32[]{:S(2)}) collective-permute-start(bf16[20,2304]{1,0:T(8,128)(2,1)S(1)} %concatenate.21), channel_id=1, source_target_pairs={{32,0},{0,32},{33,1},{1,33},{34,2},{2,34},{35,3},{3,35},{36,4},{4,... | collective-permute-start | bytes 276488 | tf_op jit(solution)/shard_map/ppermute | solution.py:29
  14.9 4.6 %collective-permute-start.11 = (bf16[64,384]{1,0:T(8,128)(2,1)S(1)}, bf16[64,384]{1,0:T(8,128)(2,1)S(1)}, u32[]{:S(2)}, u32[]{:S(2)}) collective-permute-start(bf16[64,384]{1,0:T(8,128)(2,1)S(1)} %reshape.67), channel_id=1, source_target_pairs={{32,0},{0,32},{33,1},{1,33},{34,2},{2,34},{35,3},{3,35},{36,4},{4,... | collective-permute-start | bytes 147464 | tf_op jit(solution)/shard_map/ppermute | solution.py:29
  19.7 0.7 copy-start.4
  20.4 14.5 %collective-permute-start = (bf16[4,1,16,320]{3,2,1,0:T(8,128)(2,1)S(1)}, bf16[4,1,16,320]{3,2,1,0:T(8,128)(2,1)S(1)}, u32[]{:S(2)}, u32[]{:S(2)}) collective-permute-start(bf16[4,1,16,320]{3,2,1,0:T(8,128)(2,1)S(1)} %copy-done.9), channel_id=1, source_target_pairs={{0,1},{1,2},{2,3},{3,4},{4,5},{5,6},{6,7},{7,8},{8,9},{9,10},{10,1... | collective-permute-start | bytes 122888 | tf_op jit(solution)/shard_map/ppermute | solution.py:320
  23.4 11.5 %collective-permute-start.1 = (bf16[4,1,16,320]{3,2,1,0:T(8,128)(2,1)S(1)}, bf16[4,1,16,320]{3,2,1,0:T(8,128)(2,1)S(1)}, u32[]{:S(2)}, u32[]{:S(2)}) collective-permute-start(bf16[4,1,16,320]{3,2,1,0:T(8,128)(2,1)S(1)} %copy-done.9), channel_id=1, source_target_pairs={{1,0},{2,1},{3,2},{4,3},{5,4},{6,5},{7,6},{8,7},{9,8},{10,9},{11,1... | collective-permute-start | bytes 122888 | tf_op jit(solution)/shard_map/ppermute | solution.py:321
  24.9 15.5 %collective-permute-start.2 = (bf16[20,2880]{1,0:T(8,128)(2,1)S(1)}, bf16[20,2880]{1,0:T(8,128)(2,1)S(1)}, u32[]{:S(2)}, u32[]{:S(2)}) collective-permute-start(bf16[20,2880]{1,0:T(8,128)(2,1)S(1)} %reshape.61), channel_id=1, source_target_pairs={{32,0},{0,32},{33,1},{1,33},{34,2},{2,34},{35,3},{3,35},{36,4},{4,... | collective-permute-start | bytes 345608 | tf_op jit(solution)/shard_map/ppermute | solution.py:29
  36.2 42.4 %all-to-all-start = ((bf16[8,3,4,16,320]{4,3,2,1,0:T(8,128)(2,1)}), bf16[8,3,4,16,320]{4,3,2,1,0:T(8,128)(2,1)}, u32[]{:S(2)}, u32[]{:S(2)}) async-start(bf16[8,3,4,16,320]{4,3,2,1,0:T(8,128)(2,1)} %broadcast_in_dim.9), calls=%async_computation | async-start | bytes 2359296 | tf_op jit(solution)/shard_map/all_to_all | solution.py:344
  40.5 6.8 %collective-permute-start.3 = (bf16[40,2880]{1,0:T(8,128)(2,1)S(1)}, bf16[40,2880]{1,0:T(8,128)(2,1)S(1)}, u32[]{:S(2)}, u32[]{:S(2)}) collective-permute-start(bf16[40,2880]{1,0:T(8,128)(2,1)S(1)} %pad_maximum_fusion.1), channel_id=1, source_target_pairs={{1,0},{2,1},{3,2},{0,3},{5,4},{6,5},{7,6},{4,7},{9,8},{10,9},{11,1... | collective-permute-start | bytes 691208 | tf_op jit(solution)/shard_map/ppermute | solution.py:29
  43.6 6.9 %collective-permute-start.4 = (bf16[40,2880]{1,0:T(8,128)(2,1)S(1)}, bf16[40,2880]{1,0:T(8,128)(2,1)}, u32[]{:S(2)}, u32[]{:S(2)}) collective-permute-start(bf16[40,2880]{1,0:T(8,128)(2,1)S(1)} %pad_maximum_fusion.1), channel_id=1, source_target_pairs={{2,0},{3,1},{0,2},{1,3},{6,4},{7,5},{4,6},{5,7},{10,8},{11,9},{8,1... | collective-permute-start | bytes 691208 | tf_op jit(solution)/shard_map/ppermute | solution.py:29
  43.6 14.7 %collective-permute-start.5 = (bf16[40,2880]{1,0:T(8,128)(2,1)S(1)}, bf16[40,2880]{1,0:T(8,128)(2,1)}, u32[]{:S(2)}, u32[]{:S(2)}) collective-permute-start(bf16[40,2880]{1,0:T(8,128)(2,1)S(1)} %pad_maximum_fusion.1), channel_id=1, source_target_pairs={{3,0},{0,1},{1,2},{2,3},{7,4},{4,5},{5,6},{6,7},{11,8},{8,9},{9,10... | collective-permute-start | bytes 691208 | tf_op jit(solution)/shard_map/ppermute | solution.py:29
  59.8 29.5 %copy-start.7 = (f32[1280]{0:T(1024)S(1)}, f32[1280]{0:T(1024)}, u32[]{:S(2)}) copy-start(f32[1280]{0:T(1024)} %param.17) | copy-start | bytes 15364
  59.8 29.6 %copy-start.8 = (f32[1280]{0:T(1024)S(1)}, f32[1280]{0:T(1024)}, u32[]{:S(2)}) copy-start(f32[1280]{0:T(1024)} %param.18) | copy-start | bytes 15364
  82.1 0.7 copy-start.3
  82.8 4.6 %collective-permute-start.6 = (f32[2,128,160]{2,1,0:T(8,128)}, f32[2,128,160]{2,1,0:T(8,128)S(1)}, u32[]{:S(2)}, u32[]{:S(2)}) collective-permute-start(f32[2,128,160]{2,1,0:T(8,128)} %get-tuple-element.13), channel_id=1, source_target_pairs={{0,64},{64,0},{1,65},{65,1},{2,66},{66,2},{3,67},{67,3},{4,68},{68... | collective-permute-start | bytes 491528 | tf_op jit(solution)/shard_map/ppermute | solution.py:288
  88.4 4.9 %collective-permute-start.7 = (f32[128,160]{1,0:T(8,128)S(1)}, f32[128,160]{1,0:T(8,128)S(1)}, u32[]{:S(2)}, u32[]{:S(2)}) collective-permute-start(f32[128,160]{1,0:T(8,128)S(1)} %get-tuple-element.32), channel_id=1, source_target_pairs={{0,128},{128,0},{1,129},{129,1},{2,130},{130,2},{3,131},{131,3},{4... | collective-permute-start | bytes 245768 | tf_op jit(solution)/shard_map/ppermute | solution.py:288
  94.2 10.9 %all-to-all-start.1 = ((f32[8,8,128]{2,1,0:T(8,128)}), f32[8,8,128]{2,1,0:T(8,128)S(1)}, u32[]{:S(2)}, u32[]{:S(2)}) async-start(f32[8,8,128]{2,1,0:T(8,128)} %broadcast_in_dim.10), calls=%async_computation.1 | async-start | bytes 65536 | tf_op jit(solution)/shard_map/all_to_all | solution.py:357
  115.6 4.6 %collective-permute-start.8 = (bf16[8,16,160]{2,1,0:T(8,128)(2,1)S(1)}, bf16[8,16,160]{2,1,0:T(8,128)(2,1)S(1)}, u32[]{:S(2)}, u32[]{:S(2)}) collective-permute-start(bf16[8,16,160]{2,1,0:T(8,128)(2,1)S(1)} %all_to_all.15.refs_0_), channel_id=1, source_target_pairs={{0,64},{64,0},{1,65},{65,1},{2,66},{66,2},{3,67},{67,3},{4,68},{68... | collective-permute-start | bytes 122888 | tf_op jit(solution)/shard_map/ppermute | solution.py:288
  119.3 3.8 %collective-permute-start.9 = (bf16[8,16,160]{2,1,0:T(8,128)(2,1)S(1)}, bf16[8,16,160]{2,1,0:T(8,128)(2,1)S(1)}, u32[]{:S(2)}, u32[]{:S(2)}) collective-permute-start(bf16[8,16,160]{2,1,0:T(8,128)(2,1)S(1)} %all_to_all.15.refs_0_), channel_id=1, source_target_pairs={{0,128},{128,0},{1,129},{129,1},{2,130},{130,2},{3,131},{131,3},{4... | collective-permute-start | bytes 122888 | tf_op jit(solution)/shard_map/ppermute | solution.py:288
  120.2 4.3 %collective-permute-start.10 = (bf16[8,16,160]{2,1,0:T(8,128)(2,1)S(1)}, bf16[8,16,160]{2,1,0:T(8,128)(2,1)S(1)}, u32[]{:S(2)}, u32[]{:S(2)}) collective-permute-start(bf16[8,16,160]{2,1,0:T(8,128)(2,1)S(1)} %collective-permute-done.8.refs_1_), channel_id=1, source_target_pairs={{0,128},{128,0},{1,129},{129,1},{2,130},{130,2},{3,131},{131,3},{4... | collective-permute-start | bytes 122888 | tf_op jit(solution)/shard_map/ppermute | solution.py:288
  137.6 3.6 %copy-start.1 = (bf16[11776,384]{1,0:T(8,128)(2,1)S(1)}, bf16[11776,384]{1,0:T(8,128)(2,1)}, u32[]{:S(2)}) copy-start(bf16[11776,384]{1,0:T(8,128)(2,1)} %all-gather.3.cloned.1.call-done) | copy-start | bytes 27131908
  141.2 15.7 %copy-start.2 = (bf16[11776,384]{1,0:T(8,128)(2,1)S(1)}, bf16[11776,384]{1,0:T(8,128)(2,1)}, u32[]{:S(2)}) copy-start(bf16[11776,384]{1,0:T(8,128)(2,1)} %all-gather.3.cloned.1.call-done) | copy-start | bytes 27131908
  145.3 2.4 %collective-permute-start.13 = (f32[2,16,1280]{2,1,0:T(8,128)S(1)}, f32[2,16,1280]{2,1,0:T(8,128)S(1)}, u32[]{:S(2)}, u32[]{:S(2)}) collective-permute-start(f32[2,16,1280]{2,1,0:T(8,128)S(1)} %get-tuple-element.18), channel_id=1, source_target_pairs={{0,64},{64,0},{1,65},{65,1},{2,66},{66,2},{3,67},{67,3},{4,68},{68... | collective-permute-start | bytes 491528 | tf_op jit(solution)/shard_map/ppermute | solution.py:288
  147.7 3.8 %collective-permute-start.14 = (f32[16,1280]{1,0:T(8,128)S(1)}, f32[16,1280]{1,0:T(8,128)S(1)}, u32[]{:S(2)}, u32[]{:S(2)}) collective-permute-start(f32[16,1280]{1,0:T(8,128)S(1)} %fusion.7), channel_id=1, source_target_pairs={{0,128},{128,0},{1,129},{129,1},{2,130},{130,2},{3,131},{131,3},{4... | collective-permute-start | bytes 245768 | tf_op jit(solution)/shard_map/ppermute | solution.py:288
  151.5 2.5 %collective-permute-start.15 = (bf16[16,1280]{1,0:T(8,128)(2,1)S(1)}, bf16[16,1280]{1,0:T(8,128)(2,1)S(1)}, u32[]{:S(2)}, u32[]{:S(2)}) collective-permute-start(bf16[16,1280]{1,0:T(8,128)(2,1)S(1)} %fusion.11.refs_0_), channel_id=1, source_target_pairs={{0,64},{64,0},{1,65},{65,1},{2,66},{66,2},{3,67},{67,3},{4,68},{68... | collective-permute-start | bytes 122888 | tf_op jit(solution)/shard_map/ppermute | solution.py:288
  152.8 2.9 %collective-permute-start.16 = (bf16[16,1280]{1,0:T(8,128)(2,1)S(1)}, bf16[16,1280]{1,0:T(8,128)(2,1)S(1)}, u32[]{:S(2)}, u32[]{:S(2)}) collective-permute-start(bf16[16,1280]{1,0:T(8,128)(2,1)S(1)} %fusion.11.refs_0_), channel_id=1, source_target_pairs={{0,128},{128,0},{1,129},{129,1},{2,130},{130,2},{3,131},{131,3},{4... | collective-permute-start | bytes 122888 | tf_op jit(solution)/shard_map/ppermute | solution.py:288
  154.0 2.9 %collective-permute-start.17 = (bf16[16,1280]{1,0:T(8,128)(2,1)S(1)}, bf16[16,1280]{1,0:T(8,128)(2,1)S(1)}, u32[]{:S(2)}, u32[]{:S(2)}) collective-permute-start(bf16[16,1280]{1,0:T(8,128)(2,1)S(1)} %collective-permute-done.15.refs_1_), channel_id=1, source_target_pairs={{0,128},{128,0},{1,129},{129,1},{2,130},{130,2},{3,131},{131,3},{4... | collective-permute-start | bytes 122888 | tf_op jit(solution)/shard_map/ppermute | solution.py:288
  160.5 2.6 %collective-permute-start.18 = (f32[2,16,1280]{2,1,0:T(8,128)S(1)}, f32[2,16,1280]{2,1,0:T(8,128)S(1)}, u32[]{:S(2)}, u32[]{:S(2)}) collective-permute-start(f32[2,16,1280]{2,1,0:T(8,128)S(1)} %get-tuple-element.20), channel_id=1, source_target_pairs={{0,64},{64,0},{1,65},{65,1},{2,66},{66,2},{3,67},{67,3},{4,68},{68... | collective-permute-start | bytes 491528 | tf_op jit(solution)/shard_map/ppermute | solution.py:288
  163.1 3.8 %collective-permute-start.19 = (f32[16,1280]{1,0:T(8,128)S(1)}, f32[16,1280]{1,0:T(8,128)S(1)}, u32[]{:S(2)}, u32[]{:S(2)}) collective-permute-start(f32[16,1280]{1,0:T(8,128)S(1)} %fusion.2), channel_id=1, source_target_pairs={{0,128},{128,0},{1,129},{129,1},{2,130},{130,2},{3,131},{131,3},{4... | collective-permute-start | bytes 245768 | tf_op jit(solution)/shard_map/ppermute | solution.py:288
  166.9 2.2 %collective-permute-start.20 = (bf16[16,1280]{1,0:T(8,128)(2,1)S(1)}, bf16[16,1280]{1,0:T(8,128)(2,1)S(1)}, u32[]{:S(2)}, u32[]{:S(2)}) collective-permute-start(bf16[16,1280]{1,0:T(8,128)(2,1)S(1)} %fusion.6.refs_0_), channel_id=1, source_target_pairs={{0,64},{64,0},{1,65},{65,1},{2,66},{66,2},{3,67},{67,3},{4,68},{68... | collective-permute-start | bytes 122888 | tf_op jit(solution)/shard_map/ppermute | solution.py:288
  168.2 2.9 %collective-permute-start.21 = (bf16[16,1280]{1,0:T(8,128)(2,1)S(1)}, bf16[16,1280]{1,0:T(8,128)(2,1)S(1)}, u32[]{:S(2)}, u32[]{:S(2)}) collective-permute-start(bf16[16,1280]{1,0:T(8,128)(2,1)S(1)} %fusion.6.refs_0_), channel_id=1, source_target_pairs={{0,128},{128,0},{1,129},{129,1},{2,130},{130,2},{3,131},{131,3},{4... | collective-permute-start | bytes 122888 | tf_op jit(solution)/shard_map/ppermute | solution.py:288
  169.0 3.0 %collective-permute-start.22 = (bf16[16,1280]{1,0:T(8,128)(2,1)S(1)}, bf16[16,1280]{1,0:T(8,128)(2,1)S(1)}, u32[]{:S(2)}, u32[]{:S(2)}) collective-permute-start(bf16[16,1280]{1,0:T(8,128)(2,1)S(1)} %collective-permute-done.20.refs_1_), channel_id=1, source_target_pairs={{0,128},{128,0},{1,129},{129,1},{2,130},{130,2},{3,131},{131,3},{4... | collective-permute-start | bytes 122888 | tf_op jit(solution)/shard_map/ppermute | solution.py:288
Sparse Core Ops, SparseCore 0:
  20.5 117.0 all-gather.2
where the time goes:
time: 181 us; the launch traced here: 180 us
  waiting for transfers between devices  75.8 us (42%)
  starting transfers between devices  51.1 us (28%)
  between operations  15 us (8%)
  Pallas kernels  12.8 us (7%)
  local copies, waits for them, and re-layouts  12.2 us (7%)
  blocking collectives  10.3 us (6%)
  other arithmetic  2.78 us (2%)
    ppermute x15, starting transfers between devices, swap(): return lax.ppermute(value, axis, [(0, 1), (1, 0)])  20.8 us
    ppermute x15, waiting for transfers between devices, swap(): return lax.ppermute(value, axis, [(0, 1), (1, 0)])  18.8 us
    all_to_all x1, waiting for transfers between devices, shards(): rows = lax.all_to_all(jnp.broadcast_to(rows, (8,) + rows.shape), 'z', 0, 0)  18.8 us
    ppermute x6, waiting for transfers between devices, from_shift(): lax.ppermute(value, axis, [((i + offset) % size, i) for i in range(size)])  18.5 us
    ppermute x6, starting transfers between devices, from_shift(): lax.ppermute(value, axis, [((i + offset) % size, i) for i in range(size)])  17.6 us
    all_gather x1, waiting for transfers between devices, shards(): packed = lax.all_gather(packed, ('z', 'x'), axis=0, tiled=False)  13.1 us
    pallas_call x6, Pallas kernels, call(): pl.pallas_call(kernel, out_shape=out_shape, in_specs=[SMEM if smem and i...  12.8 us
    all_to_all x1, blocking collectives, shards(): activated = lax.all_to_all(activated, 'z', 0, 0)  10.3 us
  transfers between devices with their start and end apart: 26, of which 20 were waited for; matrix products, arithmetic and copies ran while one was open for 4% of the time, Pallas kernels for 2%

commit v1 on v0

--- a/solution.py
+++ b/solution.py
@@ -15,18 +15,27 @@
 SIZES = {"yl": 2, "c": 2, "yh": 2, "z": 8, "x": 4}
 FRAME = ("yl", "c")
 PATCH = ("yh", "z", "x")
+RING = (0, 1, 7, 2, 6, 3, 5, 4)
 BF16 = jnp.bfloat16
 F32 = jnp.float32
 VMEM = pl.BlockSpec(memory_space=pltpu.VMEM)
 SMEM = pl.BlockSpec(memory_space=pltpu.SMEM)
-HBM = pl.BlockSpec(memory_space=pl.ANY)
-PARAMS = pltpu.CompilerParams(vmem_limit_bytes=40 * 1024 * 1024)
+HBM = pl.BlockSpec(memory_space=pltpu.HBM)
 NT = (((1,), (1,)), ((), ()))
 
 
 def from_shift(value, axis, offset):
     size = SIZES[axis]
     return lax.ppermute(value, axis, [((i + offset) % size, i) for i in range(size)])
+
+
+def ring_gather(block):
+    ahead, behind = [block], [block]
+    for _ in range(3):
+        ahead.append(from_shift(ahead[-1], "z", 1))
+        behind.append(from_shift(behind[-1], "z", -1))
+    far = from_shift(ahead[-1], "z", 1)
+    return [block, ahead[1], behind[1], ahead[2], behind[2], ahead[3], behind[3], far]
 
 
 def pair_yh(block, yh):
@@ -47,14 +56,15 @@
     return ordered
 
 
-def conv_kernel(where_ref, rows_ref, weight_ref, keep_ref, send_ref):
-    yl, c = where_ref[0], where_ref[1]
+def conv_kernel(where_ref, *refs):
+    rows_refs, weight_ref, keep_ref, send_ref = refs[:8], refs[8], refs[9], refs[10]
+    yl, c, z = where_ref[0], where_ref[1], where_ref[2]
     column = lax.broadcasted_iota(jnp.int32, (512, 1), 0) % COLUMNS
     sums = []
     for col_tap in range(3):
         total = None
         for row_tap in range(3):
-            lhs = rows_ref[:, row_tap].reshape(512, 320)
+            lhs = jnp.concatenate([r[row_tap] for r in rows_refs], axis=0)
             tap = 3 * row_tap + col_tap
             part = lax.dot_general(
                 lhs,
@@ -67,17 +77,19 @@
     left = jnp.where(column == 0, 0.0, pltpu.roll(sums[0], 1, 0))
     right = jnp.where(column == COLUMNS - 1, 0.0, pltpu.roll(sums[2], 511, 0))
     hidden = (sums[1] + left + right).reshape(8, FRAMES, COLUMNS, 160)
-    for frame in range(FRAMES):
-        value = hidden[:, frame].reshape(128, 160)
-        place = yl ^ (frame // 2)
-
-        @pl.when(c == frame % 2)
-        def _():
-            keep_ref[place] = value
-
-        @pl.when(c != frame % 2)
-        def _():
-            send_ref[place] = value
+    for k, offset in enumerate(RING):
+        start = pl.multiple_of((z + offset) % 8 * COLUMNS, COLUMNS)
+        for frame in range(FRAMES):
+            value = hidden[k, frame]
+            place = yl ^ (frame // 2)
+
+            @pl.when(c == frame % 2)
+            def _():
+                keep_ref[place, pl.ds(start, COLUMNS)] = value
+
+            @pl.when(c != frame % 2)
+            def _():
+                send_ref[place, pl.ds(start, COLUMNS)] = value
 
 
 def group_masks():
@@ -142,32 +154,33 @@
     return jnp.concatenate([t[80 * h : 80 * h + 80] for h in range(2) for t in turned], axis=0)
 
 
-def chunk_of(w_scr, chunk, blocks):
+def chunk_of(w_ref, chunk, blocks):
     places = slice(4 * chunk, 4 * chunk + 4)
-    parts = [w_scr[places, 40 * k : 40 * k + 40, :].reshape(160, 384) for k in blocks]
+    parts = [w_ref[places, 40 * k : 40 * k + 40, :].reshape(160, 256) for k in blocks]
     return jnp.concatenate(parts, axis=1)
 
 
 def spatial_kernel(where_ref, *refs):
     acts, packed_ref = refs[:4], refs[4]
-    keep_ref, send_ref, fresh_ref, own_ref, w_scr, kv_scr, w_sem, kv_sem = refs[5:]
-    w_copy = pltpu.make_async_copy(packed_ref.at[:, 128:208], w_scr, w_sem)
-    kv_copy = pltpu.make_async_copy(packed_ref.at[:, :128], kv_scr, kv_sem)
+    out_ref, fresh_ref, own_ref, w_scr, kv_scr, w_sem, kv_sem = refs[5:]
+    w_copy = pltpu.make_async_copy(packed_ref.at[:, 192:312], w_scr, w_sem)
+    kv_copy = pltpu.make_async_copy(packed_ref.at[:, :192], kv_scr, kv_sem)
     w_copy.start()
     kv_copy.start()
     yl, c, place = where_ref[0], where_ref[1], where_ref[2] * 4 + where_ref[4]
     turn = order_matrix()
-    own = [
-        jnp.dot(acts[0][chunk], turn, preferred_element_type=F32).astype(BF16) for chunk in range(8)
-    ]
-    own_ref[...] = jnp.concatenate([o[:, 80 * h : 80 * h + 80] for h in range(2) for o in own], axis=1)
+    frames = [(2 * yl + c) ^ rel for rel in range(FRAMES)]
+    sources = [jnp.concatenate([a[chunk] for a in acts], axis=0) for chunk in range(8)]
+    own = [jnp.dot(v, turn, preferred_element_type=F32).astype(BF16) for v in sources]
+    own = jnp.concatenate([o[:, 80 * h : 80 * h + 80] for h in range(2) for o in own], axis=1)
+    for rel, frame in enumerate(frames):
+        own_ref[frame] = own[rel * COLUMNS : (rel + 1) * COLUMNS]
     w_copy.wait()
     projected = None
     out_weights = []
     for chunk in range(8):
-        lhs = jnp.concatenate([a[chunk] for a in acts], axis=0)
-        rhs = chunk_of(w_scr, chunk, (0, 1))
-        part = jnp.dot(lhs, rhs[:, :576], preferred_element_type=F32)
+        rhs = chunk_of(w_scr, chunk, range(3))
+        part = jnp.dot(sources[chunk], rhs[:, :576], preferred_element_type=F32)
         projected = part if projected is None else projected + part
         out_weights.append(rhs[:, 576:])
     projected = projected.astype(BF16)
@@ -177,33 +190,39 @@
     key_row = lax.broadcasted_iota(jnp.int32, (1, 512), 1) // COLUMNS
     attended = []
     kv_copy.wait()
-    for rel in range(FRAMES):
-        frame = (2 * yl + c) ^ rel
+    for rel, frame in enumerate(frames):
         mine = projected[rel * COLUMNS : (rel + 1) * COLUMNS]
         fresh = mine[:, 192:]
         fresh_ref[frame] = fresh
         query = mine[:, :192]
         zero = jnp.zeros_like(query)
         queries = jnp.concatenate([jnp.where(head_of == h, query, zero) for h in range(3)], axis=0)
-        blocks = [fresh]
+        start = pl.multiple_of(frame * COLUMNS, COLUMNS)
+        low, high = [], []
         for half in range(2):
-            start = pl.multiple_of(half * 64 + frame * COLUMNS, COLUMNS)
-            blocks.append(kv_scr[:, pl.ds(start, COLUMNS), :].reshape(512, 384))
-        scores = [
-            lax.dot_general(queries, b[:, :192], NT, preferred_element_type=F32) * score_scale
-            for b in blocks
-        ]
+            rows = pl.ds(half * 64 + start, COLUMNS)
+            low.append(kv_scr[:, rows, :].reshape(512, 256))
+            rows = pl.ds(128 + start, COLUMNS)
+            high.append(kv_scr[:, rows, half * 128 : half * 128 + 128].reshape(512, 128))
+        scores = [lax.dot_general(queries, fresh[:, :192], NT, preferred_element_type=F32)]
+        for a, b in zip(low, high):
+            far = lax.dot_general(queries[:, :128], a[:, :128], NT, preferred_element_type=F32)
+            scores.append(
+                far
+                + lax.dot_general(queries[:, 128:], b[:, :64], NT, preferred_element_type=F32)
+            )
+        scores = [s * score_scale for s in scores]
         scores[1] = jnp.where(key_row == place, -jnp.inf, scores[1])
         top = jnp.max(scores[0], axis=-1, keepdims=True)
         for s in scores[1:]:
             top = jnp.maximum(top, jnp.max(s, axis=-1, keepdims=True))
-        numerator, total = None, None
-        for s, b in zip(scores, blocks):
-            expo = jnp.exp(s - top)
-            part = jnp.dot(expo.astype(BF16), b[:, 192:], preferred_element_type=F32)
-            weight = jnp.sum(expo, axis=-1, keepdims=True)
-            numerator = part if numerator is None else numerator + part
-            total = weight if total is None else total + weight
+        expo = [jnp.exp(s - top) for s in scores]
+        total = sum(jnp.sum(e, axis=-1, keepdims=True) for e in expo)
+        expo = [e.astype(BF16) for e in expo]
+        numerator = jnp.dot(expo[0], fresh[:, 192:], preferred_element_type=F32)
+        for e, a, b in zip(expo[1:], low, high):
+            values = jnp.concatenate([a[:, 128:], b[:, 64:]], axis=1)
+            numerator = numerator + jnp.dot(e, values, preferred_element_type=F32)
         result = numerator / total
         rows = jnp.zeros((COLUMNS, 192), F32)
         for h in range(3):
@@ -211,32 +230,29 @@
         attended.append(rows.astype(BF16))
     attended = jnp.concatenate(attended, axis=0)
     part = lax.dot_general(attended, out_weights, NT, preferred_element_type=F32)
-    for rel in range(FRAMES):
-        target = send_ref if rel % 2 else keep_ref
-        target[rel // 2] = part[rel * COLUMNS : (rel + 1) * COLUMNS]
-
-
-def temporal_kernel(where_ref, *refs):
-    pieces, packed_ref = refs[:4], refs[4]
-    keep_ref, send_ref, w_scr, w_sem = refs[5:]
-    w_copy = pltpu.make_async_copy(packed_ref.at[:, 208:], w_scr, w_sem)
-    w_copy.start()
+    for rel, frame in enumerate(frames):
+        out_ref[frame] = part[rel * COLUMNS : (rel + 1) * COLUMNS]
+
+
+def temporal_kernel(own_ref, mine_ref, got_ref, packed_ref, out_ref, section_ref):
     turn = order_matrix()
-    section = jnp.concatenate([p[...] for p in pieces], axis=0)
+    total = mine_ref[...].astype(F32) + got_ref[...].astype(F32)
+    section = (own_ref[...].astype(F32) + total).astype(BF16)
+    section_ref[...] = section
+    section = section.reshape(64, CHANNELS)
     sources = []
     for chunk in range(8):
         lhs = jnp.concatenate(
             [section[:, k * 640 + chunk * 80 : k * 640 + chunk * 80 + 80] for k in range(2)], axis=1
         )
         sources.append(lax.dot_general(lhs, turn, NT, preferred_element_type=F32).astype(BF16))
-    w_copy.wait()
     temporal = None
     out_weights = []
     for chunk in range(8):
-        rhs = chunk_of(w_scr, chunk, range(4))
+        rhs = chunk_of(packed_ref, chunk, range(5))
         part = jnp.dot(sources[chunk], rhs[:, :960], preferred_element_type=F32)
         temporal = part if temporal is None else temporal + part
-        out_weights.append(rhs[:, 960:1280])
+        out_weights.append(rhs[:, 960:])
     temporal = temporal.astype(BF16)
     score_scale = HEAD_DIM ** (-0.5)
     row = lax.broadcasted_iota(jnp.int32, (64, 64), 0) % COLUMNS
@@ -253,29 +269,20 @@
     part = lax.dot_general(
         mixed, reorder_rows(turn, out_weights), NT, preferred_element_type=F32
     )
-    for rel in range(FRAMES):
-        target = send_ref if rel % 2 else keep_ref
-        target[rel // 2] = part[rel * COLUMNS : (rel + 1) * COLUMNS]
-
-
-def final_kernel(where_ref, *refs):
-    out_ref = refs[4]
-    mine = 2 * where_ref[0] + where_ref[1]
-    for rel in range(FRAMES):
-        out_ref[mine ^ rel] = refs[rel][...]
-
-
-def call(kernel, out_shape, *args, scratch=(), flops=0, smem=False, hbm=None):
+    out_ref[...] = part.reshape(FRAMES, COLUMNS, CHANNELS)
+
+
+def call(kernel, out_shape, *args, scratch=(), flops=0, smem=False, hbm=(), limit=40):
     moved = sum(a.size * a.dtype.itemsize for a in args)
     return pl.pallas_call(
         kernel,
         out_shape=out_shape,
         in_specs=[
-            SMEM if smem and i == 0 else HBM if i == hbm else VMEM for i in range(len(args))
+            SMEM if smem and i == 0 else HBM if i in hbm else VMEM for i in range(len(args))
         ],
         out_specs=jax.tree.map(lambda _: VMEM, out_shape),
         scratch_shapes=list(scratch),
-        compiler_params=PARAMS,
+        compiler_params=pltpu.CompilerParams(vmem_limit_bytes=limit * 1024 * 1024),
         cost_estimate=pl.CostEstimate(flops=flops, bytes_accessed=moved, transcendentals=0),
     )(*args)
 
@@ -292,6 +299,11 @@
     got = swap(send, "c")
     away = keep[1] + got[1]
     return keep[0] + got[0], swap(away, "yl")
+
+
+def sum_both(part):
+    mine = (part + swap(part, "c")).astype(BF16)
+    return mine, swap(mine, "yl")
 
 
 def gather_frame(piece):
@@ -329,21 +341,24 @@
             w_sout.T,
             w_tqkv.reshape(20, 960),
             w_tout.T,
-            jnp.zeros((20, 256), BF16),
         ],
         axis=1,
     )
-    kv = stale_kv.reshape(FRAMES * COLUMNS, 384)
+    keys, values = [stale_kv[:, :, :, k].reshape(FRAMES * COLUMNS, 192) for k in range(2)]
+    kv = jnp.concatenate(
+        [keys[:, :128], values[:, :128], keys[:, 128:], values[:, 128:]], axis=1
+    )
     kv_other = from_shift(kv, "yh", 1)
+    kv = [kv[:, :256], kv_other[:, :256], jnp.concatenate([kv[:, 256:], kv_other[:, 256:]], axis=1)]
     weights = pair_yh(weights, yh)
-    weights = [weights[:, k * 384 : (k + 1) * 384] for k in range(6)]
-    packed = jnp.concatenate([kv, kv_other] + weights, axis=0)
+    weights = [weights[:, k * 256 : (k + 1) * 256] for k in range(8)]
+    packed = jnp.concatenate(kv + weights, axis=0)
     packed = lax.all_gather(packed, ("z", "x"), axis=0, tiled=False)
 
     rows = jnp.concatenate([above, latent, below], axis=1).transpose(1, 0, 2, 3)
-    rows = lax.all_to_all(jnp.broadcast_to(rows, (8,) + rows.shape), "z", 0, 0)
+    rows = ring_gather(rows.reshape(3, FRAMES * COLUMNS, 320))
     half = shape((2, 128, 160), F32)
-    keep, send = call(conv_kernel, (half, half), where, rows, conv_full, smem=True, flops=3 * 10**9)
+    keep, send = call(conv_kernel, (half, half), where, *rows, conv_full, smem=True, flops=3 * 10**9)
     mine, got = sum_over_frame(keep, send)
 
     def channels_of(vector):
@@ -365,45 +380,36 @@
     )
     activated = lax.all_to_all(activated, "z", 0, 0)
 
-    share = shape((2, COLUMNS, CHANNELS), F32)
-    keep, send, fresh, own = call(
+    full = (FRAMES, COLUMNS, CHANNELS)
+    part, fresh, own = call(
         spatial_kernel,
-        (share, share, shape((FRAMES, COLUMNS, 384), BF16), shape((COLUMNS, CHANNELS), BF16)),
+        (shape(full, F32), shape((FRAMES, COLUMNS, 384), BF16), shape(full, BF16)),
         where,
         *gather_frame(activated),
         packed,
         smem=True,
-        hbm=5,
+        hbm=(5,),
+        limit=56,
         scratch=[
-            pltpu.VMEM((32, 80, 384), BF16),
-            pltpu.VMEM((32, 128, 384), BF16),
+            pltpu.VMEM((32, 120, 256), BF16),
+            pltpu.VMEM((32, 192, 256), BF16),
             pltpu.SemaphoreType.DMA,
             pltpu.SemaphoreType.DMA,
         ],
         flops=10**9,
     )
-    mine, got = sum_over_frame(keep, send)
-    section = (own.astype(F32) + (mine + got)).astype(BF16)
-    keep, send = call(
+    packed, part = lax.optimization_barrier((packed, part))
+    second = packed[:, 312:]
+    part, section = call(
         temporal_kernel,
-        (share, share),
-        where,
-        *gather_frame(section),
-        packed,
-        smem=True,
-        hbm=5,
-        scratch=[pltpu.VMEM((32, 160, 384), BF16), pltpu.SemaphoreType.DMA],
+        (shape(full, F32), shape(full, BF16)),
+        own,
+        *sum_both(part),
+        second,
         flops=10**9,
     )
-    mine, got = sum_over_frame(keep, send)
-    mixed = (section.astype(F32) + (mine + got)).astype(BF16)
-    mixed = call(
-        final_kernel,
-        shape((FRAMES, COLUMNS, CHANNELS), BF16),
-        where,
-        *gather_frame(mixed),
-        smem=True,
-    )
+    mine, got = sum_both(part)
+    mixed = (section.astype(F32) + (mine.astype(F32) + got.astype(F32))).astype(BF16)
     return (
         mixed.reshape(FRAMES, 1, COLUMNS, CHANNELS),
         fresh.reshape(FRAMES, 1, COLUMNS, 2, 192),

time: 181 us -> 159 us (0.88)
  waiting for transfers between devices: 75.8 us -> 39.4 us
  starting transfers between devices: 51.1 us -> 60.9 us
  other arithmetic: 2.78 us -> 6.52 us
  blocking collectives: 10.3 us -> 12.4 us
    all_to_all x1 -> x0, waiting for transfers between devices: 18.8 us -> none  [shards(): rows = lax.all_to_all(jnp.broadcast_to(rows, (8,) + rows.shape), 'z', 0, 0)]
    all_gather x1, waiting for transfers between devices: 13.1 us -> 0.01 us  [shards(): packed = lax.all_gather(packed, ('z', 'x'), axis=0, tiled=False)]
    ppermute x6 -> x13, starting transfers between devices: 17.6 us -> 30.2 us  [from_shift(): lax.ppermute(value, axis, [((i + offset) % size, i) for i in range(size)])]
    all_to_all x1, starting transfers between devices: 4.15 us -> 9.61 us  [shards(): lax.all_to_all(jnp.broadcast_to(stats, (8, 8, 128)), ('yh', 'x'), 0, 0)]
    ppermute x15 -> x9, starting transfers between devices: 20.8 us -> 15.8 us  [swap(): return lax.ppermute(value, axis, [(0, 1), (1, 0)])]
    all_to_all x1 -> x0, starting transfers between devices: 4.26 us -> none  [shards(): rows = lax.all_to_all(jnp.broadcast_to(rows, (8,) + rows.shape), 'z', 0, 0)]
    ppermute x6 -> x13, waiting for transfers between devices: 18.5 us -> 14.5 us  [from_shift(): lax.ppermute(value, axis, [((i + offset) % size, i) for i in range(size)])]
    slice x0 -> x7, local copies, waits for them, and re-layouts: none -> 3.19 us  [the longest x1 2.14 us: shards(): second = packed[:, 312:]]
  transfers between devices with their start and end apart: 26 -> 26, of which waited for: 20 -> 14; matrix products, arithmetic and copies ran while one was open for 4% -> 6% of each run, Pallas kernels for 2% -> 2%
where the time goes in v1:
time: 159 us
  starting transfers between devices  60.9 us (38%)
  waiting for transfers between devices  39.4 us (25%)
  between operations  15.2 us (10%)
  local copies, waits for them, and re-layouts  12.4 us (8%)
  blocking collectives  12.4 us (8%)
  Pallas kernels  11.8 us (7%)
  other arithmetic  6.52 us (4%)
    ppermute x13, starting transfers between devices, from_shift(): lax.ppermute(value, axis, [((i + offset) % size, i) for i in range(size)])  30.2 us
    ppermute x9, waiting for transfers between devices, swap(): return lax.ppermute(value, axis, [(0, 1), (1, 0)])  18.2 us
    ppermute x9, starting transfers between devices, swap(): return lax.ppermute(value, axis, [(0, 1), (1, 0)])  15.8 us
    ppermute x13, waiting for transfers between devices, from_shift(): lax.ppermute(value, axis, [((i + offset) % size, i) for i in range(size)])  14.5 us
    all_to_all x1, blocking collectives, shards(): activated = lax.all_to_all(activated, 'z', 0, 0)  12.4 us
    pallas_call x5, Pallas kernels, call(): pl.pallas_call(kernel, out_shape=out_shape, in_specs=[SMEM if smem and i...  11.8 us
    all_to_all x1, starting transfers between devices, shards(): lax.all_to_all(jnp.broadcast_to(stats, (8, 8, 128)), ('yh', 'x'), 0, 0)  9.61 us
    all_to_all x1, waiting for transfers between devices, shards(): lax.all_to_all(jnp.broadcast_to(stats, (8, 8, 128)), ('yh', 'x'), 0, 0)  6.57 us
  transfers between devices with their start and end apart: 26, of which 14 were waited for; matrix products, arithmetic and copies ran while one was open for 6% of the time, Pallas kernels for 2%

profile of v1, /device:TPU:1, one launch (start us, length us, event | category | flops | bytes accessed | tf_op | source)
XLA Modules:
  0.0 158.7 jit_solution(7196104075555540411)
XLA Ops:
  7.2 0.9 copy.34
  8.3 0.9 copy.35
  9.3 0.8 concatenate.35
  10.1 3.8 %collective-permute-start.19 = (bf16[20,2048]{1,0:T(8,128)(2,1)S(1)}, bf16[20,2048]{1,0:T(8,128)(2,1)S(1)}, u32[]{:S(2)}, u32[]{:S(2)}) collective-permute-start(bf16[20,2048]{1,0:T(8,128)(2,1)S(1)} %concatenate.35), channel_id=1, source_target_pairs={{32,0},{0,32},{33,1},{1,33},{34,2},{2,34},{35,3},{3,35},{36,4},{4,... | collective-permute-start | bytes 245768 | tf_op jit(solution)/shard_map/ppermute | solution.py:29
  13.9 1.0 fusion.10
  15.2 4.4 %collective-permute-done.18 = bf16[64,384]{1,0:T(8,128)(2,1)S(1)} collective-permute-done((bf16[64,384]{1,0:T(8,128)(2,1)S(1)}, bf16[64,384]{1,0:T(8,128)(2,1)S(1)}, u32[]{:S(2)}, u32[]{:S(2)}) %collective-permute-start.18) | collective-permute-done | bytes 49184 | tf_op jit(solution)/shard_map/ppermute | solution.py:29
  19.9 0.7 copy-done.12
  20.6 1.3 collective-permute-start.1
  21.9 4.0 %collective-permute-start = (bf16[4,1,16,320]{3,2,1,0:T(8,128)(2,1)S(1)}, bf16[4,1,16,320]{3,2,1,0:T(8,128)(2,1)S(1)}, u32[]{:S(2)}, u32[]{:S(2)}) collective-permute-start(bf16[4,1,16,320]{3,2,1,0:T(8,128)(2,1)S(1)} %copy-done.22), channel_id=1, source_target_pairs={{0,1},{1,2},{2,3},{3,4},{4,5},{5,6},{6,7},{7,8},{8,9},{9,10},{10,1... | collective-permute-start | bytes 122888 | tf_op jit(solution)/shard_map/ppermute | solution.py:332
  26.1 9.1 %collective-permute-start.9 = (bf16[20,2880]{1,0:T(8,128)(2,1)S(1)}, bf16[20,2880]{1,0:T(8,128)(2,1)S(1)}, u32[]{:S(2)}, u32[]{:S(2)}) collective-permute-start(bf16[20,2880]{1,0:T(8,128)(2,1)S(1)} %reshape.58), channel_id=1, source_target_pairs={{32,0},{0,32},{33,1},{1,33},{34,2},{2,34},{35,3},{3,35},{36,4},{4,... | collective-permute-start | bytes 345608 | tf_op jit(solution)/shard_map/ppermute | solution.py:29
  35.4 2.8 %collective-permute-start.2 = (bf16[3,64,320]{2,1,0:T(8,128)(2,1)S(1)}, bf16[3,64,320]{2,1,0:T(8,128)(2,1)S(1)}, u32[]{:S(2)}, u32[]{:S(2)}) collective-permute-start(bf16[3,64,320]{2,1,0:T(8,128)(2,1)S(1)} %bitcast.41), channel_id=1, source_target_pairs={{4,0},{8,4},{12,8},{16,12},{20,16},{24,20},{28,24},{0,28},{5,1},{9... | collective-permute-start | bytes 368648 | tf_op jit(solution)/shard_map/ppermute | solution.py:29
  38.2 0.9 broadcast_select_fusion.1
  39.2 0.8 pad_maximum_fusion.1
  39.9 4.1 %collective-permute-start.11 = (bf16[40,2880]{1,0:T(8,128)(2,1)}, bf16[40,2880]{1,0:T(8,128)(2,1)}, u32[]{:S(2)}, u32[]{:S(2)}) collective-permute-start(bf16[40,2880]{1,0:T(8,128)(2,1)} %pad_maximum_fusion.1), channel_id=1, source_target_pairs={{2,0},{3,1},{0,2},{1,3},{6,4},{7,5},{4,6},{5,7},{10,8},{11,9},{8,1... | collective-permute-start | bytes 691208 | tf_op jit(solution)/shard_map/ppermute | solution.py:29
  44.1 4.4 %collective-permute-start.4 = (bf16[3,64,320]{2,1,0:T(8,128)(2,1)S(1)}, bf16[3,64,320]{2,1,0:T(8,128)(2,1)S(1)}, u32[]{:S(2)}, u32[]{:S(2)}) collective-permute-start(bf16[3,64,320]{2,1,0:T(8,128)(2,1)S(1)} %collective-permute-done.2.refs_1_), channel_id=1, source_target_pairs={{4,0},{8,4},{12,8},{16,12},{20,16},{24,20},{28,24},{0,28},{5,1},{9... | collective-permute-start | bytes 368648 | tf_op jit(solution)/shard_map/ppermute | solution.py:29
  48.6 3.7 %collective-permute-done.5.refs_4_ = bf16[3,64,320]{2,1,0:T(8,128)(2,1)S(1)} collective-permute-done((bf16[3,64,320]{2,1,0:T(8,128)(2,1)S(1)}, bf16[3,64,320]{2,1,0:T(8,128)(2,1)S(1)}, u32[]{:S(2)}, u32[]{:S(2)}) %collective-permute-start.5) | collective-permute-done | bytes 122912 | tf_op jit(solution)/shard_map/ppermute | solution.py:29
  52.3 2.7 %collective-permute-start.6 = (bf16[3,64,320]{2,1,0:T(8,128)(2,1)S(1)}, bf16[3,64,320]{2,1,0:T(8,128)(2,1)S(1)}, u32[]{:S(2)}, u32[]{:S(2)}) collective-permute-start(bf16[3,64,320]{2,1,0:T(8,128)(2,1)S(1)} %collective-permute-done.4.refs_3_), channel_id=1, source_target_pairs={{4,0},{8,4},{12,8},{16,12},{20,16},{24,20},{28,24},{0,28},{5,1},{9... | collective-permute-start | bytes 368648 | tf_op jit(solution)/shard_map/ppermute | solution.py:29
  55.0 1.6 %select_select_fusion.3 = (bf16[40,2880]{1,0:T(8,128)(2,1)S(1)}, bf16[40,2880]{1,0:T(8,128)(2,1)S(1)}, bf16[40,2880]{1,0:T(8,128)(2,1)S(1)}, bf16[40,2880]{1,0:T(8,128)(2,1)S(1)}) fusion(bf16[40,2880]{1,0:T(8,128)(2,1)} %collective-permute-done.10, bf16[40,2880]{1,0:T(8,128)(2,1)} %collective-permute-done.11, bf16[40,2880]{1,0:T(8,128)(2,1)} %collective-permute-done.12, ...), kind=kLoop, calls=%fused_computation.22 | loop fusion | flops 1843200 | bytes 1843203 | tf_op jit(solution)/shard_map/jit(_where)/select_n | solution.py:54
  56.6 2.6 %collective-permute-done.6.refs_5_ = bf16[3,64,320]{2,1,0:T(8,128)(2,1)S(1)} collective-permute-done((bf16[3,64,320]{2,1,0:T(8,128)(2,1)S(1)}, bf16[3,64,320]{2,1,0:T(8,128)(2,1)S(1)}, u32[]{:S(2)}, u32[]{:S(2)}) %collective-permute-start.6) | collective-permute-done | bytes 122912 | tf_op jit(solution)/shard_map/ppermute | solution.py:29
  59.2 3.0 %collective-permute-start.8 = (bf16[3,64,320]{2,1,0:T(8,128)(2,1)S(1)}, bf16[3,64,320]{2,1,0:T(8,128)(2,1)S(1)}, u32[]{:S(2)}, u32[]{:S(2)}) collective-permute-start(bf16[3,64,320]{2,1,0:T(8,128)(2,1)S(1)} %collective-permute-done.6.refs_5_), channel_id=1, source_target_pairs={{4,0},{8,4},{12,8},{16,12},{20,16},{24,20},{28,24},{0,28},{5,1},{9... | collective-permute-start | bytes 368648 | tf_op jit(solution)/shard_map/ppermute | solution.py:29
  62.4 3.9 %collective-permute-done.8.refs_7_ = bf16[3,64,320]{2,1,0:T(8,128)(2,1)S(1)} collective-permute-done((bf16[3,64,320]{2,1,0:T(8,128)(2,1)S(1)}, bf16[3,64,320]{2,1,0:T(8,128)(2,1)S(1)}, u32[]{:S(2)}, u32[]{:S(2)}) %collective-permute-start.8) | collective-permute-done | bytes 122912 | tf_op jit(solution)/shard_map/ppermute | solution.py:29
  66.3 0.9 copy-done.4
  67.2 0.9 copy-done.6
  68.1 0.9 copy-done.8
  69.0 2.4 %shard_map.131 = (f32[2,128,160]{2,1,0:T(8,128)S(1)}, f32[2,128,160]{2,1,0:T(8,128)S(1)}) custom-call(s32[5]{0:T(128)S(1)} %stack.23.where_ref, bf16[3,64,320]{2,1,0:T(8,128)(2,1)S(1)} %bitcast.42, bf16[3,64,320]{2,1,0:T(8,128)(2,1)S(1)} %copy-done.4, bf16[3,64,320]{2,1,0:T(8,128)(2,1)S(1)} %collective-permute-done.3.refs_2_, ...), custom_call_target="tpu_custom_call" | custom-call | flops 3000000000 | bytes 1904660 | tf_op jit(solution)/shard_map/pallas_call | solution.py:277
  71.4 7.0 %collective-permute-start.13 = (f32[2,128,160]{2,1,0:T(8,128)S(1)}, f32[2,128,160]{2,1,0:T(8,128)}, u32[]{:S(2)}, u32[]{:S(2)}) collective-permute-start(f32[2,128,160]{2,1,0:T(8,128)S(1)} %get-tuple-element.14), channel_id=1, source_target_pairs={{0,64},{64,0},{1,65},{65,1},{2,66},{66,2},{3,67},{67,3},{4,68},{68... | collective-permute-start | bytes 491528 | tf_op jit(solution)/shard_map/ppermute | solution.py:295
  79.7 1.0 fusion.1
  81.2 4.5 %collective-permute-done.14.got_ref = f32[128,160]{1,0:T(8,128)S(1)} collective-permute-done((f32[128,160]{1,0:T(8,128)S(1)}, f32[128,160]{1,0:T(8,128)S(1)}, u32[]{:S(2)}, u32[]{:S(2)}) %collective-permute-start.14) | collective-permute-done | bytes 81952 | tf_op jit(solution)/shard_map/ppermute | solution.py:295
  86.5 9.6 %all-to-all-start = ((f32[8,8,128]{2,1,0:T(8,128)}), f32[8,8,128]{2,1,0:T(8,128)S(1)}, u32[]{:S(2)}, u32[]{:S(2)}) async-start(f32[8,8,128]{2,1,0:T(8,128)} %broadcast_in_dim.3), calls=%async_computation | async-start | bytes 65536 | tf_op jit(solution)/shard_map/all_to_all | solution.py:372
  96.3 6.6 %all-to-all-done.stats_ref = f32[8,8,128]{2,1,0:T(8,128)S(1)} async-done(((f32[8,8,128]{2,1,0:T(8,128)}), f32[8,8,128]{2,1,0:T(8,128)S(1)}, u32[]{:S(2)}, u32[]{:S(2)}) %all-to-all-start) | async-done | bytes 32800 | tf_op jit(solution)/shard_map/all_to_all | solution.py:372
  103.1 12.4 %all_to_all.10.refs_0_ = bf16[8,16,160]{2,1,0:T(8,128)(2,1)S(1)} all-to-all(bf16[8,16,160]{2,1,0:T(8,128)(2,1)S(1)} %shard_map.133), channel_id=1, replica_groups=mesh['yl'=2,'c'=2,'yh'=2,'z'=8,'x'=4] {'z'}, dimensions={0} | all-to-all | bytes 81920 | tf_op jit(solution)/shard_map/all_to_all | solution.py:381
  115.5 4.0 %collective-permute-start.15 = (bf16[8,16,160]{2,1,0:T(8,128)(2,1)S(1)}, bf16[8,16,160]{2,1,0:T(8,128)(2,1)S(1)}, u32[]{:S(2)}, u32[]{:S(2)}) collective-permute-start(bf16[8,16,160]{2,1,0:T(8,128)(2,1)S(1)} %all_to_all.10.refs_0_), channel_id=1, source_target_pairs={{0,64},{64,0},{1,65},{65,1},{2,66},{66,2},{3,67},{67,3},{4,68},{68... | collective-permute-start | bytes 122888 | tf_op jit(solution)/shard_map/ppermute | solution.py:295
  121.0 2.2 %collective-permute-done.16.refs_2_ = bf16[8,16,160]{2,1,0:T(8,128)(2,1)S(1)} collective-permute-done((bf16[8,16,160]{2,1,0:T(8,128)(2,1)S(1)}, bf16[8,16,160]{2,1,0:T(8,128)(2,1)S(1)}, u32[]{:S(2)}, u32[]{:S(2)}) %collective-permute-start.16) | collective-permute-done | bytes 40992 | tf_op jit(solution)/shard_map/ppermute | solution.py:295
  123.2 1.4 collective-permute-done.17.refs_3_
  125.2 6.3 %shard_map.134 = (f32[4,16,1280]{2,1,0:T(8,128)}, bf16[4,16,384]{2,1,0:T(8,128)(2,1)}, bf16[4,16,1280]{2,1,0:T(8,128)(2,1)}) custom-call(s32[5]{0:T(128)} %copy-done.2, bf16[8,16,160]{2,1,0:T(8,128)(2,1)} %copy-done.13, bf16[8,16,160]{2,1,0:T(8,128)(2,1)} %copy-done.15, bf16[8,16,160]{2,1,0:T(8,128)(2,1)} %copy-done.16, bf16[8,16,160]{2,1,0:T(8,128)(2,1)} %copy-done.17, ...), custom_call_target="tpu_custom_call" | custom-call | flops 1000000000 | bytes 8552468 | tf_op jit(solution)/shard_map/pallas_call | solution.py:277
  131.5 0.9 collective-permute-start.20
  132.4 1.5 collective-permute-done.20
  133.9 1.0 add_convert_fusion.2.mine_ref
  134.9 0.7 collective-permute-start.21
  135.6 2.1 %slice.87.packed_ref = bf16[32,200,256]{2,1,0:T(8,128)(2,1)S(1)} slice(bf16[32,512,256]{2,1,0:T(8,128)(2,1)} %bitcast.44), slice={[0:32], [312:512], [0:256]} | slice | bytes 6553600 | tf_op jit(solution)/shard_map/slice | solution.py:402
  137.7 2.7 %collective-permute-done.21.got_ref = bf16[4,16,1280]{2,1,0:T(8,128)(2,1)S(1)} collective-permute-done((bf16[4,16,1280]{2,1,0:T(8,128)(2,1)S(1)}, bf16[4,16,1280]{2,1,0:T(8,128)(2,1)S(1)}, u32[]{:S(2)}, u32[]{:S(2)}) %collective-permute-start.21) | collective-permute-done | bytes 163872 | tf_op jit(solution)/shard_map/ppermute | solution.py:295
  140.4 2.6 %shard_map.135 = (f32[4,16,1280]{2,1,0:T(8,128)S(1)}, bf16[4,16,1280]{2,1,0:T(8,128)(2,1)S(1)}) custom-call(bf16[4,16,1280]{2,1,0:T(8,128)(2,1)S(1)} %copy-done.1, bf16[4,16,1280]{2,1,0:T(8,128)(2,1)S(1)} %add_convert_fusion.2.mine_ref, bf16[4,16,1280]{2,1,0:T(8,128)(2,1)S(1)} %collective-permute-done.21.got_ref, bf16[32,200,256]{2,1,0:T(8,128)(2,1)S(1)} %slice.87.packed_ref), custom_call_target="tpu_custom_call" | custom-call | flops 1000000000 | bytes 3768320 | tf_op jit(solution)/shard_map/pallas_call | solution.py:277
  143.0 1.3 collective-permute-start.22
  144.3 1.3 collective-permute-done.22
  145.6 0.7 collective-permute-start.23
  146.3 0.7 reshape.67
  147.0 4.1 %collective-permute-done.23 = bf16[4,16,1280]{2,1,0:T(8,128)(2,1)S(1)} collective-permute-done((bf16[4,16,1280]{2,1,0:T(8,128)(2,1)S(1)}, bf16[4,16,1280]{2,1,0:T(8,128)(2,1)S(1)}, u32[]{:S(2)}, u32[]{:S(2)}) %collective-permute-start.23) | collective-permute-done | bytes 163872 | tf_op jit(solution)/shard_map/ppermute | solution.py:295
  151.1 0.7 fusion
  (111 shorter events, 5.7 us)
Async XLA Ops:
  7.2 71.9 %copy-start = (bf16[1000,1280]{1,0:T(8,128)(2,1)S(1)}, bf16[1000,1280]{1,0:T(8,128)(2,1)}, u32[]{:S(2)}) copy-start(bf16[1000,1280]{1,0:T(8,128)(2,1)} %param.15) | copy-start | bytes 7680004
  7.2 117.4 %all-gather.3.cloned.1.call-start = ((), (), s32[]{:S(2)}) async-start(), calls=%async_computation.2 | async-start | bytes 8650752 | tf_op jit(solution)/shard_map/all_gather | solution.py:356
  8.3 12.3 %copy-start.22 = (bf16[4,1,16,320]{3,2,1,0:T(8,128)(2,1)S(1)}, bf16[4,1,16,320]{3,2,1,0:T(8,128)(2,1)}, u32[]{:S(2)}) copy-start(bf16[4,1,16,320]{3,2,1,0:T(8,128)(2,1)} %param.13) | copy-start | bytes 122884
  8.3 17.6 %copy-start.14 = (bf16[9,320,20]{1,2,0:T(8,128)(2,1)S(1)}, bf16[9,320,20]{1,2,0:T(8,128)(2,1)}, u32[]{:S(2)}) copy-start(bf16[9,320,20]{1,2,0:T(8,128)(2,1)} %param.14) | copy-start | bytes 345604
  10.1 9.6 %collective-permute-start.19 = (bf16[20,2048]{1,0:T(8,128)(2,1)S(1)}, bf16[20,2048]{1,0:T(8,128)(2,1)S(1)}, u32[]{:S(2)}, u32[]{:S(2)}) collective-permute-start(bf16[20,2048]{1,0:T(8,128)(2,1)S(1)} %concatenate.35), channel_id=1, source_target_pairs={{32,0},{0,32},{33,1},{1,33},{34,2},{2,34},{35,3},{3,35},{36,4},{4,... | collective-permute-start | bytes 245768 | tf_op jit(solution)/shard_map/ppermute | solution.py:29
  15.0 20.2 %copy-start.18 = (bf16[4,1,16,320]{3,2,1,0:T(8,128)(2,1)S(1)}, bf16[4,1,16,320]{3,2,1,0:T(8,128)(2,1)}, u32[]{:S(2)}) copy-start(bf16[4,1,16,320]{3,2,1,0:T(8,128)(2,1)} %param.12) | copy-start | bytes 122884
  15.1 4.5 %collective-permute-start.18 = (bf16[64,384]{1,0:T(8,128)(2,1)S(1)}, bf16[64,384]{1,0:T(8,128)(2,1)S(1)}, u32[]{:S(2)}, u32[]{:S(2)}) collective-permute-start(bf16[64,384]{1,0:T(8,128)(2,1)S(1)} %pad_maximum_fusion.2), channel_id=1, source_target_pairs={{32,0},{0,32},{33,1},{1,33},{34,2},{2,34},{35,3},{3,35},{36,4},{4,... | collective-permute-start | bytes 147464 | tf_op jit(solution)/shard_map/ppermute | solution.py:29
  19.9 0.7 copy-start.12
  20.6 14.6 %collective-permute-start.1 = (bf16[4,1,16,320]{3,2,1,0:T(8,128)(2,1)S(1)}, bf16[4,1,16,320]{3,2,1,0:T(8,128)(2,1)S(1)}, u32[]{:S(2)}, u32[]{:S(2)}) collective-permute-start(bf16[4,1,16,320]{3,2,1,0:T(8,128)(2,1)S(1)} %copy-done.22), channel_id=1, source_target_pairs={{1,0},{2,1},{3,2},{4,3},{5,4},{6,5},{7,6},{8,7},{9,8},{10,9},{11,1... | collective-permute-start | bytes 122888 | tf_op jit(solution)/shard_map/ppermute | solution.py:333
  21.9 13.3 %collective-permute-start = (bf16[4,1,16,320]{3,2,1,0:T(8,128)(2,1)S(1)}, bf16[4,1,16,320]{3,2,1,0:T(8,128)(2,1)S(1)}, u32[]{:S(2)}, u32[]{:S(2)}) collective-permute-start(bf16[4,1,16,320]{3,2,1,0:T(8,128)(2,1)S(1)} %copy-done.22), channel_id=1, source_target_pairs={{0,1},{1,2},{2,3},{3,4},{4,5},{5,6},{6,7},{7,8},{8,9},{9,10},{10,1... | collective-permute-start | bytes 122888 | tf_op jit(solution)/shard_map/ppermute | solution.py:332
  26.1 12.1 %copy-start.11 = (bf16[20,2880]{1,0:T(8,128)(2,1)}, bf16[20,2880]{1,0:T(8,128)(2,1)S(1)}, u32[]{:S(2)}) copy-start(bf16[20,2880]{1,0:T(8,128)(2,1)S(1)} %reshape.58) | copy-start | bytes 345604
  26.1 12.1 %collective-permute-start.9 = (bf16[20,2880]{1,0:T(8,128)(2,1)S(1)}, bf16[20,2880]{1,0:T(8,128)(2,1)S(1)}, u32[]{:S(2)}, u32[]{:S(2)}) collective-permute-start(bf16[20,2880]{1,0:T(8,128)(2,1)S(1)} %reshape.58), channel_id=1, source_target_pairs={{32,0},{0,32},{33,1},{1,33},{34,2},{2,34},{35,3},{3,35},{36,4},{4,... | collective-permute-start | bytes 345608 | tf_op jit(solution)/shard_map/ppermute | solution.py:29
  35.3 8.7 %collective-permute-start.3 = (bf16[3,64,320]{2,1,0:T(8,128)(2,1)S(1)}, bf16[3,64,320]{2,1,0:T(8,128)(2,1)S(1)}, u32[]{:S(2)}, u32[]{:S(2)}) collective-permute-start(bf16[3,64,320]{2,1,0:T(8,128)(2,1)S(1)} %bitcast.40), channel_id=1, source_target_pairs={{28,0},{0,4},{4,8},{8,12},{12,16},{16,20},{20,24},{24,28},{29,1},{... | collective-permute-start | bytes 368648 | tf_op jit(solution)/shard_map/ppermute | solution.py:29
  35.4 8.7 %collective-permute-start.2 = (bf16[3,64,320]{2,1,0:T(8,128)(2,1)S(1)}, bf16[3,64,320]{2,1,0:T(8,128)(2,1)S(1)}, u32[]{:S(2)}, u32[]{:S(2)}) collective-permute-start(bf16[3,64,320]{2,1,0:T(8,128)(2,1)S(1)} %bitcast.41), channel_id=1, source_target_pairs={{4,0},{8,4},{12,8},{16,12},{20,16},{24,20},{28,24},{0,28},{5,1},{9... | collective-permute-start | bytes 368648 | tf_op jit(solution)/shard_map/ppermute | solution.py:29
  39.2 4.9 %copy-start.9 = (bf16[20,2880]{1,0:T(8,128)(2,1)}, bf16[20,2880]{1,0:T(8,128)(2,1)S(1)}, u32[]{:S(2)}) copy-start(bf16[20,2880]{1,0:T(8,128)(2,1)S(1)} %get-tuple-element.36) | copy-start | bytes 345604
  39.2 4.8 %copy-start.10 = (bf16[20,2880]{1,0:T(8,128)(2,1)}, bf16[20,2880]{1,0:T(8,128)(2,1)S(1)}, u32[]{:S(2)}) copy-start(bf16[20,2880]{1,0:T(8,128)(2,1)S(1)} %get-tuple-element.37) | copy-start | bytes 345604
  39.9 15.1 %collective-permute-start.12 = (bf16[40,2880]{1,0:T(8,128)(2,1)}, bf16[40,2880]{1,0:T(8,128)(2,1)}, u32[]{:S(2)}, u32[]{:S(2)}) collective-permute-start(bf16[40,2880]{1,0:T(8,128)(2,1)} %pad_maximum_fusion.1), channel_id=1, source_target_pairs={{3,0},{0,1},{1,2},{2,3},{7,4},{4,5},{5,6},{6,7},{11,8},{8,9},{9,10... | collective-permute-start | bytes 691208 | tf_op jit(solution)/shard_map/ppermute | solution.py:29
  39.9 15.1 %collective-permute-start.11 = (bf16[40,2880]{1,0:T(8,128)(2,1)}, bf16[40,2880]{1,0:T(8,128)(2,1)}, u32[]{:S(2)}, u32[]{:S(2)}) collective-permute-start(bf16[40,2880]{1,0:T(8,128)(2,1)} %pad_maximum_fusion.1), channel_id=1, source_target_pairs={{2,0},{3,1},{0,2},{1,3},{6,4},{7,5},{4,6},{5,7},{10,8},{11,9},{8,1... | collective-permute-start | bytes 691208 | tf_op jit(solution)/shard_map/ppermute | solution.py:29
  44.0 11.0 %collective-permute-start.10 = (bf16[40,2880]{1,0:T(8,128)(2,1)}, bf16[40,2880]{1,0:T(8,128)(2,1)}, u32[]{:S(2)}, u32[]{:S(2)}) collective-permute-start(bf16[40,2880]{1,0:T(8,128)(2,1)} %pad_maximum_fusion.1), channel_id=1, source_target_pairs={{1,0},{2,1},{3,2},{0,3},{5,4},{6,5},{7,6},{4,7},{9,8},{10,9},{11,1... | collective-permute-start | bytes 691208 | tf_op jit(solution)/shard_map/ppermute | solution.py:29
  44.0 8.3 %collective-permute-start.5 = (bf16[3,64,320]{2,1,0:T(8,128)(2,1)S(1)}, bf16[3,64,320]{2,1,0:T(8,128)(2,1)S(1)}, u32[]{:S(2)}, u32[]{:S(2)}) collective-permute-start(bf16[3,64,320]{2,1,0:T(8,128)(2,1)S(1)} %collective-permute-done.3.refs_2_), channel_id=1, source_target_pairs={{28,0},{0,4},{4,8},{8,12},{12,16},{16,20},{20,24},{24,28},{29,1},{... | collective-permute-start | bytes 368648 | tf_op jit(solution)/shard_map/ppermute | solution.py:29
  44.1 18.2 %copy-start.3 = (bf16[3,64,320]{2,1,0:T(8,128)(2,1)}, bf16[3,64,320]{2,1,0:T(8,128)(2,1)S(1)}, u32[]{:S(2)}) copy-start(bf16[3,64,320]{2,1,0:T(8,128)(2,1)S(1)} %collective-permute-done.2.refs_1_) | copy-start | bytes 368644
  44.1 8.2 %collective-permute-start.4 = (bf16[3,64,320]{2,1,0:T(8,128)(2,1)S(1)}, bf16[3,64,320]{2,1,0:T(8,128)(2,1)S(1)}, u32[]{:S(2)}, u32[]{:S(2)}) collective-permute-start(bf16[3,64,320]{2,1,0:T(8,128)(2,1)S(1)} %collective-permute-done.2.refs_1_), channel_id=1, source_target_pairs={{4,0},{8,4},{12,8},{16,12},{20,16},{24,20},{28,24},{0,28},{5,1},{9... | collective-permute-start | bytes 368648 | tf_op jit(solution)/shard_map/ppermute | solution.py:29
  48.6 17.6 %copy-start.2 = (s32[5]{0:T(128)}, s32[5]{0:T(128)S(1)}, u32[]{:S(2)}) copy-start(s32[5]{0:T(128)S(1)} %stack.23.where_ref) | copy-start | bytes 64
  52.3 10.1 %copy-start.5 = (bf16[3,64,320]{2,1,0:T(8,128)(2,1)}, bf16[3,64,320]{2,1,0:T(8,128)(2,1)S(1)}, u32[]{:S(2)}) copy-start(bf16[3,64,320]{2,1,0:T(8,128)(2,1)S(1)} %collective-permute-done.5.refs_4_) | copy-start | bytes 368644
  52.3 10.1 %collective-permute-start.7 = (bf16[3,64,320]{2,1,0:T(8,128)(2,1)S(1)}, bf16[3,64,320]{2,1,0:T(8,128)(2,1)S(1)}, u32[]{:S(2)}, u32[]{:S(2)}) collective-permute-start(bf16[3,64,320]{2,1,0:T(8,128)(2,1)S(1)} %collective-permute-done.5.refs_4_), channel_id=1, source_target_pairs={{28,0},{0,4},{4,8},{8,12},{12,16},{16,20},{20,24},{24,28},{29,1},{... | collective-permute-start | bytes 368648 | tf_op jit(solution)/shard_map/ppermute | solution.py:29
  52.3 10.1 %copy-start.7 = (bf16[3,64,320]{2,1,0:T(8,128)(2,1)}, bf16[3,64,320]{2,1,0:T(8,128)(2,1)S(1)}, u32[]{:S(2)}) copy-start(bf16[3,64,320]{2,1,0:T(8,128)(2,1)S(1)} %collective-permute-done.4.refs_3_) | copy-start | bytes 368644
  52.3 6.9 %collective-permute-start.6 = (bf16[3,64,320]{2,1,0:T(8,128)(2,1)S(1)}, bf16[3,64,320]{2,1,0:T(8,128)(2,1)S(1)}, u32[]{:S(2)}, u32[]{:S(2)}) collective-permute-start(bf16[3,64,320]{2,1,0:T(8,128)(2,1)S(1)} %collective-permute-done.4.refs_3_), channel_id=1, source_target_pairs={{4,0},{8,4},{12,8},{16,12},{20,16},{24,20},{28,24},{0,28},{5,1},{9... | collective-permute-start | bytes 368648 | tf_op jit(solution)/shard_map/ppermute | solution.py:29
  59.2 7.0 %collective-permute-start.8 = (bf16[3,64,320]{2,1,0:T(8,128)(2,1)S(1)}, bf16[3,64,320]{2,1,0:T(8,128)(2,1)S(1)}, u32[]{:S(2)}, u32[]{:S(2)}) collective-permute-start(bf16[3,64,320]{2,1,0:T(8,128)(2,1)S(1)} %collective-permute-done.6.refs_5_), channel_id=1, source_target_pairs={{4,0},{8,4},{12,8},{16,12},{20,16},{24,20},{28,24},{0,28},{5,1},{9... | collective-permute-start | bytes 368648 | tf_op jit(solution)/shard_map/ppermute | solution.py:29
  62.3 18.6 %copy-start.20 = (f32[1280]{0:T(1024)S(1)}, f32[1280]{0:T(1024)}, u32[]{:S(2)}) copy-start(f32[1280]{0:T(1024)} %param.17) | copy-start | bytes 15364
  62.3 18.8 %copy-start.21 = (f32[1280]{0:T(1024)S(1)}, f32[1280]{0:T(1024)}, u32[]{:S(2)}) copy-start(f32[1280]{0:T(1024)} %param.18) | copy-start | bytes 15364
  66.3 0.9 copy-start.4
  67.2 0.9 copy-start.6
  68.1 0.9 copy-start.8
  71.4 8.3 %collective-permute-start.13 = (f32[2,128,160]{2,1,0:T(8,128)S(1)}, f32[2,128,160]{2,1,0:T(8,128)}, u32[]{:S(2)}, u32[]{:S(2)}) collective-permute-start(f32[2,128,160]{2,1,0:T(8,128)S(1)} %get-tuple-element.14), channel_id=1, source_target_pairs={{0,64},{64,0},{1,65},{65,1},{2,66},{66,2},{3,67},{67,3},{4,68},{68... | collective-permute-start | bytes 491528 | tf_op jit(solution)/shard_map/ppermute | solution.py:295
  80.7 4.9 %collective-permute-start.14 = (f32[128,160]{1,0:T(8,128)S(1)}, f32[128,160]{1,0:T(8,128)S(1)}, u32[]{:S(2)}, u32[]{:S(2)}) collective-permute-start(f32[128,160]{1,0:T(8,128)S(1)} %get-tuple-element.34), channel_id=1, source_target_pairs={{0,128},{128,0},{1,129},{129,1},{2,130},{130,2},{3,131},{131,3},{4... | collective-permute-start | bytes 245768 | tf_op jit(solution)/shard_map/ppermute | solution.py:295
  86.5 16.4 %all-to-all-start = ((f32[8,8,128]{2,1,0:T(8,128)}), f32[8,8,128]{2,1,0:T(8,128)S(1)}, u32[]{:S(2)}, u32[]{:S(2)}) async-start(f32[8,8,128]{2,1,0:T(8,128)} %broadcast_in_dim.3), calls=%async_computation | async-start | bytes 65536 | tf_op jit(solution)/shard_map/all_to_all | solution.py:372
  115.5 9.1 %copy-start.13 = (bf16[8,16,160]{2,1,0:T(8,128)(2,1)}, bf16[8,16,160]{2,1,0:T(8,128)(2,1)S(1)}, u32[]{:S(2)}) copy-start(bf16[8,16,160]{2,1,0:T(8,128)(2,1)S(1)} %all_to_all.10.refs_0_) | copy-start | bytes 122884
  115.5 4.9 %collective-permute-start.15 = (bf16[8,16,160]{2,1,0:T(8,128)(2,1)S(1)}, bf16[8,16,160]{2,1,0:T(8,128)(2,1)S(1)}, u32[]{:S(2)}, u32[]{:S(2)}) collective-permute-start(bf16[8,16,160]{2,1,0:T(8,128)(2,1)S(1)} %all_to_all.10.refs_0_), channel_id=1, source_target_pairs={{0,64},{64,0},{1,65},{65,1},{2,66},{66,2},{3,67},{67,3},{4,68},{68... | collective-permute-start | bytes 122888 | tf_op jit(solution)/shard_map/ppermute | solution.py:295
  119.4 3.7 %collective-permute-start.16 = (bf16[8,16,160]{2,1,0:T(8,128)(2,1)S(1)}, bf16[8,16,160]{2,1,0:T(8,128)(2,1)S(1)}, u32[]{:S(2)}, u32[]{:S(2)}) collective-permute-start(bf16[8,16,160]{2,1,0:T(8,128)(2,1)S(1)} %all_to_all.10.refs_0_), channel_id=1, source_target_pairs={{0,128},{128,0},{1,129},{129,1},{2,130},{130,2},{3,131},{131,3},{4... | collective-permute-start | bytes 122888 | tf_op jit(solution)/shard_map/ppermute | solution.py:295
  120.3 4.2 %copy-start.15 = (bf16[8,16,160]{2,1,0:T(8,128)(2,1)}, bf16[8,16,160]{2,1,0:T(8,128)(2,1)S(1)}, u32[]{:S(2)}) copy-start(bf16[8,16,160]{2,1,0:T(8,128)(2,1)S(1)} %collective-permute-done.15.refs_1_) | copy-start | bytes 122884
  120.3 4.2 %collective-permute-start.17 = (bf16[8,16,160]{2,1,0:T(8,128)(2,1)S(1)}, bf16[8,16,160]{2,1,0:T(8,128)(2,1)S(1)}, u32[]{:S(2)}, u32[]{:S(2)}) collective-permute-start(bf16[8,16,160]{2,1,0:T(8,128)(2,1)S(1)} %collective-permute-done.15.refs_1_), channel_id=1, source_target_pairs={{0,128},{128,0},{1,129},{129,1},{2,130},{130,2},{3,131},{131,3},{4... | collective-permute-start | bytes 122888 | tf_op jit(solution)/shard_map/ppermute | solution.py:295
  123.2 1.4 copy-start.16
  131.5 2.3 %collective-permute-start.20 = (f32[4,16,1280]{2,1,0:T(8,128)}, f32[4,16,1280]{2,1,0:T(8,128)S(1)}, u32[]{:S(2)}, u32[]{:S(2)}) collective-permute-start(f32[4,16,1280]{2,1,0:T(8,128)} %get-tuple-element.19), channel_id=1, source_target_pairs={{0,64},{64,0},{1,65},{65,1},{2,66},{66,2},{3,67},{67,3},{4,68},{68... | collective-permute-start | bytes 983048 | tf_op jit(solution)/shard_map/ppermute | solution.py:295
  134.9 5.5 %copy-start.1 = (bf16[4,16,1280]{2,1,0:T(8,128)(2,1)S(1)}, bf16[4,16,1280]{2,1,0:T(8,128)(2,1)}, u32[]{:S(2)}) copy-start(bf16[4,16,1280]{2,1,0:T(8,128)(2,1)} %get-tuple-element.17.own_ref) | copy-start | bytes 491524
  134.9 5.5 %collective-permute-start.21 = (bf16[4,16,1280]{2,1,0:T(8,128)(2,1)S(1)}, bf16[4,16,1280]{2,1,0:T(8,128)(2,1)S(1)}, u32[]{:S(2)}, u32[]{:S(2)}) collective-permute-start(bf16[4,16,1280]{2,1,0:T(8,128)(2,1)S(1)} %add_convert_fusion.2.mine_ref), channel_id=1, source_target_pairs={{0,128},{128,0},{1,129},{129,1},{2,130},{130,2},{3,131},{131,3},{4... | collective-permute-start | bytes 491528 | tf_op jit(solution)/shard_map/ppermute | solution.py:295
  140.4 5.9 %copy-start.19 = (bf16[4,16,384]{2,1,0:T(8,128)(2,1)S(1)}, bf16[4,16,384]{2,1,0:T(8,128)(2,1)}, u32[]{:S(2)}) copy-start(bf16[4,16,384]{2,1,0:T(8,128)(2,1)} %get-tuple-element.23) | copy-start | bytes 147460
  143.0 2.5 %collective-permute-start.22 = (f32[4,16,1280]{2,1,0:T(8,128)S(1)}, f32[4,16,1280]{2,1,0:T(8,128)S(1)}, u32[]{:S(2)}, u32[]{:S(2)}) collective-permute-start(f32[4,16,1280]{2,1,0:T(8,128)S(1)} %get-tuple-element.22), channel_id=1, source_target_pairs={{0,64},{64,0},{1,65},{65,1},{2,66},{66,2},{3,67},{67,3},{4,68},{68... | collective-permute-start | bytes 983048 | tf_op jit(solution)/shard_map/ppermute | solution.py:295
  145.6 5.5 %collective-permute-start.23 = (bf16[4,16,1280]{2,1,0:T(8,128)(2,1)S(1)}, bf16[4,16,1280]{2,1,0:T(8,128)(2,1)S(1)}, u32[]{:S(2)}, u32[]{:S(2)}) collective-permute-start(bf16[4,16,1280]{2,1,0:T(8,128)(2,1)S(1)} %add_convert_fusion.1), channel_id=1, source_target_pairs={{0,128},{128,0},{1,129},{129,1},{2,130},{130,2},{3,131},{131,3},{4... | collective-permute-start | bytes 491528 | tf_op jit(solution)/shard_map/ppermute | solution.py:295
  (1 other events, 0.6 us)
Sparse Core Ops, SparseCore 0:
  20.7 101.9 all-gather.2

commit v2 on v1

--- a/solution.py
+++ b/solution.py
@@ -168,11 +168,9 @@
     w_copy.start()
     kv_copy.start()
     yl, c, place = where_ref[0], where_ref[1], where_ref[2] * 4 + where_ref[4]
-    turn = order_matrix()
     frames = [(2 * yl + c) ^ rel for rel in range(FRAMES)]
     sources = [jnp.concatenate([a[chunk] for a in acts], axis=0) for chunk in range(8)]
-    own = [jnp.dot(v, turn, preferred_element_type=F32).astype(BF16) for v in sources]
-    own = jnp.concatenate([o[:, 80 * h : 80 * h + 80] for h in range(2) for o in own], axis=1)
+    own = jnp.concatenate(sources, axis=1)
     for rel, frame in enumerate(frames):
         own_ref[frame] = own[rel * COLUMNS : (rel + 1) * COLUMNS]
     w_copy.wait()
@@ -184,7 +182,7 @@
         projected = part if projected is None else projected + part
         out_weights.append(rhs[:, 576:])
     projected = projected.astype(BF16)
-    out_weights = reorder_rows(turn, out_weights)
+    out_weights = jnp.concatenate(out_weights, axis=0)
     score_scale = HEAD_DIM ** (-0.5)
     head_of = lax.broadcasted_iota(jnp.int32, (COLUMNS, 192), 1) // HEAD_DIM
     key_row = lax.broadcasted_iota(jnp.int32, (1, 512), 1) // COLUMNS
@@ -231,21 +229,13 @@
     attended = jnp.concatenate(attended, axis=0)
     part = lax.dot_general(attended, out_weights, NT, preferred_element_type=F32)
     for rel, frame in enumerate(frames):
-        out_ref[frame] = part[rel * COLUMNS : (rel + 1) * COLUMNS]
+        out_ref[frame] = part[rel * COLUMNS : (rel + 1) * COLUMNS].astype(BF16)
 
 
 def temporal_kernel(own_ref, mine_ref, got_ref, packed_ref, out_ref, section_ref):
-    turn = order_matrix()
     total = mine_ref[...].astype(F32) + got_ref[...].astype(F32)
-    section = (own_ref[...].astype(F32) + total).astype(BF16)
-    section_ref[...] = section
-    section = section.reshape(64, CHANNELS)
-    sources = []
-    for chunk in range(8):
-        lhs = jnp.concatenate(
-            [section[:, k * 640 + chunk * 80 : k * 640 + chunk * 80 + 80] for k in range(2)], axis=1
-        )
-        sources.append(lax.dot_general(lhs, turn, NT, preferred_element_type=F32).astype(BF16))
+    section = (own_ref[...].astype(F32) + total).astype(BF16).reshape(64, CHANNELS)
+    sources = [section[:, chunk * 160 : (chunk + 1) * 160] for chunk in range(8)]
     temporal = None
     out_weights = []
     for chunk in range(8):
@@ -266,10 +256,14 @@
         expo, total = softmax_parts(jnp.where(row == col, scores, -jnp.inf))
         outs.append(jnp.dot(expo, value, preferred_element_type=F32) / total)
     mixed = jnp.concatenate(outs, axis=1).astype(BF16)
+    turn = order_matrix()
+    turned = [jnp.dot(v, turn, preferred_element_type=F32).astype(BF16) for v in sources]
+    turned = jnp.concatenate([t[:, 80 * h : 80 * h + 80] for h in range(2) for t in turned], axis=1)
+    section_ref[...] = turned.reshape(FRAMES, COLUMNS, CHANNELS)
     part = lax.dot_general(
         mixed, reorder_rows(turn, out_weights), NT, preferred_element_type=F32
     )
-    out_ref[...] = part.reshape(FRAMES, COLUMNS, CHANNELS)
+    out_ref[...] = part.astype(BF16).reshape(FRAMES, COLUMNS, CHANNELS)
 
 
 def call(kernel, out_shape, *args, scratch=(), flops=0, smem=False, hbm=(), limit=40):
@@ -302,7 +296,7 @@
 
 
 def sum_both(part):
-    mine = (part + swap(part, "c")).astype(BF16)
+    mine = (part.astype(F32) + swap(part, "c").astype(F32)).astype(BF16)
     return mine, swap(mine, "yl")
 
 
@@ -383,7 +377,7 @@
     full = (FRAMES, COLUMNS, CHANNELS)
     part, fresh, own = call(
         spatial_kernel,
-        (shape(full, F32), shape((FRAMES, COLUMNS, 384), BF16), shape(full, BF16)),
+        (shape(full, BF16), shape((FRAMES, COLUMNS, 384), BF16), shape(full, BF16)),
         where,
         *gather_frame(activated),
         packed,
@@ -402,7 +396,7 @@
     second = packed[:, 312:]
     part, section = call(
         temporal_kernel,
-        (shape(full, F32), shape(full, BF16)),
+        (shape(full, BF16), shape(full, BF16)),
         own,
         *sum_both(part),
         second,

time: 159 us -> 159 us (level)
  no operation moved by 1% of the time
where the time goes in v2:
time: 159 us; the launch traced here: 158 us
  starting transfers between devices  60.9 us (38%)
  waiting for transfers between devices  38.9 us (24%)
  between operations  15.2 us (10%)
  local copies, waits for them, and re-layouts  12.4 us (8%)
  blocking collectives  12.4 us (8%)
  Pallas kernels  11.6 us (7%)
  other arithmetic  6.48 us (4%)
    ppermute x13, starting transfers between devices, from_shift(): lax.ppermute(value, axis, [((i + offset) % size, i) for i in range(size)])  30.2 us
    ppermute x9, waiting for transfers between devices, swap(): return lax.ppermute(value, axis, [(0, 1), (1, 0)])  17.8 us
    ppermute x9, starting transfers between devices, swap(): return lax.ppermute(value, axis, [(0, 1), (1, 0)])  15.8 us
    ppermute x13, waiting for transfers between devices, from_shift(): lax.ppermute(value, axis, [((i + offset) % size, i) for i in range(size)])  14.5 us
    all_to_all x1, blocking collectives, shards(): activated = lax.all_to_all(activated, 'z', 0, 0)  12.4 us
    pallas_call x5, Pallas kernels, call(): pl.pallas_call(kernel, out_shape=out_shape, in_specs=[SMEM if smem and i...  11.6 us
    all_to_all x1, starting transfers between devices, shards(): lax.all_to_all(jnp.broadcast_to(stats, (8, 8, 128)), ('yh', 'x'), 0, 0)  9.61 us
    all_to_all x1, waiting for transfers between devices, shards(): lax.all_to_all(jnp.broadcast_to(stats, (8, 8, 128)), ('yh', 'x'), 0, 0)  6.57 us
  transfers between devices with their start and end apart: 26, of which 14 were waited for; matrix products, arithmetic and copies ran while one was open for 6% of the time, Pallas kernels for 2%

profile of v2, /device:TPU:1, one launch (start us, length us, event | category | flops | bytes accessed | tf_op | source)
XLA Modules:
  0.0 157.9 jit_solution(11557559535094064340)
XLA Ops:
  7.2 0.9 copy.34
  8.3 0.9 copy.35
  9.3 0.8 concatenate.35
  10.1 3.8 %collective-permute-start.19 = (bf16[20,2048]{1,0:T(8,128)(2,1)S(1)}, bf16[20,2048]{1,0:T(8,128)(2,1)S(1)}, u32[]{:S(2)}, u32[]{:S(2)}) collective-permute-start(bf16[20,2048]{1,0:T(8,128)(2,1)S(1)} %concatenate.35), channel_id=1, source_target_pairs={{32,0},{0,32},{33,1},{1,33},{34,2},{2,34},{35,3},{3,35},{36,4},{4,... | collective-permute-start | bytes 245768 | tf_op jit(solution)/shard_map/ppermute | solution.py:29
  13.9 1.0 fusion.10
  15.2 4.4 %collective-permute-done.18 = bf16[64,384]{1,0:T(8,128)(2,1)S(1)} collective-permute-done((bf16[64,384]{1,0:T(8,128)(2,1)S(1)}, bf16[64,384]{1,0:T(8,128)(2,1)S(1)}, u32[]{:S(2)}, u32[]{:S(2)}) %collective-permute-start.18) | collective-permute-done | bytes 49184 | tf_op jit(solution)/shard_map/ppermute | solution.py:29
  19.9 0.7 copy-done.12
  20.6 1.3 collective-permute-start.1
  21.9 4.0 %collective-permute-start = (bf16[4,1,16,320]{3,2,1,0:T(8,128)(2,1)S(1)}, bf16[4,1,16,320]{3,2,1,0:T(8,128)(2,1)S(1)}, u32[]{:S(2)}, u32[]{:S(2)}) collective-permute-start(bf16[4,1,16,320]{3,2,1,0:T(8,128)(2,1)S(1)} %copy-done.22), channel_id=1, source_target_pairs={{0,1},{1,2},{2,3},{3,4},{4,5},{5,6},{6,7},{7,8},{8,9},{9,10},{10,1... | collective-permute-start | bytes 122888 | tf_op jit(solution)/shard_map/ppermute | solution.py:326
  26.1 9.1 %collective-permute-start.9 = (bf16[20,2880]{1,0:T(8,128)(2,1)S(1)}, bf16[20,2880]{1,0:T(8,128)(2,1)S(1)}, u32[]{:S(2)}, u32[]{:S(2)}) collective-permute-start(bf16[20,2880]{1,0:T(8,128)(2,1)S(1)} %reshape.58), channel_id=1, source_target_pairs={{32,0},{0,32},{33,1},{1,33},{34,2},{2,34},{35,3},{3,35},{36,4},{4,... | collective-permute-start | bytes 345608 | tf_op jit(solution)/shard_map/ppermute | solution.py:29
  35.4 2.8 %collective-permute-start.2 = (bf16[3,64,320]{2,1,0:T(8,128)(2,1)S(1)}, bf16[3,64,320]{2,1,0:T(8,128)(2,1)S(1)}, u32[]{:S(2)}, u32[]{:S(2)}) collective-permute-start(bf16[3,64,320]{2,1,0:T(8,128)(2,1)S(1)} %bitcast.41), channel_id=1, source_target_pairs={{4,0},{8,4},{12,8},{16,12},{20,16},{24,20},{28,24},{0,28},{5,1},{9... | collective-permute-start | bytes 368648 | tf_op jit(solution)/shard_map/ppermute | solution.py:29
  38.2 0.9 broadcast_select_fusion.1
  39.2 0.8 pad_maximum_fusion.1
  39.9 4.1 %collective-permute-start.11 = (bf16[40,2880]{1,0:T(8,128)(2,1)}, bf16[40,2880]{1,0:T(8,128)(2,1)}, u32[]{:S(2)}, u32[]{:S(2)}) collective-permute-start(bf16[40,2880]{1,0:T(8,128)(2,1)} %pad_maximum_fusion.1), channel_id=1, source_target_pairs={{2,0},{3,1},{0,2},{1,3},{6,4},{7,5},{4,6},{5,7},{10,8},{11,9},{8,1... | collective-permute-start | bytes 691208 | tf_op jit(solution)/shard_map/ppermute | solution.py:29
  44.1 4.4 %collective-permute-start.4 = (bf16[3,64,320]{2,1,0:T(8,128)(2,1)S(1)}, bf16[3,64,320]{2,1,0:T(8,128)(2,1)S(1)}, u32[]{:S(2)}, u32[]{:S(2)}) collective-permute-start(bf16[3,64,320]{2,1,0:T(8,128)(2,1)S(1)} %collective-permute-done.2.refs_1_), channel_id=1, source_target_pairs={{4,0},{8,4},{12,8},{16,12},{20,16},{24,20},{28,24},{0,28},{5,1},{9... | collective-permute-start | bytes 368648 | tf_op jit(solution)/shard_map/ppermute | solution.py:29
  48.6 3.7 %collective-permute-done.5.refs_4_ = bf16[3,64,320]{2,1,0:T(8,128)(2,1)S(1)} collective-permute-done((bf16[3,64,320]{2,1,0:T(8,128)(2,1)S(1)}, bf16[3,64,320]{2,1,0:T(8,128)(2,1)S(1)}, u32[]{:S(2)}, u32[]{:S(2)}) %collective-permute-start.5) | collective-permute-done | bytes 122912 | tf_op jit(solution)/shard_map/ppermute | solution.py:29
  52.3 2.7 %collective-permute-start.6 = (bf16[3,64,320]{2,1,0:T(8,128)(2,1)S(1)}, bf16[3,64,320]{2,1,0:T(8,128)(2,1)S(1)}, u32[]{:S(2)}, u32[]{:S(2)}) collective-permute-start(bf16[3,64,320]{2,1,0:T(8,128)(2,1)S(1)} %collective-permute-done.4.refs_3_), channel_id=1, source_target_pairs={{4,0},{8,4},{12,8},{16,12},{20,16},{24,20},{28,24},{0,28},{5,1},{9... | collective-permute-start | bytes 368648 | tf_op jit(solution)/shard_map/ppermute | solution.py:29
  55.0 1.6 %select_select_fusion.3 = (bf16[40,2880]{1,0:T(8,128)(2,1)S(1)}, bf16[40,2880]{1,0:T(8,128)(2,1)S(1)}, bf16[40,2880]{1,0:T(8,128)(2,1)S(1)}, bf16[40,2880]{1,0:T(8,128)(2,1)S(1)}) fusion(bf16[40,2880]{1,0:T(8,128)(2,1)} %collective-permute-done.10, bf16[40,2880]{1,0:T(8,128)(2,1)} %collective-permute-done.11, bf16[40,2880]{1,0:T(8,128)(2,1)} %collective-permute-done.12, ...), kind=kLoop, calls=%fused_computation.22 | loop fusion | flops 1843200 | bytes 1843203 | tf_op jit(solution)/shard_map/jit(_where)/select_n | solution.py:54
  56.6 2.6 %collective-permute-done.6.refs_5_ = bf16[3,64,320]{2,1,0:T(8,128)(2,1)S(1)} collective-permute-done((bf16[3,64,320]{2,1,0:T(8,128)(2,1)S(1)}, bf16[3,64,320]{2,1,0:T(8,128)(2,1)S(1)}, u32[]{:S(2)}, u32[]{:S(2)}) %collective-permute-start.6) | collective-permute-done | bytes 122912 | tf_op jit(solution)/shard_map/ppermute | solution.py:29
  59.2 3.0 %collective-permute-start.8 = (bf16[3,64,320]{2,1,0:T(8,128)(2,1)S(1)}, bf16[3,64,320]{2,1,0:T(8,128)(2,1)S(1)}, u32[]{:S(2)}, u32[]{:S(2)}) collective-permute-start(bf16[3,64,320]{2,1,0:T(8,128)(2,1)S(1)} %collective-permute-done.6.refs_5_), channel_id=1, source_target_pairs={{4,0},{8,4},{12,8},{16,12},{20,16},{24,20},{28,24},{0,28},{5,1},{9... | collective-permute-start | bytes 368648 | tf_op jit(solution)/shard_map/ppermute | solution.py:29
  62.4 3.9 %collective-permute-done.8.refs_7_ = bf16[3,64,320]{2,1,0:T(8,128)(2,1)S(1)} collective-permute-done((bf16[3,64,320]{2,1,0:T(8,128)(2,1)S(1)}, bf16[3,64,320]{2,1,0:T(8,128)(2,1)S(1)}, u32[]{:S(2)}, u32[]{:S(2)}) %collective-permute-start.8) | collective-permute-done | bytes 122912 | tf_op jit(solution)/shard_map/ppermute | solution.py:29
  66.3 0.9 copy-done.4
  67.2 0.9 copy-done.6
  68.1 0.9 copy-done.8
  69.0 2.4 %shard_map.131 = (f32[2,128,160]{2,1,0:T(8,128)S(1)}, f32[2,128,160]{2,1,0:T(8,128)S(1)}) custom-call(s32[5]{0:T(128)S(1)} %stack.23.where_ref, bf16[3,64,320]{2,1,0:T(8,128)(2,1)S(1)} %bitcast.42, bf16[3,64,320]{2,1,0:T(8,128)(2,1)S(1)} %copy-done.4, bf16[3,64,320]{2,1,0:T(8,128)(2,1)S(1)} %collective-permute-done.3.refs_2_, ...), custom_call_target="tpu_custom_call" | custom-call | flops 3000000000 | bytes 1904660 | tf_op jit(solution)/shard_map/pallas_call | solution.py:271
  71.4 7.0 %collective-permute-start.13 = (f32[2,128,160]{2,1,0:T(8,128)S(1)}, f32[2,128,160]{2,1,0:T(8,128)}, u32[]{:S(2)}, u32[]{:S(2)}) collective-permute-start(f32[2,128,160]{2,1,0:T(8,128)S(1)} %get-tuple-element.14), channel_id=1, source_target_pairs={{0,64},{64,0},{1,65},{65,1},{2,66},{66,2},{3,67},{67,3},{4,68},{68... | collective-permute-start | bytes 491528 | tf_op jit(solution)/shard_map/ppermute | solution.py:289
  79.7 1.0 fusion.1
  81.2 4.5 %collective-permute-done.14.got_ref = f32[128,160]{1,0:T(8,128)S(1)} collective-permute-done((f32[128,160]{1,0:T(8,128)S(1)}, f32[128,160]{1,0:T(8,128)S(1)}, u32[]{:S(2)}, u32[]{:S(2)}) %collective-permute-start.14) | collective-permute-done | bytes 81952 | tf_op jit(solution)/shard_map/ppermute | solution.py:289
  86.5 9.6 %all-to-all-start = ((f32[8,8,128]{2,1,0:T(8,128)}), f32[8,8,128]{2,1,0:T(8,128)S(1)}, u32[]{:S(2)}, u32[]{:S(2)}) async-start(f32[8,8,128]{2,1,0:T(8,128)} %broadcast_in_dim.3), calls=%async_computation | async-start | bytes 65536 | tf_op jit(solution)/shard_map/all_to_all | solution.py:366
  96.3 6.6 %all-to-all-done.stats_ref = f32[8,8,128]{2,1,0:T(8,128)S(1)} async-done(((f32[8,8,128]{2,1,0:T(8,128)}), f32[8,8,128]{2,1,0:T(8,128)S(1)}, u32[]{:S(2)}, u32[]{:S(2)}) %all-to-all-start) | async-done | bytes 32800 | tf_op jit(solution)/shard_map/all_to_all | solution.py:366
  103.1 12.4 %all_to_all.10.refs_0_ = bf16[8,16,160]{2,1,0:T(8,128)(2,1)S(1)} all-to-all(bf16[8,16,160]{2,1,0:T(8,128)(2,1)S(1)} %shard_map.133), channel_id=1, replica_groups=mesh['yl'=2,'c'=2,'yh'=2,'z'=8,'x'=4] {'z'}, dimensions={0} | all-to-all | bytes 81920 | tf_op jit(solution)/shard_map/all_to_all | solution.py:375
  115.5 4.0 %collective-permute-start.15 = (bf16[8,16,160]{2,1,0:T(8,128)(2,1)S(1)}, bf16[8,16,160]{2,1,0:T(8,128)(2,1)S(1)}, u32[]{:S(2)}, u32[]{:S(2)}) collective-permute-start(bf16[8,16,160]{2,1,0:T(8,128)(2,1)S(1)} %all_to_all.10.refs_0_), channel_id=1, source_target_pairs={{0,64},{64,0},{1,65},{65,1},{2,66},{66,2},{3,67},{67,3},{4,68},{68... | collective-permute-start | bytes 122888 | tf_op jit(solution)/shard_map/ppermute | solution.py:289
  121.0 2.2 %collective-permute-done.16.refs_2_ = bf16[8,16,160]{2,1,0:T(8,128)(2,1)S(1)} collective-permute-done((bf16[8,16,160]{2,1,0:T(8,128)(2,1)S(1)}, bf16[8,16,160]{2,1,0:T(8,128)(2,1)S(1)}, u32[]{:S(2)}, u32[]{:S(2)}) %collective-permute-start.16) | collective-permute-done | bytes 40992 | tf_op jit(solution)/shard_map/ppermute | solution.py:289
  123.2 1.4 collective-permute-done.17.refs_3_
  125.2 6.3 %shard_map.134 = (bf16[4,16,1280]{2,1,0:T(8,128)(2,1)}, bf16[4,16,384]{2,1,0:T(8,128)(2,1)}, bf16[4,16,1280]{2,1,0:T(8,128)(2,1)}) custom-call(s32[5]{0:T(128)} %copy-done.2, bf16[8,16,160]{2,1,0:T(8,128)(2,1)} %copy-done.13, bf16[8,16,160]{2,1,0:T(8,128)(2,1)} %copy-done.15, bf16[8,16,160]{2,1,0:T(8,128)(2,1)} %copy-done.16, ...), custom_call_target="tpu_custom_call" | custom-call | flops 1000000000 | bytes 8552468 | tf_op jit(solution)/shard_map/pallas_call | solution.py:271
  131.5 0.9 collective-permute-start.20
  132.4 1.2 collective-permute-done.20
  133.6 1.0 add_convert_fusion.2.mine_ref
  134.6 0.7 collective-permute-start.21
  135.3 2.1 %slice.87.packed_ref = bf16[32,200,256]{2,1,0:T(8,128)(2,1)S(1)} slice(bf16[32,512,256]{2,1,0:T(8,128)(2,1)} %bitcast.44), slice={[0:32], [312:512], [0:256]} | slice | bytes 6553600 | tf_op jit(solution)/shard_map/slice | solution.py:396
  137.4 2.7 %collective-permute-done.21.got_ref = bf16[4,16,1280]{2,1,0:T(8,128)(2,1)S(1)} collective-permute-done((bf16[4,16,1280]{2,1,0:T(8,128)(2,1)S(1)}, bf16[4,16,1280]{2,1,0:T(8,128)(2,1)S(1)}, u32[]{:S(2)}, u32[]{:S(2)}) %collective-permute-start.21) | collective-permute-done | bytes 163872 | tf_op jit(solution)/shard_map/ppermute | solution.py:289
  140.1 2.4 %shard_map.135 = (bf16[4,16,1280]{2,1,0:T(8,128)(2,1)S(1)}, bf16[4,16,1280]{2,1,0:T(8,128)(2,1)S(1)}) custom-call(bf16[4,16,1280]{2,1,0:T(8,128)(2,1)S(1)} %copy-done.1, bf16[4,16,1280]{2,1,0:T(8,128)(2,1)S(1)} %add_convert_fusion.2.mine_ref, bf16[4,16,1280]{2,1,0:T(8,128)(2,1)S(1)} %collective-permute-done.21.got_ref, ...), custom_call_target="tpu_custom_call" | custom-call | flops 1000000000 | bytes 3768320 | tf_op jit(solution)/shard_map/pallas_call | solution.py:271
  142.5 1.3 collective-permute-start.22
  143.8 1.0 collective-permute-done.22
  144.8 0.7 collective-permute-start.23
  145.6 0.7 reshape.67
  146.3 4.1 %collective-permute-done.23 = bf16[4,16,1280]{2,1,0:T(8,128)(2,1)S(1)} collective-permute-done((bf16[4,16,1280]{2,1,0:T(8,128)(2,1)S(1)}, bf16[4,16,1280]{2,1,0:T(8,128)(2,1)S(1)}, u32[]{:S(2)}, u32[]{:S(2)}) %collective-permute-start.23) | collective-permute-done | bytes 163872 | tf_op jit(solution)/shard_map/ppermute | solution.py:289
  150.3 0.7 fusion
  (111 shorter events, 5.7 us)
Async XLA Ops:
  7.2 71.9 %copy-start = (bf16[1000,1280]{1,0:T(8,128)(2,1)S(1)}, bf16[1000,1280]{1,0:T(8,128)(2,1)}, u32[]{:S(2)}) copy-start(bf16[1000,1280]{1,0:T(8,128)(2,1)} %param.15) | copy-start | bytes 7680004
  7.2 117.4 %all-gather.3.cloned.1.call-start = ((), (), s32[]{:S(2)}) async-start(), calls=%async_computation.2 | async-start | bytes 8650752 | tf_op jit(solution)/shard_map/all_gather | solution.py:350
  8.3 12.3 %copy-start.22 = (bf16[4,1,16,320]{3,2,1,0:T(8,128)(2,1)S(1)}, bf16[4,1,16,320]{3,2,1,0:T(8,128)(2,1)}, u32[]{:S(2)}) copy-start(bf16[4,1,16,320]{3,2,1,0:T(8,128)(2,1)} %param.13) | copy-start | bytes 122884
  8.3 17.6 %copy-start.14 = (bf16[9,320,20]{1,2,0:T(8,128)(2,1)S(1)}, bf16[9,320,20]{1,2,0:T(8,128)(2,1)}, u32[]{:S(2)}) copy-start(bf16[9,320,20]{1,2,0:T(8,128)(2,1)} %param.14) | copy-start | bytes 345604
  10.1 9.6 %collective-permute-start.19 = (bf16[20,2048]{1,0:T(8,128)(2,1)S(1)}, bf16[20,2048]{1,0:T(8,128)(2,1)S(1)}, u32[]{:S(2)}, u32[]{:S(2)}) collective-permute-start(bf16[20,2048]{1,0:T(8,128)(2,1)S(1)} %concatenate.35), channel_id=1, source_target_pairs={{32,0},{0,32},{33,1},{1,33},{34,2},{2,34},{35,3},{3,35},{36,4},{4,... | collective-permute-start | bytes 245768 | tf_op jit(solution)/shard_map/ppermute | solution.py:29
  15.0 20.2 %copy-start.18 = (bf16[4,1,16,320]{3,2,1,0:T(8,128)(2,1)S(1)}, bf16[4,1,16,320]{3,2,1,0:T(8,128)(2,1)}, u32[]{:S(2)}) copy-start(bf16[4,1,16,320]{3,2,1,0:T(8,128)(2,1)} %param.12) | copy-start | bytes 122884
  15.1 4.5 %collective-permute-start.18 = (bf16[64,384]{1,0:T(8,128)(2,1)S(1)}, bf16[64,384]{1,0:T(8,128)(2,1)S(1)}, u32[]{:S(2)}, u32[]{:S(2)}) collective-permute-start(bf16[64,384]{1,0:T(8,128)(2,1)S(1)} %pad_maximum_fusion.2), channel_id=1, source_target_pairs={{32,0},{0,32},{33,1},{1,33},{34,2},{2,34},{35,3},{3,35},{36,4},{4,... | collective-permute-start | bytes 147464 | tf_op jit(solution)/shard_map/ppermute | solution.py:29
  19.9 0.7 copy-start.12
  20.6 14.6 %collective-permute-start.1 = (bf16[4,1,16,320]{3,2,1,0:T(8,128)(2,1)S(1)}, bf16[4,1,16,320]{3,2,1,0:T(8,128)(2,1)S(1)}, u32[]{:S(2)}, u32[]{:S(2)}) collective-permute-start(bf16[4,1,16,320]{3,2,1,0:T(8,128)(2,1)S(1)} %copy-done.22), channel_id=1, source_target_pairs={{1,0},{2,1},{3,2},{4,3},{5,4},{6,5},{7,6},{8,7},{9,8},{10,9},{11,1... | collective-permute-start | bytes 122888 | tf_op jit(solution)/shard_map/ppermute | solution.py:327
  21.9 13.3 %collective-permute-start = (bf16[4,1,16,320]{3,2,1,0:T(8,128)(2,1)S(1)}, bf16[4,1,16,320]{3,2,1,0:T(8,128)(2,1)S(1)}, u32[]{:S(2)}, u32[]{:S(2)}) collective-permute-start(bf16[4,1,16,320]{3,2,1,0:T(8,128)(2,1)S(1)} %copy-done.22), channel_id=1, source_target_pairs={{0,1},{1,2},{2,3},{3,4},{4,5},{5,6},{6,7},{7,8},{8,9},{9,10},{10,1... | collective-permute-start | bytes 122888 | tf_op jit(solution)/shard_map/ppermute | solution.py:326
  26.1 12.1 %copy-start.11 = (bf16[20,2880]{1,0:T(8,128)(2,1)}, bf16[20,2880]{1,0:T(8,128)(2,1)S(1)}, u32[]{:S(2)}) copy-start(bf16[20,2880]{1,0:T(8,128)(2,1)S(1)} %reshape.58) | copy-start | bytes 345604
  26.1 12.1 %collective-permute-start.9 = (bf16[20,2880]{1,0:T(8,128)(2,1)S(1)}, bf16[20,2880]{1,0:T(8,128)(2,1)S(1)}, u32[]{:S(2)}, u32[]{:S(2)}) collective-permute-start(bf16[20,2880]{1,0:T(8,128)(2,1)S(1)} %reshape.58), channel_id=1, source_target_pairs={{32,0},{0,32},{33,1},{1,33},{34,2},{2,34},{35,3},{3,35},{36,4},{4,... | collective-permute-start | bytes 345608 | tf_op jit(solution)/shard_map/ppermute | solution.py:29
  35.3 8.7 %collective-permute-start.3 = (bf16[3,64,320]{2,1,0:T(8,128)(2,1)S(1)}, bf16[3,64,320]{2,1,0:T(8,128)(2,1)S(1)}, u32[]{:S(2)}, u32[]{:S(2)}) collective-permute-start(bf16[3,64,320]{2,1,0:T(8,128)(2,1)S(1)} %bitcast.40), channel_id=1, source_target_pairs={{28,0},{0,4},{4,8},{8,12},{12,16},{16,20},{20,24},{24,28},{29,1},{... | collective-permute-start | bytes 368648 | tf_op jit(solution)/shard_map/ppermute | solution.py:29
  35.4 8.7 %collective-permute-start.2 = (bf16[3,64,320]{2,1,0:T(8,128)(2,1)S(1)}, bf16[3,64,320]{2,1,0:T(8,128)(2,1)S(1)}, u32[]{:S(2)}, u32[]{:S(2)}) collective-permute-start(bf16[3,64,320]{2,1,0:T(8,128)(2,1)S(1)} %bitcast.41), channel_id=1, source_target_pairs={{4,0},{8,4},{12,8},{16,12},{20,16},{24,20},{28,24},{0,28},{5,1},{9... | collective-permute-start | bytes 368648 | tf_op jit(solution)/shard_map/ppermute | solution.py:29
  39.2 4.9 %copy-start.9 = (bf16[20,2880]{1,0:T(8,128)(2,1)}, bf16[20,2880]{1,0:T(8,128)(2,1)S(1)}, u32[]{:S(2)}) copy-start(bf16[20,2880]{1,0:T(8,128)(2,1)S(1)} %get-tuple-element.36) | copy-start | bytes 345604
  39.2 4.8 %copy-start.10 = (bf16[20,2880]{1,0:T(8,128)(2,1)}, bf16[20,2880]{1,0:T(8,128)(2,1)S(1)}, u32[]{:S(2)}) copy-start(bf16[20,2880]{1,0:T(8,128)(2,1)S(1)} %get-tuple-element.37) | copy-start | bytes 345604
  39.9 15.1 %collective-permute-start.12 = (bf16[40,2880]{1,0:T(8,128)(2,1)}, bf16[40,2880]{1,0:T(8,128)(2,1)}, u32[]{:S(2)}, u32[]{:S(2)}) collective-permute-start(bf16[40,2880]{1,0:T(8,128)(2,1)} %pad_maximum_fusion.1), channel_id=1, source_target_pairs={{3,0},{0,1},{1,2},{2,3},{7,4},{4,5},{5,6},{6,7},{11,8},{8,9},{9,10... | collective-permute-start | bytes 691208 | tf_op jit(solution)/shard_map/ppermute | solution.py:29
  39.9 15.1 %collective-permute-start.11 = (bf16[40,2880]{1,0:T(8,128)(2,1)}, bf16[40,2880]{1,0:T(8,128)(2,1)}, u32[]{:S(2)}, u32[]{:S(2)}) collective-permute-start(bf16[40,2880]{1,0:T(8,128)(2,1)} %pad_maximum_fusion.1), channel_id=1, source_target_pairs={{2,0},{3,1},{0,2},{1,3},{6,4},{7,5},{4,6},{5,7},{10,8},{11,9},{8,1... | collective-permute-start | bytes 691208 | tf_op jit(solution)/shard_map/ppermute | solution.py:29
  44.0 11.0 %collective-permute-start.10 = (bf16[40,2880]{1,0:T(8,128)(2,1)}, bf16[40,2880]{1,0:T(8,128)(2,1)}, u32[]{:S(2)}, u32[]{:S(2)}) collective-permute-start(bf16[40,2880]{1,0:T(8,128)(2,1)} %pad_maximum_fusion.1), channel_id=1, source_target_pairs={{1,0},{2,1},{3,2},{0,3},{5,4},{6,5},{7,6},{4,7},{9,8},{10,9},{11,1... | collective-permute-start | bytes 691208 | tf_op jit(solution)/shard_map/ppermute | solution.py:29
  44.0 8.3 %collective-permute-start.5 = (bf16[3,64,320]{2,1,0:T(8,128)(2,1)S(1)}, bf16[3,64,320]{2,1,0:T(8,128)(2,1)S(1)}, u32[]{:S(2)}, u32[]{:S(2)}) collective-permute-start(bf16[3,64,320]{2,1,0:T(8,128)(2,1)S(1)} %collective-permute-done.3.refs_2_), channel_id=1, source_target_pairs={{28,0},{0,4},{4,8},{8,12},{12,16},{16,20},{20,24},{24,28},{29,1},{... | collective-permute-start | bytes 368648 | tf_op jit(solution)/shard_map/ppermute | solution.py:29
  44.1 18.2 %copy-start.3 = (bf16[3,64,320]{2,1,0:T(8,128)(2,1)}, bf16[3,64,320]{2,1,0:T(8,128)(2,1)S(1)}, u32[]{:S(2)}) copy-start(bf16[3,64,320]{2,1,0:T(8,128)(2,1)S(1)} %collective-permute-done.2.refs_1_) | copy-start | bytes 368644
  44.1 8.2 %collective-permute-start.4 = (bf16[3,64,320]{2,1,0:T(8,128)(2,1)S(1)}, bf16[3,64,320]{2,1,0:T(8,128)(2,1)S(1)}, u32[]{:S(2)}, u32[]{:S(2)}) collective-permute-start(bf16[3,64,320]{2,1,0:T(8,128)(2,1)S(1)} %collective-permute-done.2.refs_1_), channel_id=1, source_target_pairs={{4,0},{8,4},{12,8},{16,12},{20,16},{24,20},{28,24},{0,28},{5,1},{9... | collective-permute-start | bytes 368648 | tf_op jit(solution)/shard_map/ppermute | solution.py:29
  48.6 17.6 %copy-start.2 = (s32[5]{0:T(128)}, s32[5]{0:T(128)S(1)}, u32[]{:S(2)}) copy-start(s32[5]{0:T(128)S(1)} %stack.23.where_ref) | copy-start | bytes 64
  52.3 10.1 %copy-start.5 = (bf16[3,64,320]{2,1,0:T(8,128)(2,1)}, bf16[3,64,320]{2,1,0:T(8,128)(2,1)S(1)}, u32[]{:S(2)}) copy-start(bf16[3,64,320]{2,1,0:T(8,128)(2,1)S(1)} %collective-permute-done.5.refs_4_) | copy-start | bytes 368644
  52.3 10.1 %collective-permute-start.7 = (bf16[3,64,320]{2,1,0:T(8,128)(2,1)S(1)}, bf16[3,64,320]{2,1,0:T(8,128)(2,1)S(1)}, u32[]{:S(2)}, u32[]{:S(2)}) collective-permute-start(bf16[3,64,320]{2,1,0:T(8,128)(2,1)S(1)} %collective-permute-done.5.refs_4_), channel_id=1, source_target_pairs={{28,0},{0,4},{4,8},{8,12},{12,16},{16,20},{20,24},{24,28},{29,1},{... | collective-permute-start | bytes 368648 | tf_op jit(solution)/shard_map/ppermute | solution.py:29
  52.3 10.1 %copy-start.7 = (bf16[3,64,320]{2,1,0:T(8,128)(2,1)}, bf16[3,64,320]{2,1,0:T(8,128)(2,1)S(1)}, u32[]{:S(2)}) copy-start(bf16[3,64,320]{2,1,0:T(8,128)(2,1)S(1)} %collective-permute-done.4.refs_3_) | copy-start | bytes 368644
  52.3 6.9 %collective-permute-start.6 = (bf16[3,64,320]{2,1,0:T(8,128)(2,1)S(1)}, bf16[3,64,320]{2,1,0:T(8,128)(2,1)S(1)}, u32[]{:S(2)}, u32[]{:S(2)}) collective-permute-start(bf16[3,64,320]{2,1,0:T(8,128)(2,1)S(1)} %collective-permute-done.4.refs_3_), channel_id=1, source_target_pairs={{4,0},{8,4},{12,8},{16,12},{20,16},{24,20},{28,24},{0,28},{5,1},{9... | collective-permute-start | bytes 368648 | tf_op jit(solution)/shard_map/ppermute | solution.py:29
  59.2 7.0 %collective-permute-start.8 = (bf16[3,64,320]{2,1,0:T(8,128)(2,1)S(1)}, bf16[3,64,320]{2,1,0:T(8,128)(2,1)S(1)}, u32[]{:S(2)}, u32[]{:S(2)}) collective-permute-start(bf16[3,64,320]{2,1,0:T(8,128)(2,1)S(1)} %collective-permute-done.6.refs_5_), channel_id=1, source_target_pairs={{4,0},{8,4},{12,8},{16,12},{20,16},{24,20},{28,24},{0,28},{5,1},{9... | collective-permute-start | bytes 368648 | tf_op jit(solution)/shard_map/ppermute | solution.py:29
  62.3 18.6 %copy-start.20 = (f32[1280]{0:T(1024)S(1)}, f32[1280]{0:T(1024)}, u32[]{:S(2)}) copy-start(f32[1280]{0:T(1024)} %param.17) | copy-start | bytes 15364
  62.3 18.8 %copy-start.21 = (f32[1280]{0:T(1024)S(1)}, f32[1280]{0:T(1024)}, u32[]{:S(2)}) copy-start(f32[1280]{0:T(1024)} %param.18) | copy-start | bytes 15364
  66.3 0.9 copy-start.4
  67.2 0.9 copy-start.6
  68.1 0.9 copy-start.8
  71.4 8.3 %collective-permute-start.13 = (f32[2,128,160]{2,1,0:T(8,128)S(1)}, f32[2,128,160]{2,1,0:T(8,128)}, u32[]{:S(2)}, u32[]{:S(2)}) collective-permute-start(f32[2,128,160]{2,1,0:T(8,128)S(1)} %get-tuple-element.14), channel_id=1, source_target_pairs={{0,64},{64,0},{1,65},{65,1},{2,66},{66,2},{3,67},{67,3},{4,68},{68... | collective-permute-start | bytes 491528 | tf_op jit(solution)/shard_map/ppermute | solution.py:289
  80.7 4.9 %collective-permute-start.14 = (f32[128,160]{1,0:T(8,128)S(1)}, f32[128,160]{1,0:T(8,128)S(1)}, u32[]{:S(2)}, u32[]{:S(2)}) collective-permute-start(f32[128,160]{1,0:T(8,128)S(1)} %get-tuple-element.34), channel_id=1, source_target_pairs={{0,128},{128,0},{1,129},{129,1},{2,130},{130,2},{3,131},{131,3},{4... | collective-permute-start | bytes 245768 | tf_op jit(solution)/shard_map/ppermute | solution.py:289
  86.5 16.4 %all-to-all-start = ((f32[8,8,128]{2,1,0:T(8,128)}), f32[8,8,128]{2,1,0:T(8,128)S(1)}, u32[]{:S(2)}, u32[]{:S(2)}) async-start(f32[8,8,128]{2,1,0:T(8,128)} %broadcast_in_dim.3), calls=%async_computation | async-start | bytes 65536 | tf_op jit(solution)/shard_map/all_to_all | solution.py:366
  115.5 9.1 %copy-start.13 = (bf16[8,16,160]{2,1,0:T(8,128)(2,1)}, bf16[8,16,160]{2,1,0:T(8,128)(2,1)S(1)}, u32[]{:S(2)}) copy-start(bf16[8,16,160]{2,1,0:T(8,128)(2,1)S(1)} %all_to_all.10.refs_0_) | copy-start | bytes 122884
  115.5 4.9 %collective-permute-start.15 = (bf16[8,16,160]{2,1,0:T(8,128)(2,1)S(1)}, bf16[8,16,160]{2,1,0:T(8,128)(2,1)S(1)}, u32[]{:S(2)}, u32[]{:S(2)}) collective-permute-start(bf16[8,16,160]{2,1,0:T(8,128)(2,1)S(1)} %all_to_all.10.refs_0_), channel_id=1, source_target_pairs={{0,64},{64,0},{1,65},{65,1},{2,66},{66,2},{3,67},{67,3},{4,68},{68... | collective-permute-start | bytes 122888 | tf_op jit(solution)/shard_map/ppermute | solution.py:289
  119.4 3.7 %collective-permute-start.16 = (bf16[8,16,160]{2,1,0:T(8,128)(2,1)S(1)}, bf16[8,16,160]{2,1,0:T(8,128)(2,1)S(1)}, u32[]{:S(2)}, u32[]{:S(2)}) collective-permute-start(bf16[8,16,160]{2,1,0:T(8,128)(2,1)S(1)} %all_to_all.10.refs_0_), channel_id=1, source_target_pairs={{0,128},{128,0},{1,129},{129,1},{2,130},{130,2},{3,131},{131,3},{4... | collective-permute-start | bytes 122888 | tf_op jit(solution)/shard_map/ppermute | solution.py:289
  120.3 4.2 %copy-start.15 = (bf16[8,16,160]{2,1,0:T(8,128)(2,1)}, bf16[8,16,160]{2,1,0:T(8,128)(2,1)S(1)}, u32[]{:S(2)}) copy-start(bf16[8,16,160]{2,1,0:T(8,128)(2,1)S(1)} %collective-permute-done.15.refs_1_) | copy-start | bytes 122884
  120.3 4.2 %collective-permute-start.17 = (bf16[8,16,160]{2,1,0:T(8,128)(2,1)S(1)}, bf16[8,16,160]{2,1,0:T(8,128)(2,1)S(1)}, u32[]{:S(2)}, u32[]{:S(2)}) collective-permute-start(bf16[8,16,160]{2,1,0:T(8,128)(2,1)S(1)} %collective-permute-done.15.refs_1_), channel_id=1, source_target_pairs={{0,128},{128,0},{1,129},{129,1},{2,130},{130,2},{3,131},{131,3},{4... | collective-permute-start | bytes 122888 | tf_op jit(solution)/shard_map/ppermute | solution.py:289
  123.2 1.4 copy-start.16
  131.5 2.1 %collective-permute-start.20 = (bf16[4,16,1280]{2,1,0:T(8,128)(2,1)}, bf16[4,16,1280]{2,1,0:T(8,128)(2,1)S(1)}, u32[]{:S(2)}, u32[]{:S(2)}) collective-permute-start(bf16[4,16,1280]{2,1,0:T(8,128)(2,1)} %get-tuple-element.19), channel_id=1, source_target_pairs={{0,64},{64,0},{1,65},{65,1},{2,66},{66,2},{3,67},{67,3},{4,68},{68... | collective-permute-start | bytes 491528 | tf_op jit(solution)/shard_map/ppermute | solution.py:289
  134.6 5.5 %copy-start.1 = (bf16[4,16,1280]{2,1,0:T(8,128)(2,1)S(1)}, bf16[4,16,1280]{2,1,0:T(8,128)(2,1)}, u32[]{:S(2)}) copy-start(bf16[4,16,1280]{2,1,0:T(8,128)(2,1)} %get-tuple-element.17.own_ref) | copy-start | bytes 491524
  134.6 5.5 %collective-permute-start.21 = (bf16[4,16,1280]{2,1,0:T(8,128)(2,1)S(1)}, bf16[4,16,1280]{2,1,0:T(8,128)(2,1)S(1)}, u32[]{:S(2)}, u32[]{:S(2)}) collective-permute-start(bf16[4,16,1280]{2,1,0:T(8,128)(2,1)S(1)} %add_convert_fusion.2.mine_ref), channel_id=1, source_target_pairs={{0,128},{128,0},{1,129},{129,1},{2,130},{130,2},{3,131},{131,3},{4... | collective-permute-start | bytes 491528 | tf_op jit(solution)/shard_map/ppermute | solution.py:289
  140.1 5.5 %copy-start.19 = (bf16[4,16,384]{2,1,0:T(8,128)(2,1)S(1)}, bf16[4,16,384]{2,1,0:T(8,128)(2,1)}, u32[]{:S(2)}) copy-start(bf16[4,16,384]{2,1,0:T(8,128)(2,1)} %get-tuple-element.23) | copy-start | bytes 147460
  142.5 2.3 %collective-permute-start.22 = (bf16[4,16,1280]{2,1,0:T(8,128)(2,1)S(1)}, bf16[4,16,1280]{2,1,0:T(8,128)(2,1)S(1)}, u32[]{:S(2)}, u32[]{:S(2)}) collective-permute-start(bf16[4,16,1280]{2,1,0:T(8,128)(2,1)S(1)} %get-tuple-element.22), channel_id=1, source_target_pairs={{0,64},{64,0},{1,65},{65,1},{2,66},{66,2},{3,67},{67,3},{4,68},{68... | collective-permute-start | bytes 491528 | tf_op jit(solution)/shard_map/ppermute | solution.py:289
  144.8 5.5 %collective-permute-start.23 = (bf16[4,16,1280]{2,1,0:T(8,128)(2,1)S(1)}, bf16[4,16,1280]{2,1,0:T(8,128)(2,1)S(1)}, u32[]{:S(2)}, u32[]{:S(2)}) collective-permute-start(bf16[4,16,1280]{2,1,0:T(8,128)(2,1)S(1)} %add_convert_fusion.1), channel_id=1, source_target_pairs={{0,128},{128,0},{1,129},{129,1},{2,130},{130,2},{3,131},{131,3},{4... | collective-permute-start | bytes 491528 | tf_op jit(solution)/shard_map/ppermute | solution.py:289
  (1 other events, 0.6 us)
Sparse Core Ops, SparseCore 0:
  20.7 101.9 all-gather.2

commit v3 on v2

--- a/solution.py
+++ b/solution.py
@@ -22,6 +22,7 @@
 SMEM = pl.BlockSpec(memory_space=pltpu.SMEM)
 HBM = pl.BlockSpec(memory_space=pltpu.HBM)
 NT = (((1,), (1,)), ((), ()))
+TN = (((0,), (0,)), ((), ()))
 
 
 def from_shift(value, axis, offset):
@@ -183,9 +184,12 @@
         out_weights.append(rhs[:, 576:])
     projected = projected.astype(BF16)
     out_weights = jnp.concatenate(out_weights, axis=0)
+    diagonal = lax.broadcasted_iota(jnp.int32, (48, 48), 0) == lax.broadcasted_iota(
+        jnp.int32, (48, 48), 1
+    )
     score_scale = HEAD_DIM ** (-0.5)
     head_of = lax.broadcasted_iota(jnp.int32, (COLUMNS, 192), 1) // HEAD_DIM
-    key_row = lax.broadcasted_iota(jnp.int32, (1, 512), 1) // COLUMNS
+    key_row = lax.broadcasted_iota(jnp.int32, (512, 1), 0) // COLUMNS
     attended = []
     kv_copy.wait()
     for rel, frame in enumerate(frames):
@@ -202,25 +206,26 @@
             low.append(kv_scr[:, rows, :].reshape(512, 256))
             rows = pl.ds(128 + start, COLUMNS)
             high.append(kv_scr[:, rows, half * 128 : half * 128 + 128].reshape(512, 128))
-        scores = [lax.dot_general(queries, fresh[:, :192], NT, preferred_element_type=F32)]
+        scores = [lax.dot_general(fresh[:, :192], queries, NT, preferred_element_type=F32)]
         for a, b in zip(low, high):
-            far = lax.dot_general(queries[:, :128], a[:, :128], NT, preferred_element_type=F32)
+            far = lax.dot_general(a[:, :128], queries[:, :128], NT, preferred_element_type=F32)
             scores.append(
                 far
-                + lax.dot_general(queries[:, 128:], b[:, :64], NT, preferred_element_type=F32)
+                + lax.dot_general(b[:, :64], queries[:, 128:], NT, preferred_element_type=F32)
             )
         scores = [s * score_scale for s in scores]
         scores[1] = jnp.where(key_row == place, -jnp.inf, scores[1])
-        top = jnp.max(scores[0], axis=-1, keepdims=True)
+        top = jnp.max(scores[0], axis=0, keepdims=True)
         for s in scores[1:]:
-            top = jnp.maximum(top, jnp.max(s, axis=-1, keepdims=True))
+            top = jnp.maximum(top, jnp.max(s, axis=0, keepdims=True))
         expo = [jnp.exp(s - top) for s in scores]
-        total = sum(jnp.sum(e, axis=-1, keepdims=True) for e in expo)
+        total = sum(jnp.sum(e, axis=0, keepdims=True) for e in expo)
+        total = jnp.sum(jnp.where(diagonal, total, 0.0), axis=1, keepdims=True)
         expo = [e.astype(BF16) for e in expo]
-        numerator = jnp.dot(expo[0], fresh[:, 192:], preferred_element_type=F32)
+        numerator = lax.dot_general(expo[0], fresh[:, 192:], TN, preferred_element_type=F32)
         for e, a, b in zip(expo[1:], low, high):
             values = jnp.concatenate([a[:, 128:], b[:, 64:]], axis=1)
-            numerator = numerator + jnp.dot(e, values, preferred_element_type=F32)
+            numerator = numerator + lax.dot_general(e, values, TN, preferred_element_type=F32)
         result = numerator / total
         rows = jnp.zeros((COLUMNS, 192), F32)
         for h in range(3):

time: 159 us -> 159 us (level)
  no operation moved by 1% of the time
where the time goes in v3:
time: 159 us; the launch traced here: 158 us
  starting transfers between devices  60.9 us (38%)
  waiting for transfers between devices  38.9 us (24%)
  between operations  15.2 us (10%)
  local copies, waits for them, and re-layouts  12.4 us (8%)
  blocking collectives  12.4 us (8%)
  Pallas kernels  12.1 us (8%)
  other arithmetic  6.48 us (4%)
    ppermute x13, starting transfers between devices, from_shift(): lax.ppermute(value, axis, [((i + offset) % size, i) for i in range(size)])  30.2 us
    ppermute x9, waiting for transfers between devices, swap(): return lax.ppermute(value, axis, [(0, 1), (1, 0)])  17.8 us
    ppermute x9, starting transfers between devices, swap(): return lax.ppermute(value, axis, [(0, 1), (1, 0)])  15.8 us
    ppermute x13, waiting for transfers between devices, from_shift(): lax.ppermute(value, axis, [((i + offset) % size, i) for i in range(size)])  14.5 us
    all_to_all x1, blocking collectives, shards(): activated = lax.all_to_all(activated, 'z', 0, 0)  12.4 us
    pallas_call x5, Pallas kernels, call(): pl.pallas_call(kernel, out_shape=out_shape, in_specs=[SMEM if smem and i...  12.1 us
    all_to_all x1, starting transfers between devices, shards(): lax.all_to_all(jnp.broadcast_to(stats, (8, 8, 128)), ('yh', 'x'), 0, 0)  9.61 us
    all_to_all x1, waiting for transfers between devices, shards(): lax.all_to_all(jnp.broadcast_to(stats, (8, 8, 128)), ('yh', 'x'), 0, 0)  6.57 us
  transfers between devices with their start and end apart: 26, of which 14 were waited for; matrix products, arithmetic and copies ran while one was open for 6% of the time, Pallas kernels for 2%

profile of v3, /device:TPU:1, one launch (start us, length us, event | category | flops | bytes accessed | tf_op | source)
XLA Modules:
  0.0 158.4 jit_solution(8728450350993326716)
XLA Ops:
  7.2 0.9 copy.34
  8.3 0.9 copy.35
  9.3 0.8 concatenate.35
  10.1 3.8 %collective-permute-start.19 = (bf16[20,2048]{1,0:T(8,128)(2,1)S(1)}, bf16[20,2048]{1,0:T(8,128)(2,1)S(1)}, u32[]{:S(2)}, u32[]{:S(2)}) collective-permute-start(bf16[20,2048]{1,0:T(8,128)(2,1)S(1)} %concatenate.35), channel_id=1, source_target_pairs={{32,0},{0,32},{33,1},{1,33},{34,2},{2,34},{35,3},{3,35},{36,4},{4,... | collective-permute-start | bytes 245768 | tf_op jit(solution)/shard_map/ppermute | solution.py:30
  13.9 1.0 fusion.10
  15.2 4.4 %collective-permute-done.18 = bf16[64,384]{1,0:T(8,128)(2,1)S(1)} collective-permute-done((bf16[64,384]{1,0:T(8,128)(2,1)S(1)}, bf16[64,384]{1,0:T(8,128)(2,1)S(1)}, u32[]{:S(2)}, u32[]{:S(2)}) %collective-permute-start.18) | collective-permute-done | bytes 49184 | tf_op jit(solution)/shard_map/ppermute | solution.py:30
  19.9 0.7 copy-done.12
  20.6 1.3 collective-permute-start.1
  21.9 4.0 %collective-permute-start = (bf16[4,1,16,320]{3,2,1,0:T(8,128)(2,1)S(1)}, bf16[4,1,16,320]{3,2,1,0:T(8,128)(2,1)S(1)}, u32[]{:S(2)}, u32[]{:S(2)}) collective-permute-start(bf16[4,1,16,320]{3,2,1,0:T(8,128)(2,1)S(1)} %copy-done.22), channel_id=1, source_target_pairs={{0,1},{1,2},{2,3},{3,4},{4,5},{5,6},{6,7},{7,8},{8,9},{9,10},{10,1... | collective-permute-start | bytes 122888 | tf_op jit(solution)/shard_map/ppermute | solution.py:331
  26.1 9.1 %collective-permute-start.9 = (bf16[20,2880]{1,0:T(8,128)(2,1)S(1)}, bf16[20,2880]{1,0:T(8,128)(2,1)S(1)}, u32[]{:S(2)}, u32[]{:S(2)}) collective-permute-start(bf16[20,2880]{1,0:T(8,128)(2,1)S(1)} %reshape.58), channel_id=1, source_target_pairs={{32,0},{0,32},{33,1},{1,33},{34,2},{2,34},{35,3},{3,35},{36,4},{4,... | collective-permute-start | bytes 345608 | tf_op jit(solution)/shard_map/ppermute | solution.py:30
  35.4 2.8 %collective-permute-start.2 = (bf16[3,64,320]{2,1,0:T(8,128)(2,1)S(1)}, bf16[3,64,320]{2,1,0:T(8,128)(2,1)S(1)}, u32[]{:S(2)}, u32[]{:S(2)}) collective-permute-start(bf16[3,64,320]{2,1,0:T(8,128)(2,1)S(1)} %bitcast.41), channel_id=1, source_target_pairs={{4,0},{8,4},{12,8},{16,12},{20,16},{24,20},{28,24},{0,28},{5,1},{9... | collective-permute-start | bytes 368648 | tf_op jit(solution)/shard_map/ppermute | solution.py:30
  38.2 0.9 broadcast_select_fusion.1
  39.2 0.8 pad_maximum_fusion.1
  39.9 4.1 %collective-permute-start.11 = (bf16[40,2880]{1,0:T(8,128)(2,1)}, bf16[40,2880]{1,0:T(8,128)(2,1)}, u32[]{:S(2)}, u32[]{:S(2)}) collective-permute-start(bf16[40,2880]{1,0:T(8,128)(2,1)} %pad_maximum_fusion.1), channel_id=1, source_target_pairs={{2,0},{3,1},{0,2},{1,3},{6,4},{7,5},{4,6},{5,7},{10,8},{11,9},{8,1... | collective-permute-start | bytes 691208 | tf_op jit(solution)/shard_map/ppermute | solution.py:30
  44.1 4.4 %collective-permute-start.4 = (bf16[3,64,320]{2,1,0:T(8,128)(2,1)S(1)}, bf16[3,64,320]{2,1,0:T(8,128)(2,1)S(1)}, u32[]{:S(2)}, u32[]{:S(2)}) collective-permute-start(bf16[3,64,320]{2,1,0:T(8,128)(2,1)S(1)} %collective-permute-done.2.refs_1_), channel_id=1, source_target_pairs={{4,0},{8,4},{12,8},{16,12},{20,16},{24,20},{28,24},{0,28},{5,1},{9... | collective-permute-start | bytes 368648 | tf_op jit(solution)/shard_map/ppermute | solution.py:30
  48.6 3.7 %collective-permute-done.5.refs_4_ = bf16[3,64,320]{2,1,0:T(8,128)(2,1)S(1)} collective-permute-done((bf16[3,64,320]{2,1,0:T(8,128)(2,1)S(1)}, bf16[3,64,320]{2,1,0:T(8,128)(2,1)S(1)}, u32[]{:S(2)}, u32[]{:S(2)}) %collective-permute-start.5) | collective-permute-done | bytes 122912 | tf_op jit(solution)/shard_map/ppermute | solution.py:30
  52.3 2.7 %collective-permute-start.6 = (bf16[3,64,320]{2,1,0:T(8,128)(2,1)S(1)}, bf16[3,64,320]{2,1,0:T(8,128)(2,1)S(1)}, u32[]{:S(2)}, u32[]{:S(2)}) collective-permute-start(bf16[3,64,320]{2,1,0:T(8,128)(2,1)S(1)} %collective-permute-done.4.refs_3_), channel_id=1, source_target_pairs={{4,0},{8,4},{12,8},{16,12},{20,16},{24,20},{28,24},{0,28},{5,1},{9... | collective-permute-start | bytes 368648 | tf_op jit(solution)/shard_map/ppermute | solution.py:30
  55.0 1.6 %select_select_fusion.3 = (bf16[40,2880]{1,0:T(8,128)(2,1)S(1)}, bf16[40,2880]{1,0:T(8,128)(2,1)S(1)}, bf16[40,2880]{1,0:T(8,128)(2,1)S(1)}, bf16[40,2880]{1,0:T(8,128)(2,1)S(1)}) fusion(bf16[40,2880]{1,0:T(8,128)(2,1)} %collective-permute-done.10, bf16[40,2880]{1,0:T(8,128)(2,1)} %collective-permute-done.11, bf16[40,2880]{1,0:T(8,128)(2,1)} %collective-permute-done.12, ...), kind=kLoop, calls=%fused_computation.22 | loop fusion | flops 1843200 | bytes 1843203 | tf_op jit(solution)/shard_map/jit(_where)/select_n | solution.py:55
  56.6 2.6 %collective-permute-done.6.refs_5_ = bf16[3,64,320]{2,1,0:T(8,128)(2,1)S(1)} collective-permute-done((bf16[3,64,320]{2,1,0:T(8,128)(2,1)S(1)}, bf16[3,64,320]{2,1,0:T(8,128)(2,1)S(1)}, u32[]{:S(2)}, u32[]{:S(2)}) %collective-permute-start.6) | collective-permute-done | bytes 122912 | tf_op jit(solution)/shard_map/ppermute | solution.py:30
  59.2 3.0 %collective-permute-start.8 = (bf16[3,64,320]{2,1,0:T(8,128)(2,1)S(1)}, bf16[3,64,320]{2,1,0:T(8,128)(2,1)S(1)}, u32[]{:S(2)}, u32[]{:S(2)}) collective-permute-start(bf16[3,64,320]{2,1,0:T(8,128)(2,1)S(1)} %collective-permute-done.6.refs_5_), channel_id=1, source_target_pairs={{4,0},{8,4},{12,8},{16,12},{20,16},{24,20},{28,24},{0,28},{5,1},{9... | collective-permute-start | bytes 368648 | tf_op jit(solution)/shard_map/ppermute | solution.py:30
  62.4 3.9 %collective-permute-done.8.refs_7_ = bf16[3,64,320]{2,1,0:T(8,128)(2,1)S(1)} collective-permute-done((bf16[3,64,320]{2,1,0:T(8,128)(2,1)S(1)}, bf16[3,64,320]{2,1,0:T(8,128)(2,1)S(1)}, u32[]{:S(2)}, u32[]{:S(2)}) %collective-permute-start.8) | collective-permute-done | bytes 122912 | tf_op jit(solution)/shard_map/ppermute | solution.py:30
  66.3 0.9 copy-done.4
  67.2 0.9 copy-done.6
  68.1 0.9 copy-done.8
  69.0 2.4 %shard_map.131 = (f32[2,128,160]{2,1,0:T(8,128)S(1)}, f32[2,128,160]{2,1,0:T(8,128)S(1)}) custom-call(s32[5]{0:T(128)S(1)} %stack.23.where_ref, bf16[3,64,320]{2,1,0:T(8,128)(2,1)S(1)} %bitcast.42, bf16[3,64,320]{2,1,0:T(8,128)(2,1)S(1)} %copy-done.4, bf16[3,64,320]{2,1,0:T(8,128)(2,1)S(1)} %collective-permute-done.3.refs_2_, ...), custom_call_target="tpu_custom_call" | custom-call | flops 3000000000 | bytes 1904660 | tf_op jit(solution)/shard_map/pallas_call | solution.py:276
  71.4 7.0 %collective-permute-start.13 = (f32[2,128,160]{2,1,0:T(8,128)S(1)}, f32[2,128,160]{2,1,0:T(8,128)}, u32[]{:S(2)}, u32[]{:S(2)}) collective-permute-start(f32[2,128,160]{2,1,0:T(8,128)S(1)} %get-tuple-element.14), channel_id=1, source_target_pairs={{0,64},{64,0},{1,65},{65,1},{2,66},{66,2},{3,67},{67,3},{4,68},{68... | collective-permute-start | bytes 491528 | tf_op jit(solution)/shard_map/ppermute | solution.py:294
  79.7 1.0 fusion.1
  81.2 4.5 %collective-permute-done.14.got_ref = f32[128,160]{1,0:T(8,128)S(1)} collective-permute-done((f32[128,160]{1,0:T(8,128)S(1)}, f32[128,160]{1,0:T(8,128)S(1)}, u32[]{:S(2)}, u32[]{:S(2)}) %collective-permute-start.14) | collective-permute-done | bytes 81952 | tf_op jit(solution)/shard_map/ppermute | solution.py:294
  86.5 9.6 %all-to-all-start = ((f32[8,8,128]{2,1,0:T(8,128)}), f32[8,8,128]{2,1,0:T(8,128)S(1)}, u32[]{:S(2)}, u32[]{:S(2)}) async-start(f32[8,8,128]{2,1,0:T(8,128)} %broadcast_in_dim.3), calls=%async_computation | async-start | bytes 65536 | tf_op jit(solution)/shard_map/all_to_all | solution.py:371
  96.3 6.6 %all-to-all-done.stats_ref = f32[8,8,128]{2,1,0:T(8,128)S(1)} async-done(((f32[8,8,128]{2,1,0:T(8,128)}), f32[8,8,128]{2,1,0:T(8,128)S(1)}, u32[]{:S(2)}, u32[]{:S(2)}) %all-to-all-start) | async-done | bytes 32800 | tf_op jit(solution)/shard_map/all_to_all | solution.py:371
  103.1 12.4 %all_to_all.10.refs_0_ = bf16[8,16,160]{2,1,0:T(8,128)(2,1)S(1)} all-to-all(bf16[8,16,160]{2,1,0:T(8,128)(2,1)S(1)} %shard_map.133), channel_id=1, replica_groups=mesh['yl'=2,'c'=2,'yh'=2,'z'=8,'x'=4] {'z'}, dimensions={0} | all-to-all | bytes 81920 | tf_op jit(solution)/shard_map/all_to_all | solution.py:380
  115.5 4.0 %collective-permute-start.15 = (bf16[8,16,160]{2,1,0:T(8,128)(2,1)S(1)}, bf16[8,16,160]{2,1,0:T(8,128)(2,1)S(1)}, u32[]{:S(2)}, u32[]{:S(2)}) collective-permute-start(bf16[8,16,160]{2,1,0:T(8,128)(2,1)S(1)} %all_to_all.10.refs_0_), channel_id=1, source_target_pairs={{0,64},{64,0},{1,65},{65,1},{2,66},{66,2},{3,67},{67,3},{4,68},{68... | collective-permute-start | bytes 122888 | tf_op jit(solution)/shard_map/ppermute | solution.py:294
  121.0 2.2 %collective-permute-done.16.refs_2_ = bf16[8,16,160]{2,1,0:T(8,128)(2,1)S(1)} collective-permute-done((bf16[8,16,160]{2,1,0:T(8,128)(2,1)S(1)}, bf16[8,16,160]{2,1,0:T(8,128)(2,1)S(1)}, u32[]{:S(2)}, u32[]{:S(2)}) %collective-permute-start.16) | collective-permute-done | bytes 40992 | tf_op jit(solution)/shard_map/ppermute | solution.py:294
  123.2 1.4 collective-permute-done.17.refs_3_
  125.2 6.8 %shard_map.134 = (bf16[4,16,1280]{2,1,0:T(8,128)(2,1)}, bf16[4,16,384]{2,1,0:T(8,128)(2,1)}, bf16[4,16,1280]{2,1,0:T(8,128)(2,1)}) custom-call(s32[5]{0:T(128)} %copy-done.2, bf16[8,16,160]{2,1,0:T(8,128)(2,1)} %copy-done.13, bf16[8,16,160]{2,1,0:T(8,128)(2,1)} %copy-done.15, bf16[8,16,160]{2,1,0:T(8,128)(2,1)} %copy-done.16, ...), custom_call_target="tpu_custom_call" | custom-call | flops 1000000000 | bytes 8552468 | tf_op jit(solution)/shard_map/pallas_call | solution.py:276
  132.0 0.9 collective-permute-start.20
  132.9 1.2 collective-permute-done.20
  134.1 1.0 add_convert_fusion.2.mine_ref
  135.1 0.7 collective-permute-start.21
  135.8 2.1 %slice.87.packed_ref = bf16[32,200,256]{2,1,0:T(8,128)(2,1)S(1)} slice(bf16[32,512,256]{2,1,0:T(8,128)(2,1)} %bitcast.44), slice={[0:32], [312:512], [0:256]} | slice | bytes 6553600 | tf_op jit(solution)/shard_map/slice | solution.py:401
  137.9 2.7 %collective-permute-done.21.got_ref = bf16[4,16,1280]{2,1,0:T(8,128)(2,1)S(1)} collective-permute-done((bf16[4,16,1280]{2,1,0:T(8,128)(2,1)S(1)}, bf16[4,16,1280]{2,1,0:T(8,128)(2,1)S(1)}, u32[]{:S(2)}, u32[]{:S(2)}) %collective-permute-start.21) | collective-permute-done | bytes 163872 | tf_op jit(solution)/shard_map/ppermute | solution.py:294
  140.6 2.4 %shard_map.135 = (bf16[4,16,1280]{2,1,0:T(8,128)(2,1)S(1)}, bf16[4,16,1280]{2,1,0:T(8,128)(2,1)S(1)}) custom-call(bf16[4,16,1280]{2,1,0:T(8,128)(2,1)S(1)} %copy-done.1, bf16[4,16,1280]{2,1,0:T(8,128)(2,1)S(1)} %add_convert_fusion.2.mine_ref, bf16[4,16,1280]{2,1,0:T(8,128)(2,1)S(1)} %collective-permute-done.21.got_ref, ...), custom_call_target="tpu_custom_call" | custom-call | flops 1000000000 | bytes 3768320 | tf_op jit(solution)/shard_map/pallas_call | solution.py:276
  143.0 1.3 collective-permute-start.22
  144.3 1.0 collective-permute-done.22
  145.3 0.7 collective-permute-start.23
  146.0 0.7 reshape.67
  146.8 4.1 %collective-permute-done.23 = bf16[4,16,1280]{2,1,0:T(8,128)(2,1)S(1)} collective-permute-done((bf16[4,16,1280]{2,1,0:T(8,128)(2,1)S(1)}, bf16[4,16,1280]{2,1,0:T(8,128)(2,1)S(1)}, u32[]{:S(2)}, u32[]{:S(2)}) %collective-permute-start.23) | collective-permute-done | bytes 163872 | tf_op jit(solution)/shard_map/ppermute | solution.py:294
  150.8 0.7 fusion
  (111 shorter events, 5.7 us)
Async XLA Ops:
  7.2 71.9 %copy-start = (bf16[1000,1280]{1,0:T(8,128)(2,1)S(1)}, bf16[1000,1280]{1,0:T(8,128)(2,1)}, u32[]{:S(2)}) copy-start(bf16[1000,1280]{1,0:T(8,128)(2,1)} %param.15) | copy-start | bytes 7680004
  7.2 117.4 %all-gather.3.cloned.1.call-start = ((), (), s32[]{:S(2)}) async-start(), calls=%async_computation.2 | async-start | bytes 8650752 | tf_op jit(solution)/shard_map/all_gather | solution.py:355
  8.3 12.3 %copy-start.22 = (bf16[4,1,16,320]{3,2,1,0:T(8,128)(2,1)S(1)}, bf16[4,1,16,320]{3,2,1,0:T(8,128)(2,1)}, u32[]{:S(2)}) copy-start(bf16[4,1,16,320]{3,2,1,0:T(8,128)(2,1)} %param.13) | copy-start | bytes 122884
  8.3 17.6 %copy-start.14 = (bf16[9,320,20]{1,2,0:T(8,128)(2,1)S(1)}, bf16[9,320,20]{1,2,0:T(8,128)(2,1)}, u32[]{:S(2)}) copy-start(bf16[9,320,20]{1,2,0:T(8,128)(2,1)} %param.14) | copy-start | bytes 345604
  10.1 9.6 %collective-permute-start.19 = (bf16[20,2048]{1,0:T(8,128)(2,1)S(1)}, bf16[20,2048]{1,0:T(8,128)(2,1)S(1)}, u32[]{:S(2)}, u32[]{:S(2)}) collective-permute-start(bf16[20,2048]{1,0:T(8,128)(2,1)S(1)} %concatenate.35), channel_id=1, source_target_pairs={{32,0},{0,32},{33,1},{1,33},{34,2},{2,34},{35,3},{3,35},{36,4},{4,... | collective-permute-start | bytes 245768 | tf_op jit(solution)/shard_map/ppermute | solution.py:30
  15.0 20.2 %copy-start.18 = (bf16[4,1,16,320]{3,2,1,0:T(8,128)(2,1)S(1)}, bf16[4,1,16,320]{3,2,1,0:T(8,128)(2,1)}, u32[]{:S(2)}) copy-start(bf16[4,1,16,320]{3,2,1,0:T(8,128)(2,1)} %param.12) | copy-start | bytes 122884
  15.1 4.5 %collective-permute-start.18 = (bf16[64,384]{1,0:T(8,128)(2,1)S(1)}, bf16[64,384]{1,0:T(8,128)(2,1)S(1)}, u32[]{:S(2)}, u32[]{:S(2)}) collective-permute-start(bf16[64,384]{1,0:T(8,128)(2,1)S(1)} %pad_maximum_fusion.2), channel_id=1, source_target_pairs={{32,0},{0,32},{33,1},{1,33},{34,2},{2,34},{35,3},{3,35},{36,4},{4,... | collective-permute-start | bytes 147464 | tf_op jit(solution)/shard_map/ppermute | solution.py:30
  19.9 0.7 copy-start.12
  20.6 14.6 %collective-permute-start.1 = (bf16[4,1,16,320]{3,2,1,0:T(8,128)(2,1)S(1)}, bf16[4,1,16,320]{3,2,1,0:T(8,128)(2,1)S(1)}, u32[]{:S(2)}, u32[]{:S(2)}) collective-permute-start(bf16[4,1,16,320]{3,2,1,0:T(8,128)(2,1)S(1)} %copy-done.22), channel_id=1, source_target_pairs={{1,0},{2,1},{3,2},{4,3},{5,4},{6,5},{7,6},{8,7},{9,8},{10,9},{11,1... | collective-permute-start | bytes 122888 | tf_op jit(solution)/shard_map/ppermute | solution.py:332
  21.9 13.3 %collective-permute-start = (bf16[4,1,16,320]{3,2,1,0:T(8,128)(2,1)S(1)}, bf16[4,1,16,320]{3,2,1,0:T(8,128)(2,1)S(1)}, u32[]{:S(2)}, u32[]{:S(2)}) collective-permute-start(bf16[4,1,16,320]{3,2,1,0:T(8,128)(2,1)S(1)} %copy-done.22), channel_id=1, source_target_pairs={{0,1},{1,2},{2,3},{3,4},{4,5},{5,6},{6,7},{7,8},{8,9},{9,10},{10,1... | collective-permute-start | bytes 122888 | tf_op jit(solution)/shard_map/ppermute | solution.py:331
  26.1 12.1 %copy-start.11 = (bf16[20,2880]{1,0:T(8,128)(2,1)}, bf16[20,2880]{1,0:T(8,128)(2,1)S(1)}, u32[]{:S(2)}) copy-start(bf16[20,2880]{1,0:T(8,128)(2,1)S(1)} %reshape.58) | copy-start | bytes 345604
  26.1 12.1 %collective-permute-start.9 = (bf16[20,2880]{1,0:T(8,128)(2,1)S(1)}, bf16[20,2880]{1,0:T(8,128)(2,1)S(1)}, u32[]{:S(2)}, u32[]{:S(2)}) collective-permute-start(bf16[20,2880]{1,0:T(8,128)(2,1)S(1)} %reshape.58), channel_id=1, source_target_pairs={{32,0},{0,32},{33,1},{1,33},{34,2},{2,34},{35,3},{3,35},{36,4},{4,... | collective-permute-start | bytes 345608 | tf_op jit(solution)/shard_map/ppermute | solution.py:30
  35.3 8.7 %collective-permute-start.3 = (bf16[3,64,320]{2,1,0:T(8,128)(2,1)S(1)}, bf16[3,64,320]{2,1,0:T(8,128)(2,1)S(1)}, u32[]{:S(2)}, u32[]{:S(2)}) collective-permute-start(bf16[3,64,320]{2,1,0:T(8,128)(2,1)S(1)} %bitcast.40), channel_id=1, source_target_pairs={{28,0},{0,4},{4,8},{8,12},{12,16},{16,20},{20,24},{24,28},{29,1},{... | collective-permute-start | bytes 368648 | tf_op jit(solution)/shard_map/ppermute | solution.py:30
  35.4 8.7 %collective-permute-start.2 = (bf16[3,64,320]{2,1,0:T(8,128)(2,1)S(1)}, bf16[3,64,320]{2,1,0:T(8,128)(2,1)S(1)}, u32[]{:S(2)}, u32[]{:S(2)}) collective-permute-start(bf16[3,64,320]{2,1,0:T(8,128)(2,1)S(1)} %bitcast.41), channel_id=1, source_target_pairs={{4,0},{8,4},{12,8},{16,12},{20,16},{24,20},{28,24},{0,28},{5,1},{9... | collective-permute-start | bytes 368648 | tf_op jit(solution)/shard_map/ppermute | solution.py:30
  39.2 4.9 %copy-start.9 = (bf16[20,2880]{1,0:T(8,128)(2,1)}, bf16[20,2880]{1,0:T(8,128)(2,1)S(1)}, u32[]{:S(2)}) copy-start(bf16[20,2880]{1,0:T(8,128)(2,1)S(1)} %get-tuple-element.36) | copy-start | bytes 345604
  39.2 4.8 %copy-start.10 = (bf16[20,2880]{1,0:T(8,128)(2,1)}, bf16[20,2880]{1,0:T(8,128)(2,1)S(1)}, u32[]{:S(2)}) copy-start(bf16[20,2880]{1,0:T(8,128)(2,1)S(1)} %get-tuple-element.37) | copy-start | bytes 345604
  39.9 15.1 %collective-permute-start.12 = (bf16[40,2880]{1,0:T(8,128)(2,1)}, bf16[40,2880]{1,0:T(8,128)(2,1)}, u32[]{:S(2)}, u32[]{:S(2)}) collective-permute-start(bf16[40,2880]{1,0:T(8,128)(2,1)} %pad_maximum_fusion.1), channel_id=1, source_target_pairs={{3,0},{0,1},{1,2},{2,3},{7,4},{4,5},{5,6},{6,7},{11,8},{8,9},{9,10... | collective-permute-start | bytes 691208 | tf_op jit(solution)/shard_map/ppermute | solution.py:30
  39.9 15.1 %collective-permute-start.11 = (bf16[40,2880]{1,0:T(8,128)(2,1)}, bf16[40,2880]{1,0:T(8,128)(2,1)}, u32[]{:S(2)}, u32[]{:S(2)}) collective-permute-start(bf16[40,2880]{1,0:T(8,128)(2,1)} %pad_maximum_fusion.1), channel_id=1, source_target_pairs={{2,0},{3,1},{0,2},{1,3},{6,4},{7,5},{4,6},{5,7},{10,8},{11,9},{8,1... | collective-permute-start | bytes 691208 | tf_op jit(solution)/shard_map/ppermute | solution.py:30
  44.0 11.0 %collective-permute-start.10 = (bf16[40,2880]{1,0:T(8,128)(2,1)}, bf16[40,2880]{1,0:T(8,128)(2,1)}, u32[]{:S(2)}, u32[]{:S(2)}) collective-permute-start(bf16[40,2880]{1,0:T(8,128)(2,1)} %pad_maximum_fusion.1), channel_id=1, source_target_pairs={{1,0},{2,1},{3,2},{0,3},{5,4},{6,5},{7,6},{4,7},{9,8},{10,9},{11,1... | collective-permute-start | bytes 691208 | tf_op jit(solution)/shard_map/ppermute | solution.py:30
  44.0 8.3 %collective-permute-start.5 = (bf16[3,64,320]{2,1,0:T(8,128)(2,1)S(1)}, bf16[3,64,320]{2,1,0:T(8,128)(2,1)S(1)}, u32[]{:S(2)}, u32[]{:S(2)}) collective-permute-start(bf16[3,64,320]{2,1,0:T(8,128)(2,1)S(1)} %collective-permute-done.3.refs_2_), channel_id=1, source_target_pairs={{28,0},{0,4},{4,8},{8,12},{12,16},{16,20},{20,24},{24,28},{29,1},{... | collective-permute-start | bytes 368648 | tf_op jit(solution)/shard_map/ppermute | solution.py:30
  44.1 18.2 %copy-start.3 = (bf16[3,64,320]{2,1,0:T(8,128)(2,1)}, bf16[3,64,320]{2,1,0:T(8,128)(2,1)S(1)}, u32[]{:S(2)}) copy-start(bf16[3,64,320]{2,1,0:T(8,128)(2,1)S(1)} %collective-permute-done.2.refs_1_) | copy-start | bytes 368644
  44.1 8.2 %collective-permute-start.4 = (bf16[3,64,320]{2,1,0:T(8,128)(2,1)S(1)}, bf16[3,64,320]{2,1,0:T(8,128)(2,1)S(1)}, u32[]{:S(2)}, u32[]{:S(2)}) collective-permute-start(bf16[3,64,320]{2,1,0:T(8,128)(2,1)S(1)} %collective-permute-done.2.refs_1_), channel_id=1, source_target_pairs={{4,0},{8,4},{12,8},{16,12},{20,16},{24,20},{28,24},{0,28},{5,1},{9... | collective-permute-start | bytes 368648 | tf_op jit(solution)/shard_map/ppermute | solution.py:30
  48.6 17.6 %copy-start.2 = (s32[5]{0:T(128)}, s32[5]{0:T(128)S(1)}, u32[]{:S(2)}) copy-start(s32[5]{0:T(128)S(1)} %stack.23.where_ref) | copy-start | bytes 64
  52.3 10.1 %copy-start.5 = (bf16[3,64,320]{2,1,0:T(8,128)(2,1)}, bf16[3,64,320]{2,1,0:T(8,128)(2,1)S(1)}, u32[]{:S(2)}) copy-start(bf16[3,64,320]{2,1,0:T(8,128)(2,1)S(1)} %collective-permute-done.5.refs_4_) | copy-start | bytes 368644
  52.3 10.1 %collective-permute-start.7 = (bf16[3,64,320]{2,1,0:T(8,128)(2,1)S(1)}, bf16[3,64,320]{2,1,0:T(8,128)(2,1)S(1)}, u32[]{:S(2)}, u32[]{:S(2)}) collective-permute-start(bf16[3,64,320]{2,1,0:T(8,128)(2,1)S(1)} %collective-permute-done.5.refs_4_), channel_id=1, source_target_pairs={{28,0},{0,4},{4,8},{8,12},{12,16},{16,20},{20,24},{24,28},{29,1},{... | collective-permute-start | bytes 368648 | tf_op jit(solution)/shard_map/ppermute | solution.py:30
  52.3 10.1 %copy-start.7 = (bf16[3,64,320]{2,1,0:T(8,128)(2,1)}, bf16[3,64,320]{2,1,0:T(8,128)(2,1)S(1)}, u32[]{:S(2)}) copy-start(bf16[3,64,320]{2,1,0:T(8,128)(2,1)S(1)} %collective-permute-done.4.refs_3_) | copy-start | bytes 368644
  52.3 6.9 %collective-permute-start.6 = (bf16[3,64,320]{2,1,0:T(8,128)(2,1)S(1)}, bf16[3,64,320]{2,1,0:T(8,128)(2,1)S(1)}, u32[]{:S(2)}, u32[]{:S(2)}) collective-permute-start(bf16[3,64,320]{2,1,0:T(8,128)(2,1)S(1)} %collective-permute-done.4.refs_3_), channel_id=1, source_target_pairs={{4,0},{8,4},{12,8},{16,12},{20,16},{24,20},{28,24},{0,28},{5,1},{9... | collective-permute-start | bytes 368648 | tf_op jit(solution)/shard_map/ppermute | solution.py:30
  59.2 7.0 %collective-permute-start.8 = (bf16[3,64,320]{2,1,0:T(8,128)(2,1)S(1)}, bf16[3,64,320]{2,1,0:T(8,128)(2,1)S(1)}, u32[]{:S(2)}, u32[]{:S(2)}) collective-permute-start(bf16[3,64,320]{2,1,0:T(8,128)(2,1)S(1)} %collective-permute-done.6.refs_5_), channel_id=1, source_target_pairs={{4,0},{8,4},{12,8},{16,12},{20,16},{24,20},{28,24},{0,28},{5,1},{9... | collective-permute-start | bytes 368648 | tf_op jit(solution)/shard_map/ppermute | solution.py:30
  62.3 18.6 %copy-start.20 = (f32[1280]{0:T(1024)S(1)}, f32[1280]{0:T(1024)}, u32[]{:S(2)}) copy-start(f32[1280]{0:T(1024)} %param.17) | copy-start | bytes 15364
  62.3 18.8 %copy-start.21 = (f32[1280]{0:T(1024)S(1)}, f32[1280]{0:T(1024)}, u32[]{:S(2)}) copy-start(f32[1280]{0:T(1024)} %param.18) | copy-start | bytes 15364
  66.3 0.9 copy-start.4
  67.2 0.9 copy-start.6
  68.1 0.9 copy-start.8
  71.4 8.3 %collective-permute-start.13 = (f32[2,128,160]{2,1,0:T(8,128)S(1)}, f32[2,128,160]{2,1,0:T(8,128)}, u32[]{:S(2)}, u32[]{:S(2)}) collective-permute-start(f32[2,128,160]{2,1,0:T(8,128)S(1)} %get-tuple-element.14), channel_id=1, source_target_pairs={{0,64},{64,0},{1,65},{65,1},{2,66},{66,2},{3,67},{67,3},{4,68},{68... | collective-permute-start | bytes 491528 | tf_op jit(solution)/shard_map/ppermute | solution.py:294
  80.7 4.9 %collective-permute-start.14 = (f32[128,160]{1,0:T(8,128)S(1)}, f32[128,160]{1,0:T(8,128)S(1)}, u32[]{:S(2)}, u32[]{:S(2)}) collective-permute-start(f32[128,160]{1,0:T(8,128)S(1)} %get-tuple-element.34), channel_id=1, source_target_pairs={{0,128},{128,0},{1,129},{129,1},{2,130},{130,2},{3,131},{131,3},{4... | collective-permute-start | bytes 245768 | tf_op jit(solution)/shard_map/ppermute | solution.py:294
  86.5 16.4 %all-to-all-start = ((f32[8,8,128]{2,1,0:T(8,128)}), f32[8,8,128]{2,1,0:T(8,128)S(1)}, u32[]{:S(2)}, u32[]{:S(2)}) async-start(f32[8,8,128]{2,1,0:T(8,128)} %broadcast_in_dim.3), calls=%async_computation | async-start | bytes 65536 | tf_op jit(solution)/shard_map/all_to_all | solution.py:371
  115.5 9.1 %copy-start.13 = (bf16[8,16,160]{2,1,0:T(8,128)(2,1)}, bf16[8,16,160]{2,1,0:T(8,128)(2,1)S(1)}, u32[]{:S(2)}) copy-start(bf16[8,16,160]{2,1,0:T(8,128)(2,1)S(1)} %all_to_all.10.refs_0_) | copy-start | bytes 122884
  115.5 4.9 %collective-permute-start.15 = (bf16[8,16,160]{2,1,0:T(8,128)(2,1)S(1)}, bf16[8,16,160]{2,1,0:T(8,128)(2,1)S(1)}, u32[]{:S(2)}, u32[]{:S(2)}) collective-permute-start(bf16[8,16,160]{2,1,0:T(8,128)(2,1)S(1)} %all_to_all.10.refs_0_), channel_id=1, source_target_pairs={{0,64},{64,0},{1,65},{65,1},{2,66},{66,2},{3,67},{67,3},{4,68},{68... | collective-permute-start | bytes 122888 | tf_op jit(solution)/shard_map/ppermute | solution.py:294
  119.4 3.7 %collective-permute-start.16 = (bf16[8,16,160]{2,1,0:T(8,128)(2,1)S(1)}, bf16[8,16,160]{2,1,0:T(8,128)(2,1)S(1)}, u32[]{:S(2)}, u32[]{:S(2)}) collective-permute-start(bf16[8,16,160]{2,1,0:T(8,128)(2,1)S(1)} %all_to_all.10.refs_0_), channel_id=1, source_target_pairs={{0,128},{128,0},{1,129},{129,1},{2,130},{130,2},{3,131},{131,3},{4... | collective-permute-start | bytes 122888 | tf_op jit(solution)/shard_map/ppermute | solution.py:294
  120.3 4.2 %copy-start.15 = (bf16[8,16,160]{2,1,0:T(8,128)(2,1)}, bf16[8,16,160]{2,1,0:T(8,128)(2,1)S(1)}, u32[]{:S(2)}) copy-start(bf16[8,16,160]{2,1,0:T(8,128)(2,1)S(1)} %collective-permute-done.15.refs_1_) | copy-start | bytes 122884
  120.3 4.2 %collective-permute-start.17 = (bf16[8,16,160]{2,1,0:T(8,128)(2,1)S(1)}, bf16[8,16,160]{2,1,0:T(8,128)(2,1)S(1)}, u32[]{:S(2)}, u32[]{:S(2)}) collective-permute-start(bf16[8,16,160]{2,1,0:T(8,128)(2,1)S(1)} %collective-permute-done.15.refs_1_), channel_id=1, source_target_pairs={{0,128},{128,0},{1,129},{129,1},{2,130},{130,2},{3,131},{131,3},{4... | collective-permute-start | bytes 122888 | tf_op jit(solution)/shard_map/ppermute | solution.py:294
  123.2 1.4 copy-start.16
  132.0 2.1 %collective-permute-start.20 = (bf16[4,16,1280]{2,1,0:T(8,128)(2,1)}, bf16[4,16,1280]{2,1,0:T(8,128)(2,1)S(1)}, u32[]{:S(2)}, u32[]{:S(2)}) collective-permute-start(bf16[4,16,1280]{2,1,0:T(8,128)(2,1)} %get-tuple-element.19), channel_id=1, source_target_pairs={{0,64},{64,0},{1,65},{65,1},{2,66},{66,2},{3,67},{67,3},{4,68},{68... | collective-permute-start | bytes 491528 | tf_op jit(solution)/shard_map/ppermute | solution.py:294
  135.1 5.5 %copy-start.1 = (bf16[4,16,1280]{2,1,0:T(8,128)(2,1)S(1)}, bf16[4,16,1280]{2,1,0:T(8,128)(2,1)}, u32[]{:S(2)}) copy-start(bf16[4,16,1280]{2,1,0:T(8,128)(2,1)} %get-tuple-element.17.own_ref) | copy-start | bytes 491524
  135.1 5.5 %collective-permute-start.21 = (bf16[4,16,1280]{2,1,0:T(8,128)(2,1)S(1)}, bf16[4,16,1280]{2,1,0:T(8,128)(2,1)S(1)}, u32[]{:S(2)}, u32[]{:S(2)}) collective-permute-start(bf16[4,16,1280]{2,1,0:T(8,128)(2,1)S(1)} %add_convert_fusion.2.mine_ref), channel_id=1, source_target_pairs={{0,128},{128,0},{1,129},{129,1},{2,130},{130,2},{3,131},{131,3},{4... | collective-permute-start | bytes 491528 | tf_op jit(solution)/shard_map/ppermute | solution.py:294
  140.6 5.5 %copy-start.19 = (bf16[4,16,384]{2,1,0:T(8,128)(2,1)S(1)}, bf16[4,16,384]{2,1,0:T(8,128)(2,1)}, u32[]{:S(2)}) copy-start(bf16[4,16,384]{2,1,0:T(8,128)(2,1)} %get-tuple-element.23) | copy-start | bytes 147460
  143.0 2.3 %collective-permute-start.22 = (bf16[4,16,1280]{2,1,0:T(8,128)(2,1)S(1)}, bf16[4,16,1280]{2,1,0:T(8,128)(2,1)S(1)}, u32[]{:S(2)}, u32[]{:S(2)}) collective-permute-start(bf16[4,16,1280]{2,1,0:T(8,128)(2,1)S(1)} %get-tuple-element.22), channel_id=1, source_target_pairs={{0,64},{64,0},{1,65},{65,1},{2,66},{66,2},{3,67},{67,3},{4,68},{68... | collective-permute-start | bytes 491528 | tf_op jit(solution)/shard_map/ppermute | solution.py:294
  145.3 5.5 %collective-permute-start.23 = (bf16[4,16,1280]{2,1,0:T(8,128)(2,1)S(1)}, bf16[4,16,1280]{2,1,0:T(8,128)(2,1)S(1)}, u32[]{:S(2)}, u32[]{:S(2)}) collective-permute-start(bf16[4,16,1280]{2,1,0:T(8,128)(2,1)S(1)} %add_convert_fusion.1), channel_id=1, source_target_pairs={{0,128},{128,0},{1,129},{129,1},{2,130},{130,2},{3,131},{131,3},{4... | collective-permute-start | bytes 491528 | tf_op jit(solution)/shard_map/ppermute | solution.py:294
  (1 other events, 0.6 us)
Sparse Core Ops, SparseCore 0:
  20.7 101.9 all-gather.2
